TPU v7x, 256 devices: a whole 4x4x8 slice. The times are simulated.
256 devices in a mesh: sub: 64 (over z, y, core), grp: 4 (over x).
Axes of the slice: x: 4, y: 4, z: 8, core: 2. Of those that a mesh axis runs over, the one named last changes fastest.
Arguments:
- schur_up: bfloat16 [2048, 384, 384], P(('sub', 'grp')), as said below
- schur_low: bfloat16 [2048, 384, 384], P(('sub', 'grp'))
- resid_up: bfloat16 [2048, 384, 128], P(('sub', 'grp')), may hold values from -6 to 6
- resid_low: bfloat16 [2048, 384, 128], P(('sub', 'grp')), may hold values from -6 to 6
- counts: int32 [256], P(('sub', 'grp')), may hold values from 1 to 8, as said below
- coarse_up: int32 [2048], P(('sub', 'grp')), may hold values from 0 to 2047, as said below
- coarse_low: int32 [2048], P(('sub', 'grp')), may hold values from 0 to 2047
Outputs:
- average_up: float32 [2048, 384, 128], P(('sub', 'grp'))
- average_low: float32 [2048, 384, 128], P(('sub', 'grp'))
- coarse: float32 [2048, 128], P(('sub', 'grp'))
Inputs may be any that keep to these rules, and one draw needn't show every extreme that they name: counts lie between 1 and 8; counts of devices with the last sub index are not used. `coarse_up`: among the 8 upper and 8 lower slots of one device together, at most 2 name coarse unknowns of the same owner block (value // 8); every device has some owner block named exactly 2 times. `schur_up`: the two sides of a face have diagonals of one sign, of magnitude 2 to 3 each.
All inputs are finite; a program needn't handle non-finite values.
Results may differ from a plain program's by a relative error of at most 0.0003.
Values may be sent and summed in bfloat16 or wider, within the bound.
No kernel may reach another device: no remote copies, remote signals or barrier semaphores. Data moves between devices by JAX's collectives and lax.ppermute only.
A program may use at most 192 MiB of HBM per device.

v0:
```python
import jax
import jax.numpy as jnp
from jax import lax
from jax.sharding import PartitionSpec as P

F = 384
ITERS = 4
CO_DEV = 8


def passed_along(value, axis, by):
    size = lax.axis_size(axis)
    pairs = [(i, i + by) for i in range(size) if 0 <= i + by < size]
    return lax.ppermute(value, axis, pairs)


def solve_faces(lower_side, upper_side, lower_rhs, upper_rhs):
    matrix = lower_side.astype(jnp.float32) + upper_side.astype(jnp.float32)
    source = jnp.einsum("kab,kbp->kap", lower_side, lower_rhs, preferred_element_type=jnp.float32)
    source = source + jnp.einsum(
        "kab,kbp->kap", upper_side, upper_rhs, preferred_element_type=jnp.float32
    )
    pivots = jnp.diagonal(matrix, axis1=1, axis2=2)[:, :, None]
    iterate = source / pivots
    for sweep in range(ITERS):
        product = jnp.einsum("kab,kbp->kap", matrix, iterate, precision=lax.Precision.HIGHEST)
        iterate = iterate + (source - product) / pivots
    return iterate


def side_flux(schur, resid, average, live):
    column_sums = jnp.sum(schur, axis=1, dtype=jnp.float32)
    diff = resid.astype(jnp.float32) - average
    flux = jnp.einsum("mf,mfp->mp", column_sums, diff, precision=lax.Precision.HIGHEST)
    return flux * (live[:, None] / jnp.sqrt(jnp.float32(F)))


def shards(schur_up, schur_low, resid_up, resid_low, counts, coarse_up, coarse_low):
    slots = schur_up.shape[0]
    sub_index = lax.axis_index("sub")
    positions = jnp.arange(slots, dtype=jnp.int32)
    live_up = ((positions < counts[0]) & (sub_index < lax.axis_size("sub") - 1)).astype(jnp.float32)
    partner_block, partner_rhs = passed_along((schur_low, resid_low), "sub", -1)
    average_up = (
        solve_faces(schur_up, partner_block, resid_up, partner_rhs) * live_up[:, None, None]
    )
    average_low, live_low = passed_along((average_up, live_up), "sub", 1)
    fluxes = jnp.concatenate(
        [
            side_flux(schur_up, resid_up, average_up, live_up),
            side_flux(schur_low, resid_low, average_low, live_low),
        ],
        axis=0,
    )
    targets = jnp.concatenate([coarse_up, coarse_low], axis=0)
    wanted = jnp.arange(lax.axis_size(("sub", "grp")) * CO_DEV, dtype=jnp.int32)
    selector = (targets[None, :] == wanted[:, None]).astype(jnp.float32)
    coarse = lax.psum_scatter(
        jnp.dot(selector, fluxes, precision=lax.Precision.HIGHEST),
        ("sub", "grp"),
        scatter_dimension=0,
        tiled=True,
    )
    return (average_up, average_low, coarse)


def solution(mesh):
    return jax.shard_map(
        shards,
        mesh=mesh,
        in_specs=(
            P(("sub", "grp"), None, None),
            P(("sub", "grp"), None, None),
            P(("sub", "grp"), None, None),
            P(("sub", "grp"), None, None),
            P(("sub", "grp")),
            P(("sub", "grp")),
            P(("sub", "grp")),
        ),
        out_specs=(
            P(("sub", "grp"), None, None),
            P(("sub", "grp"), None, None),
            P(("sub", "grp"), None),
        ),
        check_vma=False,
    )
```

profile of v0, /device:TPU:1, one launch (start us, length us, event | category | flops | bytes accessed | tf_op | source)
XLA Modules:
  0.0 404.7 jit_solution(13896282075738217756)
XLA Ops:
  7.2 5.2 %collective-permute-start = (bf16[8,384,384]{2,1,0:T(8,128)(2,1)}, bf16[8,384,384]{2,1,0:T(8,128)(2,1)S(1)}, u32[]{:S(2)}, u32[]{:S(2)}) collective-permute-start(bf16[8,384,384]{2,1,0:T(8,128)(2,1)} %param.8), channel_id=1, source_target_pairs={{4,0},{8,4},{12,8},{16,12},{20,16},{24,20},{28,24},{32,28},{36,32}... | collective-permute-start | bytes 7077896 | tf_op jit(solution)/shard_map/ppermute | solution.py:14
  12.4 1.9 collective-permute-start.1
  15.0 3.9 fusion.27
  18.9 19.6 %collective-permute-done = bf16[8,384,384]{2,1,0:T(8,128)(2,1)S(1)} collective-permute-done((bf16[8,384,384]{2,1,0:T(8,128)(2,1)}, bf16[8,384,384]{2,1,0:T(8,128)(2,1)S(1)}, u32[]{:S(2)}, u32[]{:S(2)}) %collective-permute-start) | collective-permute-done | bytes 2359328 | tf_op jit(solution)/shard_map/ppermute | solution.py:14
  38.5 2.8 convert_reduce_fusion
  41.3 36.0 %copy.14 = f32[8,384,384]{0,2,1:T(8,128)} copy(f32[8,384,384]{2,1,0:T(8,128)} %get-tuple-element.4) | data formatting | bytes 9437184 | tf_op jit(solution)/shard_map/add | solution.py:18
  77.3 8.4 %gather_fusion = f32[384,8]{1,0:T(8,128)S(1)} fusion(f32[8,384,384]{0,2,1:T(8,128)} %copy.14, s32[384]{0:T(512)S(1)} %or_reduce_fusion), kind=kCustom, calls=%fused_computation | custom fusion | bytes 27648 | tf_op jit(solution)/shard_map/jit(diagonal)/gather | solution.py:23
  85.7 0.1 copy.15
  85.8 2.4 convolution_add_fusion
  88.2 5.1 %fusion.12 = f32[8,384,128]{2,1,0:T(8,128)S(1)} fusion(f32[8,384,128]{2,1,0:T(8,128)S(1)} %convolution_add_fusion, f32[8,384]{1,0:T(8,128)S(1)} %copy.15, bf16[8,384,384]{2,1,0:T(8,128)(2,1)S(1)} %copy-done.1, bf16[8,384,384]{2,1,0:T(8,128)(2,1)S(1)} %collective-permute-done), kind=kOutput, calls=%fused_computation.21 | convolution fusion | flops 1815871488 | bytes 7876608 | tf_op jit(solution)/shard_map/kab,kbp->kap/dot_general | solution.py:26
  93.2 5.2 %fusion.8 = f32[8,384,128]{2,1,0:T(8,128)S(1)} fusion(f32[8,384,128]{2,1,0:T(8,128)S(1)} %convolution_add_fusion, f32[8,384,128]{2,1,0:T(8,128)S(1)} %fusion.12, f32[8,384]{1,0:T(8,128)S(1)} %copy.15, bf16[8,384,384]{2,1,0:T(8,128)(2,1)S(1)} %copy-done.1, bf16[8,384,384]{2,1,0:T(8,128)(2,1)S(1)} %collective-permute-done), kind=kOutput, calls=%fused_computation.16 | convolution fusion | flops 1817051136 | bytes 9449472 | tf_op jit(solution)/shard_map/kab,kbp->kap/dot_general | solution.py:26
  98.5 5.6 %fusion.7 = f32[8,384,128]{2,1,0:T(8,128)S(1)} fusion(f32[8,384,128]{2,1,0:T(8,128)S(1)} %convolution_add_fusion, f32[8,384,128]{2,1,0:T(8,128)S(1)} %fusion.8, f32[8,384,128]{2,1,0:T(8,128)S(1)} %fusion.12, f32[8,384]{1,0:T(8,128)S(1)} %copy.15, bf16[8,384,384]{2,1,0:T(8,128)(2,1)S(1)} %copy-done.1, bf16[8,384,384]{2,1,0:T(8,128)(2,1)S(1)} %collective-permute-done), kind=kOutput, calls=%fused_computation.14 | convolution fusion | flops 1818230784 | bytes 11022336 | tf_op jit(solution)/shard_map/kab,kbp->kap/dot_general | solution.py:26
  104.1 6.6 %add_multiply_fusion = f32[8,384,128]{2,1,0:T(8,128)S(1)} fusion(f32[8,384,128]{2,1,0:T(8,128)S(1)} %convolution_add_fusion, f32[8,384,128]{2,1,0:T(8,128)S(1)} %fusion.7, f32[8,384,128]{2,1,0:T(8,128)S(1)} %fusion.8, f32[8,384,128]{2,1,0:T(8,128)S(1)} %fusion.12, f32[8]{0:T(128)S(1)} %fusion.25, f32[8,384]{1,0:T(8,128)S(1)} %copy.15, ...), kind=kOutput, calls=%fused_computation.10 | convolution fusion | flops 1824915456 | bytes 12595232 | tf_op jit(solution)/shard_map/kab,kbp->kap/dot_general | solution.py:26
  110.8 2.2 collective-permute-start.2
  113.0 3.6 collective-permute-start.3
  116.6 0.1 pad_add_fusion
  116.7 0.3 convert_reduce_fusion.1
  117.0 13.3 %collective-permute-done.3 = f32[8]{0:T(128)S(1)} collective-permute-done((f32[8]{0:T(128)S(1)}, f32[8]{0:T(128)S(1)}, u32[]{:S(2)}, u32[]{:S(2)}) %collective-permute-start.3) | collective-permute-done | bytes 64 | tf_op jit(solution)/shard_map/ppermute | solution.py:14
  130.4 1.1 fusion.3
  131.5 1.1 fusion
  132.7 1.6 fusion.14
  134.3 261.2 %all-reduce.3.cloned.1.call-done = f32[2048,128]{1,0:T(8,128)} async-done(((f32[2048,128]{1,0:T(8,128)}), f32[2048,128]{1,0:T(8,128)}) %all-reduce.3.cloned.1.call-update) | async-done | bytes 1048592
  395.5 1.3 constant_dynamic-slice_fusion
  396.8 1.1 copy.27
  (26 shorter events, 0.3 us)
Async XLA Ops:
  7.2 388.3 %all-reduce.3.cloned.1.call-start = ((), (), s32[]{:S(2)}) async-start(), calls=%async_computation | async-start | bytes 2097152
  7.2 31.3 %collective-permute-start = (bf16[8,384,384]{2,1,0:T(8,128)(2,1)}, bf16[8,384,384]{2,1,0:T(8,128)(2,1)S(1)}, u32[]{:S(2)}, u32[]{:S(2)}) collective-permute-start(bf16[8,384,384]{2,1,0:T(8,128)(2,1)} %param.8), channel_id=1, source_target_pairs={{4,0},{8,4},{12,8},{16,12},{20,16},{24,20},{28,24},{32,28},{36,32}... | collective-permute-start | bytes 7077896 | tf_op jit(solution)/shard_map/ppermute | solution.py:14
  12.4 73.4 %collective-permute-start.1 = (bf16[8,384,128]{2,1,0:T(8,128)(2,1)}, bf16[8,384,128]{2,1,0:T(8,128)(2,1)S(1)}, u32[]{:S(2)}, u32[]{:S(2)}) collective-permute-start(bf16[8,384,128]{2,1,0:T(8,128)(2,1)} %param.10), channel_id=1, source_target_pairs={{4,0},{8,4},{12,8},{16,12},{20,16},{24,20},{28,24},{32,28},{36,32}... | collective-permute-start | bytes 2359304 | tf_op jit(solution)/shard_map/ppermute | solution.py:14
  15.0 23.6 %copy-start = (bf16[8,384,384]{2,1,0:T(8,128)(2,1)S(1)}, bf16[8,384,384]{2,1,0:T(8,128)(2,1)}, u32[]{:S(2)}) copy-start(bf16[8,384,384]{2,1,0:T(8,128)(2,1)} %param.7) | copy-start | bytes 7077892
  85.8 2.4 copy-start.1
  104.1 12.5 %copy-start.6 = (s32[8]{0:T(128)S(1)}, s32[8]{0:T(128)}, u32[]{:S(2)}) copy-start(s32[8]{0:T(128)} %param.13) | copy-start | bytes 100
  104.1 12.5 %copy-start.7 = (s32[8]{0:T(128)S(1)}, s32[8]{0:T(128)}, u32[]{:S(2)}) copy-start(s32[8]{0:T(128)} %param.12) | copy-start | bytes 100
  104.1 12.6 %copy-start.3 = (bf16[8,384,384]{2,1,0:T(8,128)(2,1)S(1)}, bf16[8,384,384]{2,1,0:T(8,128)(2,1)}, u32[]{:S(2)}) copy-start(bf16[8,384,384]{2,1,0:T(8,128)(2,1)} %param.8) | copy-start | bytes 7077892
  110.8 20.7 %copy-start.4 = (f32[8,384,128]{2,1,0:T(8,128)}, f32[8,384,128]{2,1,0:T(8,128)S(1)}, u32[]{:S(2)}) copy-start(f32[8,384,128]{2,1,0:T(8,128)S(1)} %add_multiply_fusion) | copy-start | bytes 4718596
  110.8 19.6 %copy-start.2 = (bf16[8,384,128]{2,1,0:T(8,128)(2,1)S(1)}, bf16[8,384,128]{2,1,0:T(8,128)(2,1)}, u32[]{:S(2)}) copy-start(bf16[8,384,128]{2,1,0:T(8,128)(2,1)} %param.9) | copy-start | bytes 2359300
  110.8 20.7 %collective-permute-start.2 = (f32[8,384,128]{2,1,0:T(8,128)S(1)}, f32[8,384,128]{2,1,0:T(8,128)S(1)}, u32[]{:S(2)}, u32[]{:S(2)}) collective-permute-start(f32[8,384,128]{2,1,0:T(8,128)S(1)} %add_multiply_fusion), channel_id=1, source_target_pairs={{0,4},{4,8},{8,12},{12,16},{16,20},{20,24},{24,28},{28,32},{32,36}... | collective-permute-start | bytes 4718600 | tf_op jit(solution)/shard_map/ppermute | solution.py:14
  113.0 17.4 %collective-permute-start.3 = (f32[8]{0:T(128)S(1)}, f32[8]{0:T(128)S(1)}, u32[]{:S(2)}, u32[]{:S(2)}) collective-permute-start(f32[8]{0:T(128)S(1)} %fusion.25), channel_id=1, source_target_pairs={{0,4},{4,8},{8,12},{12,16},{16,20},{20,24},{24,28},{28,32},{32,36}... | collective-permute-start | bytes 104 | tf_op jit(solution)/shard_map/ppermute | solution.py:14
  117.0 14.5 %copy-start.5 = (bf16[8,384,128]{2,1,0:T(8,128)(2,1)S(1)}, bf16[8,384,128]{2,1,0:T(8,128)(2,1)}, u32[]{:S(2)}) copy-start(bf16[8,384,128]{2,1,0:T(8,128)(2,1)} %param.10) | copy-start | bytes 2359300
Sparse Core Ops, SparseCore 0:
  134.4 260.9 all-reduce.2
where the time goes:
time: 406 us; the launch traced here: 405 us
  waiting for transfers between devices  294 us (72%)
  local copies, waits for them, and re-layouts  46.9 us (12%)
  matrix products  32.6 us (8%)
  between operations  14.9 us (4%)
  starting transfers between devices  12.9 us (3%)
    unnamed x2, waiting for transfers between devices  261 us
    add x1, local copies, waits for them, and re-layouts, solve_faces(): matrix = lower_side.astype(jnp.float32) + upper_side.astype(jnp.float32)  36 us
    ppermute x4, waiting for transfers between devices, passed_along(): return lax.ppermute(value, axis, pairs)  33 us
    dot_general x4, matrix products, solve_faces(): jnp.einsum('kab,kbp->kap', matrix, iterate, precision=lax.Precision.HIGHEST)  22.5 us
    ppermute x4, starting transfers between devices, passed_along(): return lax.ppermute(value, axis, pairs)  12.8 us
    gather x2, local copies, waits for them, and re-layouts, solve_faces(): pivots = jnp.diagonal(matrix, axis1=1, axis2=2)[:, :, None]  8.47 us
  transfers between devices with their start and end apart: 5, of which 3 were waited for; matrix products, arithmetic and copies ran while one was open for 13% of the time, Pallas kernels for 0%

commit v1 on v0

v1 whole, which is shorter than its diff:
```python
import jax
import jax.numpy as jnp
from jax import lax
from jax.experimental import pallas as pl
from jax.experimental.pallas import tpu as pltpu
from jax.sharding import PartitionSpec as P

F = 384
COLS = 128
FC = 8
HALF = FC // 2
ITERS = 4
CO_DEV = 8
SLOTS = 4
BOTH = ("sub", "grp")


def swapped(value, odd):
    size = lax.axis_size("sub")
    pairs = []
    for i in range(size):
        j = ((i + 1) ^ 1) - 1 if odd else i ^ 1
        if 0 <= j < size:
            pairs.append((i, j))
    return lax.ppermute(value, "sub", pairs)


def split(value):
    high = value.astype(jnp.bfloat16)
    low = (value - high.astype(jnp.float32)).astype(jnp.bfloat16)
    return high, low


def mm(a, b):
    return jnp.dot(a, b, preferred_element_type=jnp.float32)


def three(row):
    high, low = split(row)
    rest = row - high.astype(jnp.float32) - low.astype(jnp.float32)
    return high.astype(jnp.float32), low.astype(jnp.float32), rest


def face_kernel(first, info, su, sl, ru, rl, other, x_out, flux_out):
    face = pl.program_id(0)
    use_up = info[0] == 1
    k = jnp.where(use_up, first, HALF + first) + face
    live = k < info[1]

    own_m = jnp.where(use_up, su[0], sl[0])
    own_r = jnp.where(use_up, ru[0], rl[0])
    oth_m = other[0, :, :F]
    oth_r = other[0, :, F:]

    source = mm(own_m, own_r) + mm(oth_m, oth_r)
    own_f = own_m.astype(jnp.float32)
    oth_f = oth_m.astype(jnp.float32)
    matrix = own_f + oth_f
    diagonal = lax.broadcasted_iota(jnp.int32, (F, F), 0) == lax.broadcasted_iota(
        jnp.int32, (F, F), 1
    )
    pivots = jnp.sum(jnp.where(diagonal, matrix, 0.0), axis=1, keepdims=True)
    inverse = 1.0 / pivots
    off_h, off_l = split(jnp.where(diagonal, 0.0, matrix))
    x = source * inverse
    for sweep in range(ITERS):
        x_h, x_l = split(x)
        wide = mm(off_h, jnp.concatenate([x_h, x_l], axis=1))
        product = wide[:, :COLS] + wide[:, COLS:] + mm(off_l, x_h)
        x = (source - product) * inverse
    x_out[0] = jnp.where(live, x, 0.0)

    sums_own = jnp.sum(own_f, axis=0, keepdims=True)
    sums_oth = jnp.sum(oth_f, axis=0, keepdims=True)
    rows = three(sums_own) + three(sums_oth)
    which = lax.broadcasted_iota(jnp.int32, (16, F), 0)
    left = jnp.zeros((16, F), jnp.float32)
    for i, row in enumerate(rows):
        left = jnp.where(which == i, row, left)
    x_h, x_l = split(x)
    right = jnp.concatenate([own_r, oth_r, x_h, x_l], axis=1)
    prod = mm(left.astype(jnp.bfloat16), right)
    moved = prod[:, 2 * COLS : 3 * COLS] + prod[:, 3 * COLS :]
    line = lax.broadcasted_iota(jnp.int32, (16, COLS), 0)
    own_flux = jnp.sum(jnp.where(line < 3, prod[:, :COLS] - moved, 0.0), axis=0, keepdims=True)
    oth_flux = jnp.sum(
        jnp.where((line >= 3) & (line < 6), prod[:, COLS : 2 * COLS] - moved, 0.0),
        axis=0,
        keepdims=True,
    )
    scale = 1.0 / jnp.sqrt(jnp.float32(F))
    row8 = lax.broadcasted_iota(jnp.int32, (8, COLS), 0)
    both = jnp.where(row8 == 0, own_flux, jnp.where(row8 == 1, oth_flux, 0.0)) * scale
    flux_out[0] = jnp.where(live, both, 0.0)


def solve_faces(info, first, count, su, sl, ru, rl, other):
    def up(i, s):
        return (jnp.where(s[0] == 1, first + i, first), 0, 0)

    def low(i, s):
        return (jnp.where(s[0] == 1, HALF + first, HALF + first + i), 0, 0)

    def kernel(*refs):
        face_kernel(first, *refs)

    return pl.pallas_call(
        kernel,
        grid_spec=pltpu.PrefetchScalarGridSpec(
            num_scalar_prefetch=1,
            grid=(count,),
            in_specs=[
                pl.BlockSpec((1, F, F), up),
                pl.BlockSpec((1, F, F), low),
                pl.BlockSpec((1, F, COLS), up),
                pl.BlockSpec((1, F, COLS), low),
                pl.BlockSpec((1, F, F + COLS), lambda i, s: (i, 0, 0)),
            ],
            out_specs=[
                pl.BlockSpec((1, F, COLS), lambda i, s: (i, 0, 0)),
                pl.BlockSpec((1, 8, COLS), lambda i, s: (i, 0, 0)),
            ],
        ),
        out_shape=[
            jax.ShapeDtypeStruct((count, F, COLS), jnp.float32),
            jax.ShapeDtypeStruct((count, 8, COLS), jnp.float32),
        ],
        compiler_params=pltpu.CompilerParams(vmem_limit_bytes=32 * 1024 * 1024),
        cost_estimate=pl.CostEstimate(
            flops=count * 14 * 2 * F * F * COLS, bytes_accessed=count * 1500000, transcendentals=0
        ),
    )(info, su, sl, ru, rl, other)


def shards(schur_up, schur_low, resid_up, resid_low, counts, coarse_up, coarse_low):
    subs = lax.axis_size("sub")
    devices = lax.axis_size(BOTH)
    s = lax.axis_index("sub")
    odd_core = s % 2 == 1

    def pick(if_odd, if_even):
        return jnp.where(odd_core, if_odd, if_even)

    def pack(lo, hi, use_up):
        up = jnp.concatenate([schur_up[HALF + lo : HALF + hi], resid_up[HALF + lo : HALF + hi]], 2)
        low = jnp.concatenate([schur_low[lo:hi], resid_low[lo:hi]], 2)
        return jnp.where(use_up, up, low)

    cut = HALF - 1
    got_a = swapped(pack(0, cut, odd_core), True)
    got_b = swapped(pack(cut, HALF, odd_core), True)
    got_e = swapped(pack(0, HALF, ~odd_core), False)
    below = lax.ppermute(counts, "sub", [(i, i + 1) for i in range(subs - 1)])
    their_target = swapped(pick(coarse_up[FC - 1], coarse_low[HALF - 1])[None], True)

    count_up = jnp.where(s < subs - 1, counts[0], 0)
    count_low = below[0]
    info_e = jnp.stack([pick(0, 1), pick(count_low, count_up)]).astype(jnp.int32)
    info_o = jnp.stack([pick(1, 0), pick(count_up, count_low)]).astype(jnp.int32)
    args = (schur_up, schur_low, resid_up, resid_low)

    x_e, flux_e = solve_faces(info_e, 0, HALF, *args, got_e)
    back_e, back_flux_e = swapped((x_e, flux_e[:, 1, :]), False)
    x_a, flux_a = solve_faces(info_o, 0, cut, *args, got_a)
    back_flux_a = swapped(flux_a[:, 1, :], True)
    x_b, flux_b = solve_faces(info_o, cut, 1, *args, got_b)
    x_o = jnp.concatenate([x_a, x_b], 0)
    back_o = swapped(x_o, True)

    rows = jnp.concatenate(
        [flux_e[:, 0], back_flux_e, flux_a[:, 0], flux_b[:, 0], back_flux_a, flux_b[:, 1]], 0
    )
    targets = jnp.concatenate(
        [
            pick(coarse_low[HALF:], coarse_up[:HALF]),
            pick(coarse_low[:HALF], coarse_up[HALF:]),
            pick(coarse_up[:HALF], coarse_low[HALF:]),
            pick(coarse_up[HALF : FC - 1], coarse_low[: HALF - 1]),
            their_target,
        ],
        0,
    )
    owner, local = targets // CO_DEV, targets % CO_DEV
    n = owner.shape[0]
    order = jnp.arange(n, dtype=jnp.int32)
    rank = jnp.sum(
        (owner[:, None] == owner[None, :]) & (order[None, :] < order[:, None]), axis=1
    ).astype(jnp.int32)
    heads = (jnp.arange(COLS)[None, :] == (rank * CO_DEV + local)[:, None]).astype(jnp.float32)
    places = jnp.concatenate([owner * SLOTS + rank, owner * SLOTS + SLOTS - 1], 0)
    chosen = (jnp.arange(devices * SLOTS)[:, None] == places[None, :]).astype(jnp.float32)
    parcels = jnp.dot(chosen, jnp.concatenate([rows, heads], 0), precision=lax.Precision.HIGHEST)
    arrived = lax.all_to_all(parcels.reshape(devices, SLOTS, COLS), BOTH, 0, 0, tiled=True)
    coarse = jnp.zeros((CO_DEV, COLS), jnp.float32)
    for r in range(SLOTS - 1):
        coarse = coarse + jnp.einsum(
            "dm,dp->mp",
            arrived[:, SLOTS - 1, r * CO_DEV : (r + 1) * CO_DEV],
            arrived[:, r, :],
            precision=lax.Precision.HIGHEST,
        )

    average_up = jnp.concatenate([pick(x_o, x_e), pick(back_o, back_e)], 0)
    average_low = jnp.concatenate([pick(back_e, back_o), pick(x_e, x_o)], 0)
    return (average_up, average_low, coarse)


def solution(mesh):
    return jax.shard_map(
        shards,
        mesh=mesh,
        in_specs=(
            P(BOTH, None, None),
            P(BOTH, None, None),
            P(BOTH, None, None),
            P(BOTH, None, None),
            P(BOTH),
            P(BOTH),
            P(BOTH),
        ),
        out_specs=(
            P(BOTH, None, None),
            P(BOTH, None, None),
            P(BOTH, None),
        ),
        check_vma=False,
    )
```

time: 406 us -> 106 us (0.26)
  waiting for transfers between devices: 294 us -> 17.2 us
  local copies, waits for them, and re-layouts: 46.9 us -> 11.1 us
  starting transfers between devices: 12.9 us -> 43.1 us
  matrix products: 32.6 us -> 2.83 us
  Pallas kernels: 0 us -> 15.3 us
  between operations: 14.9 us -> 4.14 us
  other arithmetic: 3.39 us -> 11.6 us
    unnamed x2 -> x0, waiting for transfers between devices: 261 us -> none
    add x1 -> x0, local copies, waits for them, and re-layouts: 36 us -> none  [solve_faces(): matrix = lower_side.astype(jnp.float32) + upper_side.astype(jnp.float32)]
    ppermute x4 -> x9, waiting for transfers between devices: 33 us -> 0.52 us  [the longest x8 0.51 us: swapped(): return lax.ppermute(value, 'sub', pairs)]
    dot_general x9 -> x4, matrix products: 32.6 us -> 2.83 us  [the longest x3 1.67 us: shards(): jnp.einsum('dm,dp->mp', arrived[:, SLOTS - 1, r * CO_DEV:(r + 1) * CO_DEV...]
    all_to_all x0 -> x1, starting transfers between devices: none -> 18 us  [shards(): lax.all_to_all(parcels.reshape(devices, SLOTS, COLS), BOTH, 0, 0, tiled=T...]
    all_to_all x0 -> x1, waiting for transfers between devices: none -> 16.7 us  [shards(): lax.all_to_all(parcels.reshape(devices, SLOTS, COLS), BOTH, 0, 0, tiled=T...]
    pallas_call x0 -> x2, Pallas kernels: none -> 15.3 us  [solve_faces(): pl.pallas_call(kernel, grid_spec=pltpu.PrefetchScalarGridSpec(num_scalar_...]
    ppermute x4 -> x9, starting transfers between devices: 12.8 us -> 25.1 us  [the longest x8 20.5 us: swapped(): return lax.ppermute(value, 'sub', pairs)]
  transfers between devices with their start and end apart: 5 -> 10, of which waited for: 3 -> 2; matrix products, arithmetic and copies ran while one was open for 13% -> 15% of each run, Pallas kernels for 0% -> 15%
where the time goes in v1:
time: 106 us; the launch traced here: 105 us
  starting transfers between devices  43.1 us (41%)
  waiting for transfers between devices  17.2 us (16%)
  Pallas kernels  15.3 us (14%)
  other arithmetic  11.6 us (11%)
  local copies, waits for them, and re-layouts  11.1 us (10%)
  between operations  4.14 us (4%)
  matrix products  2.83 us (3%)
    ppermute x8, starting transfers between devices, swapped(): return lax.ppermute(value, 'sub', pairs)  20.5 us
    all_to_all x1, starting transfers between devices, shards(): lax.all_to_all(parcels.reshape(devices, SLOTS, COLS), BOTH, 0, 0, tiled=T...  18 us
    all_to_all x1, waiting for transfers between devices, shards(): lax.all_to_all(parcels.reshape(devices, SLOTS, COLS), BOTH, 0, 0, tiled=T...  16.7 us
    pallas_call x2, Pallas kernels, solve_faces(): pl.pallas_call(kernel, grid_spec=pltpu.PrefetchScalarGridSpec(num_scalar_...  15.3 us
    unnamed x21, local copies, waits for them, and re-layouts  4.81 us
    ppermute x1, starting transfers between devices, shards(): below = lax.ppermute(counts, 'sub', [(i, i + 1) for i in range(subs - 1)])  4.6 us
    pallas_call x1, other arithmetic, solve_faces(): pl.pallas_call(kernel, grid_spec=pltpu.PrefetchScalarGridSpec(num_scalar_...  3.97 us
    select_n x3, other arithmetic, pack(): return jnp.where(use_up, up, low)  3.68 us
  transfers between devices with their start and end apart: 10, of which 2 were waited for; matrix products, arithmetic and copies ran while one was open for 15% of the time, Pallas kernels for 15%

profile of v1, /device:TPU:1, one launch (start us, length us, event | category | flops | bytes accessed | tf_op | source)
XLA Modules:
  0.0 105.2 jit_solution(3398908754860264565)
XLA Ops:
  0.6 4.6 %collective-permute-start = (s32[1]{0:T(128)}, s32[1]{0:T(128)}, u32[]{:S(2)}, u32[]{:S(2)}) collective-permute-start(s32[1]{0:T(128)} %param.11), channel_id=1, source_target_pairs={{0,4},{4,8},{8,12},{12,16},{16,20},{20,24},{24,28},{28,32},{32,36}... | collective-permute-start | bytes 20 | tf_op jit(solution)/shard_map/ppermute | solution.py:153
  5.3 1.1 %slice-done = bf16[3,384,384]{2,1,0:T(8,128)(2,1)S(1)} async-done(((bf16[8,384,384]{2,1,0:T(8,128)(2,1)}), bf16[3,384,384]{2,1,0:T(8,128)(2,1)S(1)}, s32[]{:S(2)}) %slice-start) | async-done | bytes 884760 | tf_op jit(solution)/shard_map/slice | solution.py:145
  6.8 1.3 %maximum_select_fusion.1 = bf16[3,384,512]{2,1,0:T(8,128)(2,1)} fusion(bf16[3,384,128]{2,1,0:T(8,128)(2,1)S(1)} %slice-done.6, bf16[3,384,384]{2,1,0:T(8,128)(2,1)S(1)} %slice-done, bf16[3,384,128]{2,1,0:T(8,128)(2,1)S(1)} %slice-done.9, bf16[3,384,384]{2,1,0:T(8,128)(2,1)S(1)} %slice-done.3, pred[]{:T(512)S(6)} %eq.24), kind=kLoop, calls=%fused_computation.3 | loop fusion | flops 5308416 | bytes 3538945 | tf_op jit(solution)/shard_map/jit(_where)/select_n | solution.py:147
  8.2 2.1 %collective-permute-start.1 = (bf16[3,384,512]{2,1,0:T(8,128)(2,1)}, bf16[3,384,512]{2,1,0:T(8,128)(2,1)}, u32[]{:S(2)}, u32[]{:S(2)}) collective-permute-start(bf16[3,384,512]{2,1,0:T(8,128)(2,1)} %maximum_select_fusion.1), channel_id=1, source_target_pairs={{4,8},{8,4},{12,16},{16,12},{20,24},{24,20},{28,32},{32,28},{36,40... | collective-permute-start | bytes 3538952 | tf_op jit(solution)/shard_map/ppermute | solution.py:25
  10.3 0.8 maximum_select_fusion.2
  11.1 3.6 %collective-permute-start.2 = (bf16[1,384,512]{2,1,0:T(8,128)(2,1)}, bf16[1,384,512]{2,1,0:T(8,128)(2,1)}, u32[]{:S(2)}, u32[]{:S(2)}) collective-permute-start(bf16[1,384,512]{2,1,0:T(8,128)(2,1)} %maximum_select_fusion.2), channel_id=1, source_target_pairs={{4,8},{8,4},{12,16},{16,12},{20,24},{24,20},{28,32},{32,28},{36,40... | collective-permute-start | bytes 1179656 | tf_op jit(solution)/shard_map/ppermute | solution.py:25
  14.8 1.2 %slice-done.2 = bf16[4,384,384]{2,1,0:T(8,128)(2,1)S(1)} async-done(((bf16[8,384,384]{2,1,0:T(8,128)(2,1)}), bf16[4,384,384]{2,1,0:T(8,128)(2,1)S(1)}, s32[]{:S(2)}) %slice-start.2) | async-done | bytes 1179672 | tf_op jit(solution)/shard_map/slice | solution.py:145
  16.6 1.5 %maximum_select_fusion = bf16[4,384,512]{2,1,0:T(8,128)(2,1)} fusion(bf16[4,384,128]{2,1,0:T(8,128)(2,1)S(1)} %slice-done.8, bf16[4,384,384]{2,1,0:T(8,128)(2,1)S(1)} %slice-done.2, bf16[4,384,128]{2,1,0:T(8,128)(2,1)S(1)} %slice-done.11, bf16[4,384,384]{2,1,0:T(8,128)(2,1)S(1)} %slice-done.5, pred[]{:T(512)S(6)} %not.3), kind=kLoop, calls=%fused_computation | loop fusion | flops 7077888 | bytes 4718593 | tf_op jit(solution)/shard_map/jit(_where)/select_n | solution.py:147
  20.7 7.2 %collective-permute-start.6 = (s32[1]{0:T(128)}, s32[1]{0:T(128)}, u32[]{:S(2)}, u32[]{:S(2)}) collective-permute-start(s32[1]{0:T(128)} %bitcast.8), channel_id=1, source_target_pairs={{4,8},{8,4},{12,16},{16,12},{20,24},{24,20},{28,32},{32,28},{36,40... | collective-permute-start | bytes 20 | tf_op jit(solution)/shard_map/ppermute | solution.py:25
  31.6 1.7 %copy-done.1 = bf16[8,384,384]{2,1,0:T(8,128)(2,1)S(1)} copy-done((bf16[8,384,384]{2,1,0:T(8,128)(2,1)S(1)}, bf16[8,384,384]{2,1,0:T(8,128)(2,1)}, u32[]{:S(2)}) %copy-start.1) | copy-done | bytes 2359320
  33.2 1.1 %copy-done.3 = bf16[8,384,128]{2,1,0:T(8,128)(2,1)S(1)} copy-done((bf16[8,384,128]{2,1,0:T(8,128)(2,1)S(1)}, bf16[8,384,128]{2,1,0:T(8,128)(2,1)}, u32[]{:S(2)}) %copy-start.3) | copy-done | bytes 786456
  34.4 1.1 %copy-done.5 = bf16[8,384,128]{2,1,0:T(8,128)(2,1)S(1)} copy-done((bf16[8,384,128]{2,1,0:T(8,128)(2,1)S(1)}, bf16[8,384,128]{2,1,0:T(8,128)(2,1)}, u32[]{:S(2)}) %copy-start.5) | copy-done | bytes 786456
  35.5 6.8 %shard_map.94 = (f32[3,384,128]{2,1,0:T(8,128)S(1)}, f32[3,8,128]{2,1,0:T(8,128)S(1)}) custom-call(s32[2]{0:T(128)S(1)} %pad_add_fusion.refs_0_, bf16[8,384,384]{2,1,0:T(8,128)(2,1)S(1)} %copy-done, bf16[8,384,384]{2,1,0:T(8,128)(2,1)S(1)} %copy-done.1, bf16[8,384,128]{2,1,0:T(8,128)(2,1)S(1)} %copy-done.3, bf16[8,384,128]{2,1,0:T(8,128)(2,1)S(1)} %copy-done.5, ...), custom_call_target="tpu_custom_call" | custom-call | flops 1585446912 | bytes 4500000 | tf_op jit(solution)/shard_map/pallas_call | solution.py:107
  42.3 3.9 %collective-permute-start.8 = (f32[3,128]{1,0:T(4,128)S(1)}, f32[3,128]{1,0:T(4,128)S(1)}, u32[]{:S(2)}, u32[]{:S(2)}) collective-permute-start(f32[3,128]{1,0:T(4,128)S(1)} %bitcast.44), channel_id=1, source_target_pairs={{4,8},{8,4},{12,16},{16,12},{20,24},{24,20},{28,32},{32,28},{36,40... | collective-permute-start | bytes 4616 | tf_op jit(solution)/shard_map/ppermute | solution.py:25
  46.2 0.9 constant_dynamic-update-slice_fusion.1
  47.1 4.0 %shard_map.96 = (f32[4,384,128]{2,1,0:T(8,128)}, f32[1,8,128]{2,1,0:T(8,128)S(1)}) fusion(f32[4,384,128]{2,1,0:T(8,128)} %constant_dynamic-update-slice_fusion.1, s32[2]{0:T(128)S(1)} %pad_add_fusion.refs_0_, bf16[8,384,384]{2,1,0:T(8,128)(2,1)S(1)} %copy-done, bf16[8,384,384]{2,1,0:T(8,128)(2,1)S(1)} %copy-done.1, bf16[8,384,128]{2,1,0:T(8,128)(2,1)S(1)} %copy-done.4, ...), kind=kCustom, calls=%fused_computation.19 | custom fusion | flops 528482304 | bytes 6885384 | tf_op jit(solution)/shard_map/pallas_call | solution.py:107
  51.0 8.5 %shard_map.95 = (f32[4,384,128]{2,1,0:T(8,128)S(1)}, f32[4,8,128]{2,1,0:T(8,128)S(1)}) custom-call(s32[2]{0:T(128)S(1)} %pad_add_fusion.1.refs_0_, bf16[8,384,384]{2,1,0:T(8,128)(2,1)S(1)} %copy-done, bf16[8,384,384]{2,1,0:T(8,128)(2,1)S(1)} %copy-done.2, bf16[8,384,128]{2,1,0:T(8,128)(2,1)S(1)} %copy-done.4, bf16[8,384,128]{2,1,0:T(8,128)(2,1)S(1)} %copy-done.6, ...), custom_call_target="tpu_custom_call" | custom-call | flops 2113929216 | bytes 6000000 | tf_op jit(solution)/shard_map/pallas_call | solution.py:107
  59.7 3.6 %collective-permute-start.4 = (f32[4,384,128]{2,1,0:T(8,128)}, f32[4,384,128]{2,1,0:T(8,128)S(1)}, u32[]{:S(2)}, u32[]{:S(2)}) collective-permute-start(f32[4,384,128]{2,1,0:T(8,128)} %get-tuple-element.42), channel_id=1, source_target_pairs={{4,8},{8,4},{12,16},{16,12},{20,24},{24,20},{28,32},{32,28},{36,40... | collective-permute-start | bytes 2359304 | tf_op jit(solution)/shard_map/ppermute | solution.py:25
  63.4 1.2 %fusion = f32[1024,128]{1,0:T(8,128)} fusion(f32[32,128]{1,0:T(8,128)S(1)} %concatenate.99, s32[32]{0:T(128)S(1)} %pad_add_fusion.2), kind=kOutput, calls=%fused_computation.7 | convolution fusion | flops 50364416 | bytes 540800 | tf_op jit(solution)/shard_map/dot_general | solution.py:192
  64.6 18.0 %all-to-all-start = ((f32[256,4,128]{2,1,0:T(4,128)}), f32[256,4,128]{2,1,0:T(4,128)S(1)}, u32[]{:S(2)}, u32[]{:S(2)}) async-start(f32[256,4,128]{2,1,0:T(4,128)} %bitcast.13), calls=%async_computation | async-start | bytes 1048576 | tf_op jit(solution)/shard_map/all_to_all | solution.py:193
  82.6 1.3 %broadcast_select_fusion = (f32[4,384,128]{2,1,0:T(8,128)S(1)}, f32[4,384,128]{2,1,0:T(8,128)S(1)}) fusion(f32[4,384,128]{2,1,0:T(8,128)S(1)} %get-tuple-element.11, f32[4,384,128]{2,1,0:T(8,128)} %get-tuple-element.42, pred[]{:T(512)S(6)} %eq.24), kind=kLoop, calls=%fused_computation.9 | loop fusion | flops 393216 | bytes 3145729 | tf_op jit(solution)/shard_map/jit(_where)/select_n | solution.py:142
  84.0 1.9 %pad_maximum_fusion = (f32[8,384,128]{2,1,0:T(8,128)}, f32[8,384,128]{2,1,0:T(8,128)}) fusion(f32[4,384,128]{2,1,0:T(8,128)S(1)} %get-tuple-element.18, f32[4,384,128]{2,1,0:T(8,128)S(1)} %get-tuple-element.20, f32[4,384,128]{2,1,0:T(8,128)S(1)} %get-tuple-element.19, f32[4,384,128]{2,1,0:T(8,128)S(1)} %get-tuple-element.17), kind=kLoop, calls=%fused_computation.1 | loop fusion | flops 786432 | bytes 6291456 | tf_op jit(solution)/shard_map/concatenate | solution.py:203
  85.9 16.7 %all-to-all-done = f32[256,4,128]{2,1,0:T(4,128)S(1)} async-done(((f32[256,4,128]{2,1,0:T(4,128)}), f32[256,4,128]{2,1,0:T(4,128)S(1)}, u32[]{:S(2)}, u32[]{:S(2)}) %all-to-all-start) | async-done | bytes 524320 | tf_op jit(solution)/shard_map/all_to_all | solution.py:193
  104.3 1.0 convolution_add_fusion
  (72 shorter events, 6.2 us)
Async XLA Ops:
  0.6 28.1 %collective-permute-start = (s32[1]{0:T(128)}, s32[1]{0:T(128)}, u32[]{:S(2)}, u32[]{:S(2)}) collective-permute-start(s32[1]{0:T(128)} %param.11), channel_id=1, source_target_pairs={{0,4},{4,8},{8,12},{12,16},{16,20},{20,24},{24,28},{28,32},{32,36}... | collective-permute-start | bytes 20 | tf_op jit(solution)/shard_map/ppermute | solution.py:153
  8.1 2.1 %slice-start.1 = ((bf16[8,384,384]{2,1,0:T(8,128)(2,1)}), bf16[1,384,384]{2,1,0:T(8,128)(2,1)S(1)}, s32[]{:S(2)}) async-start(bf16[8,384,384]{2,1,0:T(8,128)(2,1)} %refs_1_.4), calls=%async_computation.2 | async-start | bytes 589824 | tf_op jit(solution)/shard_map/slice | solution.py:145
  8.1 2.1 %slice-start.4 = ((bf16[8,384,384]{2,1,0:T(8,128)(2,1)}), bf16[1,384,384]{2,1,0:T(8,128)(2,1)S(1)}, s32[]{:S(2)}) async-start(bf16[8,384,384]{2,1,0:T(8,128)(2,1)} %refs_2_.4), calls=%async_computation.5 | async-start | bytes 589824 | tf_op jit(solution)/shard_map/slice | solution.py:146
  8.1 2.1 %slice-start.7 = ((bf16[8,384,128]{2,1,0:T(8,128)(2,1)}), bf16[1,384,128]{2,1,0:T(8,128)(2,1)S(1)}, s32[]{:S(2)}) async-start(bf16[8,384,128]{2,1,0:T(8,128)(2,1)} %refs_3_.4), calls=%async_computation.8 | async-start | bytes 196608 | tf_op jit(solution)/shard_map/slice | solution.py:145
  8.1 2.1 %slice-start.10 = ((bf16[8,384,128]{2,1,0:T(8,128)(2,1)}), bf16[1,384,128]{2,1,0:T(8,128)(2,1)S(1)}, s32[]{:S(2)}) async-start(bf16[8,384,128]{2,1,0:T(8,128)(2,1)} %refs_4_.4), calls=%async_computation.11 | async-start | bytes 196608 | tf_op jit(solution)/shard_map/slice | solution.py:146
  8.2 23.4 %collective-permute-start.1 = (bf16[3,384,512]{2,1,0:T(8,128)(2,1)}, bf16[3,384,512]{2,1,0:T(8,128)(2,1)}, u32[]{:S(2)}, u32[]{:S(2)}) collective-permute-start(bf16[3,384,512]{2,1,0:T(8,128)(2,1)} %maximum_select_fusion.1), channel_id=1, source_target_pairs={{4,8},{8,4},{12,16},{16,12},{20,24},{24,20},{28,32},{32,28},{36,40... | collective-permute-start | bytes 3538952 | tf_op jit(solution)/shard_map/ppermute | solution.py:25
  11.1 36.0 %collective-permute-start.2 = (bf16[1,384,512]{2,1,0:T(8,128)(2,1)}, bf16[1,384,512]{2,1,0:T(8,128)(2,1)}, u32[]{:S(2)}, u32[]{:S(2)}) collective-permute-start(bf16[1,384,512]{2,1,0:T(8,128)(2,1)} %maximum_select_fusion.2), channel_id=1, source_target_pairs={{4,8},{8,4},{12,16},{16,12},{20,24},{24,20},{28,32},{32,28},{36,40... | collective-permute-start | bytes 1179656 | tf_op jit(solution)/shard_map/ppermute | solution.py:25
  14.7 1.6 %slice-start.5 = ((bf16[8,384,384]{2,1,0:T(8,128)(2,1)}), bf16[4,384,384]{2,1,0:T(8,128)(2,1)S(1)}, s32[]{:S(2)}) async-start(bf16[8,384,384]{2,1,0:T(8,128)(2,1)} %refs_2_.4), calls=%async_computation.6 | async-start | bytes 2359296 | tf_op jit(solution)/shard_map/slice | solution.py:146
  14.8 1.7 %slice-start.8 = ((bf16[8,384,128]{2,1,0:T(8,128)(2,1)}), bf16[4,384,128]{2,1,0:T(8,128)(2,1)S(1)}, s32[]{:S(2)}) async-start(bf16[8,384,128]{2,1,0:T(8,128)(2,1)} %refs_3_.4), calls=%async_computation.9 | async-start | bytes 786432 | tf_op jit(solution)/shard_map/slice | solution.py:145
  14.8 1.8 %slice-start.11 = ((bf16[8,384,128]{2,1,0:T(8,128)(2,1)}), bf16[4,384,128]{2,1,0:T(8,128)(2,1)S(1)}, s32[]{:S(2)}) async-start(bf16[8,384,128]{2,1,0:T(8,128)(2,1)} %refs_4_.4), calls=%async_computation.12 | async-start | bytes 786432 | tf_op jit(solution)/shard_map/slice | solution.py:146
  16.6 1.6 %copy-start.7 = (s32[8]{0:T(128)S(1)}, s32[8]{0:T(128)}, u32[]{:S(2)}) copy-start(s32[8]{0:T(128)} %param.12) | copy-start | bytes 100
  16.6 2.1 %copy-start.8 = (s32[8]{0:T(128)S(1)}, s32[8]{0:T(128)}, u32[]{:S(2)}) copy-start(s32[8]{0:T(128)} %param.13) | copy-start | bytes 100
  16.6 15.0 %copy-start = (bf16[8,384,384]{2,1,0:T(8,128)(2,1)S(1)}, bf16[8,384,384]{2,1,0:T(8,128)(2,1)}, u32[]{:S(2)}) copy-start(bf16[8,384,384]{2,1,0:T(8,128)(2,1)} %refs_1_.4) | copy-start | bytes 7077892
  18.1 32.9 %collective-permute-start.3 = (bf16[4,384,512]{2,1,0:T(8,128)(2,1)}, bf16[4,384,512]{2,1,0:T(8,128)(2,1)}, u32[]{:S(2)}, u32[]{:S(2)}) collective-permute-start(bf16[4,384,512]{2,1,0:T(8,128)(2,1)} %maximum_select_fusion), channel_id=1, source_target_pairs={{0,4},{4,0},{8,12},{12,8},{16,20},{20,16},{24,28},{28,24},{32,36},... | collective-permute-start | bytes 4718600 | tf_op jit(solution)/shard_map/ppermute | solution.py:25
  20.7 9.6 %collective-permute-start.6 = (s32[1]{0:T(128)}, s32[1]{0:T(128)}, u32[]{:S(2)}, u32[]{:S(2)}) collective-permute-start(s32[1]{0:T(128)} %bitcast.8), channel_id=1, source_target_pairs={{4,8},{8,4},{12,16},{16,12},{20,24},{24,20},{28,32},{32,28},{36,40... | collective-permute-start | bytes 20 | tf_op jit(solution)/shard_map/ppermute | solution.py:25
  31.6 1.7 %copy-start.1 = (bf16[8,384,384]{2,1,0:T(8,128)(2,1)S(1)}, bf16[8,384,384]{2,1,0:T(8,128)(2,1)}, u32[]{:S(2)}) copy-start(bf16[8,384,384]{2,1,0:T(8,128)(2,1)} %refs_2_.4) | copy-start | bytes 7077892
  35.5 11.6 %copy-start.6 = (bf16[8,384,128]{2,1,0:T(8,128)(2,1)S(1)}, bf16[8,384,128]{2,1,0:T(8,128)(2,1)}, u32[]{:S(2)}) copy-start(bf16[8,384,128]{2,1,0:T(8,128)(2,1)} %refs_4_.4) | copy-start | bytes 2359300
  42.3 4.8 %copy-start.4 = (bf16[8,384,128]{2,1,0:T(8,128)(2,1)S(1)}, bf16[8,384,128]{2,1,0:T(8,128)(2,1)}, u32[]{:S(2)}) copy-start(bf16[8,384,128]{2,1,0:T(8,128)(2,1)} %refs_3_.4) | copy-start | bytes 2359300
  42.3 21.0 %collective-permute-start.8 = (f32[3,128]{1,0:T(4,128)S(1)}, f32[3,128]{1,0:T(4,128)S(1)}, u32[]{:S(2)}, u32[]{:S(2)}) collective-permute-start(f32[3,128]{1,0:T(4,128)S(1)} %bitcast.44), channel_id=1, source_target_pairs={{4,8},{8,4},{12,16},{16,12},{20,24},{24,20},{28,32},{32,28},{36,40... | collective-permute-start | bytes 4616 | tf_op jit(solution)/shard_map/ppermute | solution.py:25
  47.0 4.0 %copy-start.2 = (bf16[8,384,384]{2,1,0:T(8,128)(2,1)S(1)}, bf16[8,384,384]{2,1,0:T(8,128)(2,1)}, u32[]{:S(2)}) copy-start(bf16[8,384,384]{2,1,0:T(8,128)(2,1)} %refs_2_.4) | copy-start | bytes 7077892
  59.6 3.8 %collective-permute-start.7 = (f32[4,128]{1,0:T(4,128)S(1)}, f32[4,128]{1,0:T(4,128)S(1)}, u32[]{:S(2)}, u32[]{:S(2)}) collective-permute-start(f32[4,128]{1,0:T(4,128)S(1)} %bitcast.45), channel_id=1, source_target_pairs={{0,4},{4,0},{8,12},{12,8},{16,20},{20,16},{24,28},{28,24},{32,36},... | collective-permute-start | bytes 6152 | tf_op jit(solution)/shard_map/ppermute | solution.py:25
  59.7 24.2 %collective-permute-start.4 = (f32[4,384,128]{2,1,0:T(8,128)}, f32[4,384,128]{2,1,0:T(8,128)S(1)}, u32[]{:S(2)}, u32[]{:S(2)}) collective-permute-start(f32[4,384,128]{2,1,0:T(8,128)} %get-tuple-element.42), channel_id=1, source_target_pairs={{4,8},{8,4},{12,16},{16,12},{20,24},{24,20},{28,32},{32,28},{36,40... | collective-permute-start | bytes 2359304 | tf_op jit(solution)/shard_map/ppermute | solution.py:25
  63.3 20.6 %collective-permute-start.5 = (f32[4,384,128]{2,1,0:T(8,128)S(1)}, f32[4,384,128]{2,1,0:T(8,128)S(1)}, u32[]{:S(2)}, u32[]{:S(2)}) collective-permute-start(f32[4,384,128]{2,1,0:T(8,128)S(1)} %get-tuple-element.11), channel_id=1, source_target_pairs={{0,4},{4,0},{8,12},{12,8},{16,20},{20,16},{24,28},{28,24},{32,36},... | collective-permute-start | bytes 2359304 | tf_op jit(solution)/shard_map/ppermute | solution.py:25
  64.6 38.0 %all-to-all-start = ((f32[256,4,128]{2,1,0:T(4,128)}), f32[256,4,128]{2,1,0:T(4,128)S(1)}, u32[]{:S(2)}, u32[]{:S(2)}) async-start(f32[256,4,128]{2,1,0:T(4,128)} %bitcast.13), calls=%async_computation | async-start | bytes 1048576 | tf_op jit(solution)/shard_map/all_to_all | solution.py:193
  (7 other events, 9.2 us)

commit v2 on v0

v2 whole, which is shorter than its diff:
```python
import functools
import math

import jax
import jax.numpy as jnp
from jax import lax
from jax.experimental import pallas as pl
from jax.experimental.pallas import tpu as pltpu
from jax.sharding import PartitionSpec as P

F = 384
COLS = 128
WIDE = F + COLS
FC = 8
HALF = FC // 2
EARLY = 2
ITERS = 4
CO_DEV = 8
NOTE = 16
TAIL = 8
BOTH = ("sub", "grp")
BF, F32, I32 = jnp.bfloat16, jnp.float32, jnp.int32

ANY = pl.BlockSpec(memory_space=pl.ANY)
VM = pl.BlockSpec(memory_space=pltpu.VMEM)
SM = pl.BlockSpec(memory_space=pltpu.SMEM)
PARAMS = pltpu.CompilerParams(vmem_limit_bytes=16 * 1024 * 1024)


def vmem(shape, dtype):
    return pltpu.VMEM(shape, dtype)


def in_vmem(value):
    return pltpu.with_memory_space_constraint(value, pltpu.VMEM)


def in_hbm(value):
    return pltpu.with_memory_space_constraint(value, pltpu.HBM)


def swapped(value, odd):
    size = lax.axis_size("sub")
    pairs = []
    for i in range(size):
        j = ((i + 1) ^ 1) - 1 if odd else i ^ 1
        if 0 <= j < size:
            pairs.append((i, j))
    return lax.ppermute(value, "sub", pairs)


def load_kernel(plan, noted, info, su, sl, ru, rl, *rest):
    outs, sem = rest[-len(plan[1]) - 1 : -1], rest[-1]
    jobs, slot, place = [], 0, 0
    for kind, first, count, flag in plan[0]:
        use_up = info[flag] == 1
        for j in range(count):
            if kind == "pack":
                dst_m = outs[place].at[pl.ds(j * F, F), pl.ds(0, F)]
                dst_r = outs[place].at[pl.ds(j * F, F), pl.ds(F, COLS)]
                up, low = HALF + first + j, first + j
            else:
                dst_m, dst_r = outs[place].at[j], outs[place + 1].at[j]
                up, low = first + j, HALF + first + j
            jobs.append((use_up, up, low, dst_m, dst_r, slot))
            slot += 1
        place += 1 if kind == "pack" else 2
    for use_up, up, low, dst_m, dst_r, s in jobs:

        @pl.when(use_up)
        def _():
            pltpu.make_async_copy(su.at[up], dst_m, sem.at[0, s]).start()
            pltpu.make_async_copy(ru.at[up], dst_r, sem.at[1, s]).start()

        @pl.when(jnp.logical_not(use_up))
        def _():
            pltpu.make_async_copy(sl.at[low], dst_m, sem.at[0, s]).start()
            pltpu.make_async_copy(rl.at[low], dst_r, sem.at[1, s]).start()

    if noted:
        line = lax.broadcasted_iota(I32, (NOTE, WIDE), 0)
        note = jnp.zeros((NOTE, WIDE), I32)
        for i in range(1 + 2 * HALF):
            note = jnp.where(line == i, info[2 + i], note)
        rows = plan[0][0][2] * F
        outs[0][rows : rows + NOTE, :] = note.astype(F32).astype(BF)
    for use_up, up, low, dst_m, dst_r, s in jobs:
        pltpu.make_async_copy(su.at[up], dst_m, sem.at[0, s]).wait()
        pltpu.make_async_copy(ru.at[up], dst_r, sem.at[1, s]).wait()


def load(plan, noted, info, blocks, after=None):
    shapes, faces = [], 0
    for kind, first, count, flag in plan:
        faces += count
        if kind == "pack":
            extra = NOTE if noted and not shapes else 0
            shapes.append(vmem((count * F + extra, WIDE), BF))
        else:
            shapes += [vmem((count, F, F), BF), vmem((count, F, COLS), BF)]
    extra = [] if after is None else [in_vmem(after)]
    return pl.pallas_call(
        functools.partial(load_kernel, (plan, shapes), noted),
        in_specs=[SM] + [ANY] * (4 + len(extra)),
        out_specs=[VM] * len(shapes),
        out_shape=shapes,
        scratch_shapes=[pltpu.SemaphoreType.DMA((2, faces))],
        compiler_params=PARAMS,
    )(info, *[in_hbm(b) for b in blocks], *extra)


def split(value):
    high = value.astype(BF)
    return high, (value - high.astype(F32)).astype(BF)


def three(row):
    high, low = split(row)
    high, low = high.astype(F32), low.astype(F32)
    return high, low, row - high - low


def mm(a, b):
    return jnp.dot(a, b, preferred_element_type=F32)


def prepare(own_m, own_r, oth_m, oth_r):
    source = mm(own_m, own_r) + mm(oth_m, oth_r)
    own_f, oth_f = own_m.astype(F32), oth_m.astype(F32)
    sums = three(jnp.sum(own_f, axis=0, keepdims=True))
    sums += three(jnp.sum(oth_f, axis=0, keepdims=True))
    matrix = own_f + oth_f
    eye = lax.broadcasted_iota(I32, (128, 128), 0) == lax.broadcasted_iota(I32, (128, 128), 1)
    pivots, bands = [], []
    for b in range(F // 128):
        band = matrix[b * 128 : (b + 1) * 128]
        parts = [band[:, c * 128 : (c + 1) * 128] for c in range(F // 128)]
        pivots.append(jnp.sum(jnp.where(eye, parts[b], 0.0), axis=1, keepdims=True))
        parts[b] = jnp.where(eye, 0.0, parts[b])
        bands.append(jnp.concatenate(parts, 1))
    inverse = jnp.broadcast_to(1.0 / jnp.concatenate(pivots, 0), (F, COLS))
    high, low = split(jnp.concatenate(bands, 0))
    return source, inverse, high, low, sums


def sweep(x, state):
    source, inverse, high, low, _ = state
    x_h, x_l = split(x)
    wide = mm(high, jnp.concatenate([x_h, x_l], 1))
    return (source - (wide[:, :COLS] + wide[:, COLS:] + mm(low, x_h))) * inverse


def fluxes(x, own_r, oth_r, sums):
    line = lax.broadcasted_iota(I32, (16, F), 0)
    left = jnp.zeros((16, F), F32)
    for i, row in enumerate(sums):
        left = jnp.where(line == i, row, left)
    x_h, x_l = split(x)
    prod = mm(left.astype(BF), jnp.concatenate([own_r, oth_r, x_h, x_l], 1))[:8]
    moved = prod[:, 2 * COLS : 3 * COLS] + prod[:, 3 * COLS :]
    line = lax.broadcasted_iota(I32, (8, COLS), 0)
    scale = 1.0 / math.sqrt(F)
    own = jnp.where(line < 3, prod[:, :COLS] - moved, 0.0)
    oth = jnp.where((line >= 3) & (line < 6), prod[:, COLS : 2 * COLS] - moved, 0.0)
    return (
        jnp.sum(own, axis=0, keepdims=True) * scale,
        jnp.sum(oth, axis=0, keepdims=True) * scale,
    )


def solve_kernel(first, count, back, own_first, info, own_m, own_r, got, noted, *rest):
    x_out, flux_out = rest[-2:]
    use_up = info[0] == 1
    base = jnp.where(use_up, 0, HALF)
    rows = noted.shape[0] - NOTE
    told = noted[rows : rows + NOTE, :COLS].astype(F32)[:1]
    counts = jnp.where(info[1] == 1, info[2].astype(F32), told)
    flux_out[...] = jnp.zeros_like(flux_out)
    if back:
        x_out[HALF * F :, :] = jnp.zeros((TAIL, COLS), F32)
    for start in range(0, count, 2):
        faces = range(start, min(start + 2, count))
        others = [got[i * F : (i + 1) * F, :] for i in faces]
        states = [
            prepare(own_m[own_first + i], own_r[own_first + i], o[:, :F], o[:, F:])
            for i, o in zip(faces, others)
        ]
        xs = [s[0] * s[1] for s in states]
        for _ in range(ITERS):
            xs = [sweep(x, s) for x, s in zip(xs, states)]
        for i, x, s, o in zip(faces, xs, states, others):
            k = first + i
            live = (base + k).astype(F32) < counts
            x_out[k * F : (k + 1) * F, :] = jnp.where(live, x, 0.0)
            mine, theirs = fluxes(x, own_r[own_first + i], o[:, F:], s[4])
            flux_out[k : k + 1, :] = jnp.where(live, mine, 0.0)
            theirs = jnp.where(live, theirs, 0.0)
            if back:
                x_out[HALF * F + k : HALF * F + k + 1, :] = theirs
            else:
                flux_out[HALF + k : HALF + k + 1, :] = theirs


def solve(first, count, back, info, own_m, own_r, got, noted, after=(), into=None):
    args = [in_vmem(v) for v in (own_m, own_r, got, noted, *after)]
    alias = {}
    if into is not None:
        args.append(in_vmem(into))
        alias = {len(args): 0}
    return pl.pallas_call(
        functools.partial(solve_kernel, first, count, back, first),
        in_specs=[SM] + [VM] * len(args),
        out_specs=[VM, VM],
        out_shape=[vmem((HALF * F + (TAIL if back else 0), COLS), F32), vmem((2 * HALF, COLS), F32)],
        input_output_aliases=alias,
        compiler_params=PARAMS,
        cost_estimate=pl.CostEstimate(
            flops=count * 14 * 2 * F * F * COLS, bytes_accessed=count * 1000000, transcendentals=0
        ),
    )(info, *args)


SLOTS = 4


def encode_kernel(table, flux_e, back_e, flux_a, flux_b, out, codes, heads):
    rows = jnp.concatenate(
        [flux_e[:HALF], back_e[HALF * F : HALF * F + HALF, :], flux_a[...] + flux_b[...]], 0
    )
    top = jnp.max(jnp.abs(rows), axis=1, keepdims=True)
    step = jnp.broadcast_to(jnp.maximum(top, 1e-28) * (1.0 / 32767.0), rows.shape)
    power = jnp.clip(jnp.floor(jnp.log(step) * (1.0 / math.log(2.0))), -120.0, 120.0)
    unit = jnp.exp2(power)
    digits = jnp.round(step / unit * float(2**21))
    step = digits * unit * (2.0**-21)
    codes[...] = jnp.clip(jnp.round(rows / step), -32767.0, 32767.0).astype(I32)
    heads[...] = digits.astype(I32) * 256 + (power.astype(I32) + 128)
    out[...] = jnp.zeros_like(out)
    lane = lax.broadcasted_iota(I32, (1, COLS), 1)
    for i in range(4 * HALF):
        owner, rank, local, valid = table[0, i], table[1, i], table[2, i], table[3, i] == 1
        code = codes[i : i + 1, :]
        code = jnp.where(rank % 2 == 0, code * 65536, code & 65535)
        code = jnp.where(valid, code, 0)
        head = jnp.where((lane == rank * CO_DEV + local) & valid, heads[i : i + 1, :], 0)
        here = jnp.concatenate(
            [jnp.where(rank < 2, code, 0), jnp.where(rank >= 2, code, 0), head], 1
        )
        out[owner] = out[owner] | here


def encode(table, flux_e, back_e, flux_a, flux_b, devices):
    args = [in_vmem(v) for v in (flux_e, back_e, flux_a, flux_b)]
    return pl.pallas_call(
        encode_kernel,
        in_specs=[SM] + [VM] * 4,
        out_specs=VM,
        out_shape=vmem((devices, 1, 3 * COLS), I32),
        scratch_shapes=[pltpu.VMEM((4 * HALF, COLS), I32), pltpu.VMEM((4 * HALF, COLS), I32)],
        compiler_params=PARAMS,
    )(table, *args)


def decode_kernel(got, out):
    n = got.shape[0]
    words = [got[:, 0, c * COLS : (c + 1) * COLS] for c in range(3)]
    head = words[2]
    power = (head & 255).astype(F32) - 128.0
    step = jnp.where(head == 0, 0.0, (head >> 8).astype(F32) * (2.0**-21) * jnp.exp2(power))
    parts = []
    for w in words[:2]:
        for q in (w >> 16, (w << 16) >> 16):
            high = q >> 8
            parts.append((high.astype(F32) * 256.0).astype(BF))
            parts.append((q - high * 256).astype(F32).astype(BF))
    right = jnp.concatenate(parts, 1)
    total = jnp.zeros((CO_DEV, COLS), F32)
    prods = 0.0
    for piece in three(step):
        prods = prods + lax.dot_general(
            piece.astype(BF), right, (((0,), (0,)), ((), ())), preferred_element_type=F32
        )
    for r in range(SLOTS):
        rows = prods[r * CO_DEV : (r + 1) * CO_DEV]
        total = total + rows[:, 2 * r * COLS : (2 * r + 1) * COLS]
        total = total + rows[:, (2 * r + 1) * COLS : (2 * r + 2) * COLS]
    out[...] = total


def decode(arrived):
    return pl.pallas_call(
        decode_kernel,
        in_specs=[VM],
        out_specs=VM,
        out_shape=jax.ShapeDtypeStruct((CO_DEV, COLS), F32),
        compiler_params=PARAMS,
    )(in_vmem(arrived))


def shards(schur_up, schur_low, resid_up, resid_low, counts, coarse_up, coarse_low):
    subs = lax.axis_size("sub")
    devices = lax.axis_size(BOTH)
    s = lax.axis_index("sub")
    odd = (s % 2).astype(I32)
    even = 1 - odd
    blocks = (schur_up, schur_low, resid_up, resid_low)

    def pick(if_odd, if_even):
        return jnp.where(odd == 1, if_odd, if_even)

    sent = pick(coarse_up[HALF:], coarse_low[:HALF])
    info = jnp.concatenate([jnp.stack([odd, even]), counts, sent // 64, sent % 64]).astype(I32)

    (pack_a,) = load([("pack", 0, EARLY, 0)], True, info, blocks)
    got_a = swapped(pack_a, True)
    pack_e, own_e_m, own_e_r = load(
        [("pack", 0, HALF, 1), ("keep", 0, HALF, 1)], True, info, blocks, pack_a
    )
    got_e = swapped(pack_e, False)
    pack_b, own_o_m, own_o_r = load(
        [("pack", EARLY, HALF - EARLY, 0), ("keep", 0, HALF, 0)], False, info, blocks, pack_e
    )
    got_b = swapped(pack_b, True)

    count = jnp.where(s < subs - 1, counts[0], 0)
    info_e = jnp.stack([even, even, count])
    info_o = jnp.stack([odd, odd, count])

    x_e, flux_e = solve(0, HALF, True, info_e, own_e_m, own_e_r, got_e, got_e)
    back_e = swapped(x_e, False)
    x_a, flux_a = solve(0, EARLY, False, info_o, own_o_m, own_o_r, got_a, got_a, (flux_e,))
    x_o, flux_b = solve(
        EARLY, HALF - EARLY, False, info_o, own_o_m, own_o_r, got_b, got_a, (flux_a,), x_a
    )
    back_o = swapped(x_o, True)

    note = got_a[EARLY * F + 1 : EARLY * F + 1 + 2 * HALF, 0].astype(I32)
    theirs = note[:HALF] * 64 + note[HALF:]
    targets = jnp.concatenate(
        [
            pick(coarse_low[HALF:], coarse_up[:HALF]),
            pick(coarse_low[:HALF], coarse_up[HALF:]),
            pick(coarse_up[:HALF], coarse_low[HALF:]),
            theirs,
        ]
    )
    n = 4 * HALF
    order = jnp.arange(n, dtype=I32)
    paired = (order < n - HALF) | ((s > 0) & (s < subs - 1))
    owner, local = targets // CO_DEV, targets % CO_DEV
    same = (owner[:, None] == owner[None, :]) & (order[None, :] < order[:, None])
    rank = jnp.minimum(jnp.sum(same, axis=1), SLOTS - 1).astype(I32)
    table = jnp.stack([owner, rank, local, paired.astype(I32)])

    parcels = encode(table, flux_e, back_e, flux_a, flux_b, devices)
    arrived = lax.all_to_all(parcels, BOTH, 0, 0, tiled=True)
    coarse = decode(arrived)

    def panels(value):
        return value[: HALF * F].reshape(HALF, F, COLS)

    x_e, back_e, x_o, back_o = map(panels, (x_e, back_e, x_o, back_o))
    average_up = jnp.concatenate([pick(x_o, x_e), pick(back_o, back_e)], 0)
    average_low = jnp.concatenate([pick(back_e, back_o), pick(x_e, x_o)], 0)
    return (average_up, average_low, coarse)


def solution(mesh):
    return jax.shard_map(
        shards,
        mesh=mesh,
        in_specs=(
            P(BOTH, None, None),
            P(BOTH, None, None),
            P(BOTH, None, None),
            P(BOTH, None, None),
            P(BOTH),
            P(BOTH),
            P(BOTH),
        ),
        out_specs=(
            P(BOTH, None, None),
            P(BOTH, None, None),
            P(BOTH, None),
        ),
        check_vma=False,
    )
```

time: 406 us -> 81.6 us (0.20)
  waiting for transfers between devices: 294 us -> 16.8 us
  local copies, waits for them, and re-layouts: 46.9 us -> 5.88 us
  matrix products: 32.6 us -> 0 us
  Pallas kernels: 0 us -> 24.7 us
  starting transfers between devices: 12.9 us -> 26.8 us
  between operations: 14.9 us -> 1.47 us
    unnamed x2 -> x0, waiting for transfers between devices: 261 us -> none
    add x1 -> x0, local copies, waits for them, and re-layouts: 36 us -> none  [solve_faces(): matrix = lower_side.astype(jnp.float32) + upper_side.astype(jnp.float32)]
    dot_general x9 -> x0, matrix products: 32.6 us -> none  [the longest x4 22.5 us: solve_faces(): jnp.einsum('kab,kbp->kap', matrix, iterate, precision=lax.Precision.HIGHEST)]
    ppermute x4 -> x5, waiting for transfers between devices: 33 us -> 2.9 us  [swapped(): return lax.ppermute(value, 'sub', pairs)]
    pallas_call x0 -> x8, Pallas kernels: none -> 24.7 us  [the longest x3 12 us: solve(): pl.pallas_call(functools.partial(solve_kernel, first, count, back, first)...]
    all_to_all x0 -> x1, starting transfers between devices: none -> 15.9 us  [shards(): arrived = lax.all_to_all(parcels, BOTH, 0, 0, tiled=True)]
    all_to_all x0 -> x1, waiting for transfers between devices: none -> 13.9 us  [shards(): arrived = lax.all_to_all(parcels, BOTH, 0, 0, tiled=True)]
    gather x2 -> x0, local copies, waits for them, and re-layouts: 8.47 us -> none  [solve_faces(): pivots = jnp.diagonal(matrix, axis1=1, axis2=2)[:, :, None]]
  transfers between devices with their start and end apart: 5 -> 6, of which waited for: 3 -> 2; matrix products, arithmetic and copies ran while one was open for 13% -> 5% of each run, Pallas kernels for 0% -> 21%
where the time goes in v2:
time: 81.6 us; the launch traced here: 81.1 us
  starting transfers between devices  26.8 us (33%)
  Pallas kernels  24.7 us (30%)
  waiting for transfers between devices  16.8 us (21%)
  local copies, waits for them, and re-layouts  5.88 us (7%)
  other arithmetic  5.48 us (7%)
  between operations  1.47 us (2%)
    all_to_all x1, starting transfers between devices, shards(): arrived = lax.all_to_all(parcels, BOTH, 0, 0, tiled=True)  15.9 us
    all_to_all x1, waiting for transfers between devices, shards(): arrived = lax.all_to_all(parcels, BOTH, 0, 0, tiled=True)  13.9 us
    pallas_call x3, Pallas kernels, solve(): pl.pallas_call(functools.partial(solve_kernel, first, count, back, first)...  12 us
    ppermute x5, starting transfers between devices, swapped(): return lax.ppermute(value, 'sub', pairs)  10.9 us
    pallas_call x3, Pallas kernels, load(): pl.pallas_call(functools.partial(load_kernel, (plan, shapes), noted), in_...  7.34 us
    unnamed x16, local copies, waits for them, and re-layouts  5.8 us
    pallas_call x1, Pallas kernels, decode(): pl.pallas_call(decode_kernel, in_specs=[VM], out_specs=VM, out_shape=jax....  3.84 us
    ppermute x5, waiting for transfers between devices, swapped(): return lax.ppermute(value, 'sub', pairs)  2.9 us
  transfers between devices with their start and end apart: 6, of which 2 were waited for; matrix products, arithmetic and copies ran while one was open for 5% of the time, Pallas kernels for 21%

profile of v2, /device:TPU:1, one launch (start us, length us, event | category | flops | bytes accessed | tf_op | source)
XLA Modules:
  0.0 81.1 jit_solution(13363673407767231686)
XLA Ops:
  1.3 0.8 %and_select_fusion.3 = (s32[4]{0:T(128)S(1)}, s32[4]{0:T(128)S(1)}, s32[4]{0:T(128)S(1)}, s32[4]{0:T(128)S(1)}, s32[4]{0:T(128)S(1)}) fusion(s32[8]{0:T(128)} %param.13, s32[8]{0:T(128)} %param.12, pred[]{:T(512)S(6)} %eq.14), kind=kLoop, calls=%fused_computation.16 | loop fusion | flops 60 | bytes 145 | tf_op jit(solution)/shard_map/jit(remainder)/select_n | solution.py:312
  2.1 0.8 and_select_fusion.4
  2.9 1.7 %shard_map.94.rest_0_ = bf16[784,512]{1,0:T(8,128)(2,1)S(1)} custom-call(s32[11]{0:T(128)S(1)} %concatenate.77.info, bf16[8,384,384]{2,1,0:T(8,128)(2,1)} %su.5, bf16[8,384,384]{2,1,0:T(8,128)(2,1)} %sl.5, bf16[8,384,128]{2,1,0:T(8,128)(2,1)} %ru.5, bf16[8,384,128]{2,1,0:T(8,128)(2,1)} %rl.5), custom_call_target="tpu_custom_call" | custom-call | tf_op jit(solution)/shard_map/pallas_call | solution.py:102
  4.6 2.5 %shard_map.95 = (bf16[1552,512]{1,0:T(8,128)(2,1)S(1)}, bf16[4,384,384]{2,1,0:T(8,128)(2,1)S(1)}, bf16[4,384,128]{2,1,0:T(8,128)(2,1)S(1)}) custom-call(s32[11]{0:T(128)S(1)} %concatenate.77.info, bf16[8,384,384]{2,1,0:T(8,128)(2,1)} %su.5, bf16[8,384,384]{2,1,0:T(8,128)(2,1)} %sl.5, bf16[8,384,128]{2,1,0:T(8,128)(2,1)} %ru.5, bf16[8,384,128]{2,1,0:T(8,128)(2,1)} %rl.5, ...), custom_call_target="tpu_custom_call" | custom-call | tf_op jit(solution)/shard_map/pallas_call | solution.py:102
  7.2 1.0 %copy-done.4 = bf16[4,384,384]{2,1,0:T(8,128)(2,1)} copy-done((bf16[4,384,384]{2,1,0:T(8,128)(2,1)}, bf16[4,384,384]{2,1,0:T(8,128)(2,1)S(1)}, u32[]{:S(2)}) %copy-start.4) | copy-done | bytes 1179672
  8.2 0.8 copy-done.6
  9.0 3.2 %collective-permute-start.2 = (bf16[1552,512]{1,0:T(8,128)(2,1)S(1)}, bf16[1552,512]{1,0:T(8,128)(2,1)}, u32[]{:S(2)}, u32[]{:S(2)}) collective-permute-start(bf16[1552,512]{1,0:T(8,128)(2,1)S(1)} %get-tuple-element.15.rest_0_), channel_id=1, source_target_pairs={{0,4},{4,0},{8,12},{12,8},{16,20},{20,16},{24,28},{28,24},{32,36},... | collective-permute-start | bytes 4767752 | tf_op jit(solution)/shard_map/ppermute | solution.py:49
  12.2 1.9 %collective-permute-start.1 = (bf16[784,512]{1,0:T(8,128)(2,1)S(1)}, bf16[784,512]{1,0:T(8,128)(2,1)S(1)}, u32[]{:S(2)}, u32[]{:S(2)}) collective-permute-start(bf16[784,512]{1,0:T(8,128)(2,1)S(1)} %shard_map.94.rest_0_), channel_id=1, source_target_pairs={{4,8},{8,4},{12,16},{16,12},{20,24},{24,20},{28,32},{32,28},{36,40... | collective-permute-start | bytes 2408456 | tf_op jit(solution)/shard_map/ppermute | solution.py:49
  14.1 3.1 %shard_map.96 = (bf16[768,512]{1,0:T(8,128)(2,1)}, bf16[4,384,384]{2,1,0:T(8,128)(2,1)S(1)}, bf16[4,384,128]{2,1,0:T(8,128)(2,1)S(1)}) custom-call(s32[11]{0:T(128)S(1)} %concatenate.77.info, bf16[8,384,384]{2,1,0:T(8,128)(2,1)} %su.5, bf16[8,384,384]{2,1,0:T(8,128)(2,1)} %sl.5, bf16[8,384,128]{2,1,0:T(8,128)(2,1)} %ru.5, bf16[8,384,128]{2,1,0:T(8,128)(2,1)} %rl.5, ...), custom_call_target="tpu_custom_call" | custom-call | tf_op jit(solution)/shard_map/pallas_call | solution.py:102
  17.3 1.0 %copy-done = bf16[4,384,384]{2,1,0:T(8,128)(2,1)} copy-done((bf16[4,384,384]{2,1,0:T(8,128)(2,1)}, bf16[4,384,384]{2,1,0:T(8,128)(2,1)S(1)}, u32[]{:S(2)}) %copy-start) | copy-done | bytes 1179672
  19.0 3.6 %collective-permute-start = (bf16[768,512]{1,0:T(8,128)(2,1)}, bf16[768,512]{1,0:T(8,128)(2,1)}, u32[]{:S(2)}, u32[]{:S(2)}) collective-permute-start(bf16[768,512]{1,0:T(8,128)(2,1)} %get-tuple-element.18), channel_id=1, source_target_pairs={{4,8},{8,4},{12,16},{16,12},{20,24},{24,20},{28,32},{32,28},{36,40... | collective-permute-start | bytes 2359304 | tf_op jit(solution)/shard_map/ppermute | solution.py:49
  22.8 2.9 %collective-permute-done.1.got.noted = bf16[784,512]{1,0:T(8,128)(2,1)S(1)} collective-permute-done((bf16[784,512]{1,0:T(8,128)(2,1)S(1)}, bf16[784,512]{1,0:T(8,128)(2,1)S(1)}, u32[]{:S(2)}, u32[]{:S(2)}) %collective-permute-start.1) | collective-permute-done | bytes 802848 | tf_op jit(solution)/shard_map/ppermute | solution.py:49
  26.1 1.3 %copy-done.5 = bf16[4,384,384]{2,1,0:T(8,128)(2,1)S(1)} copy-done((bf16[4,384,384]{2,1,0:T(8,128)(2,1)S(1)}, bf16[4,384,384]{2,1,0:T(8,128)(2,1)}, u32[]{:S(2)}) %copy-start.5) | copy-done | bytes 1179672
  27.4 1.0 %copy-done.7 = bf16[4,384,128]{2,1,0:T(8,128)(2,1)S(1)} copy-done((bf16[4,384,128]{2,1,0:T(8,128)(2,1)S(1)}, bf16[4,384,128]{2,1,0:T(8,128)(2,1)}, u32[]{:S(2)}) %copy-start.7) | copy-done | bytes 393240
  28.4 6.1 %shard_map.97 = (f32[1544,128]{1,0:T(8,128)S(1)}, f32[8,128]{1,0:T(8,128)S(1)}) custom-call(s32[3]{0:T(128)S(1)} %add_add_fusion.1.info, bf16[4,384,384]{2,1,0:T(8,128)(2,1)S(1)} %copy-done.5, bf16[4,384,128]{2,1,0:T(8,128)(2,1)S(1)} %copy-done.7, bf16[1552,512]{1,0:T(8,128)(2,1)} %collective-permute-done.2.got.noted, ...), custom_call_target="tpu_custom_call" | custom-call | flops 2113929216 | bytes 4000000 | tf_op jit(solution)/shard_map/pallas_call | solution.py:210
  34.7 2.6 %shard_map.98 = (f32[1536,128]{1,0:T(8,128)S(1)}, f32[8,128]{1,0:T(8,128)S(1)}) custom-call(s32[3]{0:T(128)S(1)} %add_add_fusion.info, bf16[4,384,384]{2,1,0:T(8,128)(2,1)S(1)} %copy-done.1, bf16[4,384,128]{2,1,0:T(8,128)(2,1)S(1)} %copy-done.3, bf16[784,512]{1,0:T(8,128)(2,1)S(1)} %collective-permute-done.1.got.noted, ...), custom_call_target="tpu_custom_call" | custom-call | flops 1056964608 | bytes 2000000 | tf_op jit(solution)/shard_map/pallas_call | solution.py:210
  37.4 3.2 %shard_map.99 = (f32[1536,128]{1,0:T(8,128)S(1)}, f32[8,128]{1,0:T(8,128)S(1)}) custom-call(s32[3]{0:T(128)S(1)} %add_add_fusion.info, bf16[4,384,384]{2,1,0:T(8,128)(2,1)S(1)} %copy-done.1, bf16[4,384,128]{2,1,0:T(8,128)(2,1)S(1)} %copy-done.3, bf16[768,512]{1,0:T(8,128)(2,1)} %collective-permute-done.got, ...), custom_call_target="tpu_custom_call", output_to_operand_aliasing={{0}: (6, {})} | custom-call | flops 1056964608 | bytes 2000000 | tf_op jit(solution)/shard_map/pallas_call | solution.py:210
  40.6 2.1 %collective-permute-start.3 = (f32[1536,128]{1,0:T(8,128)S(1)}, f32[1536,128]{1,0:T(8,128)}, u32[]{:S(2)}, u32[]{:S(2)}) collective-permute-start(f32[1536,128]{1,0:T(8,128)S(1)} %get-tuple-element.24), channel_id=1, source_target_pairs={{4,8},{8,4},{12,16},{16,12},{20,24},{24,20},{28,32},{32,28},{36,40... | collective-permute-start | bytes 2359304 | tf_op jit(solution)/shard_map/ppermute | solution.py:49
  42.7 1.5 %shard_map.100 = s32[256,1,384]{2,1,0:T(1,128)} custom-call(s32[4,16]{1,0:T(4,128)S(1)} %pad_add_fusion.table, f32[8,128]{1,0:T(8,128)S(1)} %get-tuple-element.21.rest_0_.flux_e, f32[1544,128]{1,0:T(8,128)S(1)} %collective-permute-done.4.back_e, f32[8,128]{1,0:T(8,128)S(1)} %get-tuple-element.22.rest_0_.flux_a, f32[8,128]{1,0:T(8,128)S(1)} %get-tuple-element.26.flux_b), custom_call_target="tpu_custom_call" | custom-call | tf_op jit(solution)/shard_map/pallas_call | solution.py:254
  44.2 15.9 %all-to-all-start = ((s32[256,1,384]{2,1,0:T(1,128)}), s32[256,1,384]{2,1,0:T(1,128)S(1)}, u32[]{:S(2)}, u32[]{:S(2)}) async-start(s32[256,1,384]{2,1,0:T(1,128)} %shard_map.100), calls=%async_computation | async-start | bytes 786432 | tf_op jit(solution)/shard_map/all_to_all | solution.py:356
  60.3 1.2 %slice_select_fusion = (f32[1536,128]{1,0:T(8,128)S(1)}, f32[1536,128]{1,0:T(8,128)S(1)}) fusion(f32[1536,128]{1,0:T(8,128)} %collective-permute-done.3, f32[1544,128]{1,0:T(8,128)S(1)} %collective-permute-done.4.back_e, pred[]{:T(512)S(6)} %eq.14), kind=kLoop, calls=%fused_computation.2 | loop fusion | flops 393216 | bytes 3145729 | tf_op jit(solution)/shard_map/jit(_where)/select_n | solution.py:309
  61.5 1.9 %pad_maximum_fusion = (f32[8,384,128]{2,1,0:T(8,128)}, f32[8,384,128]{2,1,0:T(8,128)}) fusion(f32[4,384,128]{2,1,0:T(8,128)S(1)} %bitcast.18, f32[4,384,128]{2,1,0:T(8,128)S(1)} %bitcast.16, f32[4,384,128]{2,1,0:T(8,128)S(1)} %bitcast.15, f32[4,384,128]{2,1,0:T(8,128)S(1)} %bitcast.17), kind=kLoop, calls=%fused_computation | loop fusion | flops 786432 | bytes 6291456 | tf_op jit(solution)/shard_map/concatenate | solution.py:363
  63.4 13.9 %all-to-all-done.got = s32[256,1,384]{2,1,0:T(1,128)S(1)} async-done(((s32[256,1,384]{2,1,0:T(1,128)}), s32[256,1,384]{2,1,0:T(1,128)S(1)}, u32[]{:S(2)}, u32[]{:S(2)}) %all-to-all-start) | async-done | bytes 393248 | tf_op jit(solution)/shard_map/all_to_all | solution.py:356
  77.3 3.8 %shard_map.101 = f32[8,128]{1,0:T(8,128)} custom-call(s32[256,1,384]{2,1,0:T(1,128)S(1)} %all-to-all-done.got), custom_call_target="tpu_custom_call" | custom-call | tf_op jit(solution)/shard_map/pallas_call | solution.py:291
  (29 shorter events, 1.7 us)
Async XLA Ops:
  7.2 1.0 %copy-start.4 = (bf16[4,384,384]{2,1,0:T(8,128)(2,1)}, bf16[4,384,384]{2,1,0:T(8,128)(2,1)S(1)}, u32[]{:S(2)}) copy-start(bf16[4,384,384]{2,1,0:T(8,128)(2,1)S(1)} %get-tuple-element.19.own_m) | copy-start | bytes 3538948
  8.2 0.8 copy-start.6
  9.0 17.1 %collective-permute-start.2 = (bf16[1552,512]{1,0:T(8,128)(2,1)S(1)}, bf16[1552,512]{1,0:T(8,128)(2,1)}, u32[]{:S(2)}, u32[]{:S(2)}) collective-permute-start(bf16[1552,512]{1,0:T(8,128)(2,1)S(1)} %get-tuple-element.15.rest_0_), channel_id=1, source_target_pairs={{0,4},{4,0},{8,12},{12,8},{16,20},{20,16},{24,28},{28,24},{32,36},... | collective-permute-start | bytes 4767752 | tf_op jit(solution)/shard_map/ppermute | solution.py:49
  12.2 13.5 %collective-permute-start.1 = (bf16[784,512]{1,0:T(8,128)(2,1)S(1)}, bf16[784,512]{1,0:T(8,128)(2,1)S(1)}, u32[]{:S(2)}, u32[]{:S(2)}) collective-permute-start(bf16[784,512]{1,0:T(8,128)(2,1)S(1)} %shard_map.94.rest_0_), channel_id=1, source_target_pairs={{4,8},{8,4},{12,16},{16,12},{20,24},{24,20},{28,32},{32,28},{36,40... | collective-permute-start | bytes 2408456 | tf_op jit(solution)/shard_map/ppermute | solution.py:49
  17.2 1.0 %copy-start = (bf16[4,384,384]{2,1,0:T(8,128)(2,1)}, bf16[4,384,384]{2,1,0:T(8,128)(2,1)S(1)}, u32[]{:S(2)}) copy-start(bf16[4,384,384]{2,1,0:T(8,128)(2,1)S(1)} %get-tuple-element.16.own_m) | copy-start | bytes 3538948
  18.3 0.7 copy-start.2
  19.0 18.4 %collective-permute-start = (bf16[768,512]{1,0:T(8,128)(2,1)}, bf16[768,512]{1,0:T(8,128)(2,1)}, u32[]{:S(2)}, u32[]{:S(2)}) collective-permute-start(bf16[768,512]{1,0:T(8,128)(2,1)} %get-tuple-element.18), channel_id=1, source_target_pairs={{4,8},{8,4},{12,16},{16,12},{20,24},{24,20},{28,32},{32,28},{36,40... | collective-permute-start | bytes 2359304 | tf_op jit(solution)/shard_map/ppermute | solution.py:49
  26.1 1.3 %copy-start.5 = (bf16[4,384,384]{2,1,0:T(8,128)(2,1)S(1)}, bf16[4,384,384]{2,1,0:T(8,128)(2,1)}, u32[]{:S(2)}) copy-start(bf16[4,384,384]{2,1,0:T(8,128)(2,1)} %copy-done.4) | copy-start | bytes 3538948
  27.4 1.0 %copy-start.7 = (bf16[4,384,128]{2,1,0:T(8,128)(2,1)S(1)}, bf16[4,384,128]{2,1,0:T(8,128)(2,1)}, u32[]{:S(2)}) copy-start(bf16[4,384,128]{2,1,0:T(8,128)(2,1)} %copy-done.6) | copy-start | bytes 1179652
  28.4 6.3 %copy-start.1 = (bf16[4,384,384]{2,1,0:T(8,128)(2,1)S(1)}, bf16[4,384,384]{2,1,0:T(8,128)(2,1)}, u32[]{:S(2)}) copy-start(bf16[4,384,384]{2,1,0:T(8,128)(2,1)} %copy-done) | copy-start | bytes 3538948
  28.4 6.3 %copy-start.3 = (bf16[4,384,128]{2,1,0:T(8,128)(2,1)S(1)}, bf16[4,384,128]{2,1,0:T(8,128)(2,1)}, u32[]{:S(2)}) copy-start(bf16[4,384,128]{2,1,0:T(8,128)(2,1)} %copy-done.2) | copy-start | bytes 1179652
  34.5 8.2 %collective-permute-start.4 = (f32[1544,128]{1,0:T(8,128)S(1)}, f32[1544,128]{1,0:T(8,128)S(1)}, u32[]{:S(2)}, u32[]{:S(2)}) collective-permute-start(f32[1544,128]{1,0:T(8,128)S(1)} %get-tuple-element.25), channel_id=1, source_target_pairs={{0,4},{4,0},{8,12},{12,8},{16,20},{20,16},{24,28},{28,24},{32,36},... | collective-permute-start | bytes 2371592 | tf_op jit(solution)/shard_map/ppermute | solution.py:49
  40.6 19.7 %collective-permute-start.3 = (f32[1536,128]{1,0:T(8,128)S(1)}, f32[1536,128]{1,0:T(8,128)}, u32[]{:S(2)}, u32[]{:S(2)}) collective-permute-start(f32[1536,128]{1,0:T(8,128)S(1)} %get-tuple-element.24), channel_id=1, source_target_pairs={{4,8},{8,4},{12,16},{16,12},{20,24},{24,20},{28,32},{32,28},{36,40... | collective-permute-start | bytes 2359304 | tf_op jit(solution)/shard_map/ppermute | solution.py:49
  44.2 33.1 %all-to-all-start = ((s32[256,1,384]{2,1,0:T(1,128)}), s32[256,1,384]{2,1,0:T(1,128)S(1)}, u32[]{:S(2)}, u32[]{:S(2)}) async-start(s32[256,1,384]{2,1,0:T(1,128)} %shard_map.100), calls=%async_computation | async-start | bytes 786432 | tf_op jit(solution)/shard_map/all_to_all | solution.py:356

commit v3 on v2

v3 whole, which is shorter than its diff:
```python
import functools
import math

import jax
import jax.numpy as jnp
from jax import lax
from jax.experimental import pallas as pl
from jax.experimental.pallas import tpu as pltpu
from jax.sharding import PartitionSpec as P

F = 384
COLS = 128
WIDE = F + COLS
FC = 8
HALF = FC // 2
EARLY = 2
ITERS = 4
CO_DEV = 8
NOTE = 16
BOTH = ("sub", "grp")
BF, F32, I32, I16 = jnp.bfloat16, jnp.float32, jnp.int32, jnp.int16

ANY = pl.BlockSpec(memory_space=pl.ANY)
VM = pl.BlockSpec(memory_space=pltpu.VMEM)
SM = pl.BlockSpec(memory_space=pltpu.SMEM)
PARAMS = pltpu.CompilerParams(vmem_limit_bytes=10 * 1024 * 1024)


def vmem(shape, dtype):
    return pltpu.VMEM(shape, dtype)


def in_vmem(value):
    return pltpu.with_memory_space_constraint(value, pltpu.VMEM)


def in_hbm(value):
    return pltpu.with_memory_space_constraint(value, pltpu.HBM)


def swapped(value, odd):
    size = lax.axis_size("sub")
    pairs = []
    for i in range(size):
        j = ((i + 1) ^ 1) - 1 if odd else i ^ 1
        if 0 <= j < size:
            pairs.append((i, j))
    return lax.ppermute(value, "sub", pairs)


def pack_kernel(plans, *refs):
    su, sl, ru, rl = refs[:4]
    outs, (*small, note, sem) = refs[-4 - len(plans) : -4], refs[-4:]
    for i, (ref, kept_at) in enumerate(zip(refs[5:7], small)):
        pltpu.make_async_copy(ref, kept_at, sem.at[2, i]).start()
    odd = lax.rem(lax.axis_index("sub"), 2) == 1
    jobs = []
    for out, (first, count, across) in zip(outs, plans):
        for j in range(count):
            jobs.append((out, j, first + j, odd if across else jnp.logical_not(odd)))

    def copies(slot, out, j, m, r, face):
        return (
            pltpu.make_async_copy(m.at[face], out.at[pl.ds(j * F, F), pl.ds(0, F)], sem.at[0, slot]),
            pltpu.make_async_copy(r.at[face], out.at[pl.ds(j * F, F), pl.ds(F, COLS)], sem.at[1, slot]),
        )

    for slot, (out, j, face, use_up) in enumerate(jobs):

        @pl.when(use_up)
        def _():
            for c in copies(slot, out, j, su, ru, HALF + face):
                c.start()

        @pl.when(jnp.logical_not(use_up))
        def _():
            for c in copies(slot, out, j, sl, rl, face):
                c.start()

    for i, (ref, kept_at) in enumerate(zip(refs[5:7], small)):
        pltpu.make_async_copy(ref, kept_at, sem.at[2, i]).wait()
    coarse_up, coarse_low = small
    target = jnp.where(odd, coarse_up[:, HALF:], coarse_low[:, :HALF])
    note[...] = jnp.zeros_like(note)
    note[0:1, :] = jnp.broadcast_to(refs[4][0].astype(F32), (1, WIDE))
    note[1:2, :HALF] = (target // 64).astype(F32)
    note[2:3, :HALF] = (target % 64).astype(F32)
    rows = plans[0][1] * F
    outs[0][rows : rows + NOTE, :] = note[...].astype(BF)
    for slot, (out, j, face, _) in enumerate(jobs):
        for c in copies(slot, out, j, su, ru, HALF + face):
            c.wait()


def pack(plans, blocks, small, after=()):
    shapes = [vmem((count * F + (0 if i else NOTE), WIDE), BF) for i, (_, count, _) in enumerate(plans)]
    return pl.pallas_call(
        functools.partial(pack_kernel, plans),
        in_specs=[ANY] * 4 + [SM] + [ANY] * (2 + len(after)),
        out_specs=[VM] * len(shapes),
        out_shape=shapes,
        scratch_shapes=[
            vmem((1, FC), I32),
            vmem((1, FC), I32),
            vmem((NOTE, WIDE), F32),
            pltpu.SemaphoreType.DMA((3, FC)),
        ],
        compiler_params=PARAMS,
        cost_estimate=SMALL,
    )(*[in_hbm(b) for b in blocks], small[0], *[in_hbm(v[None]) for v in small[1:]], *after)


def split(value):
    high = value.astype(BF)
    return high, (value - high.astype(F32)).astype(BF)


def three(row):
    high, low = split(row)
    high, low = high.astype(F32), low.astype(F32)
    return high, low, row - high - low


def mm(a, b):
    return jnp.dot(a, b, preferred_element_type=F32)


def prepare(own_m, own_r, oth_m, oth_r):
    source = mm(own_m, own_r) + mm(oth_m, oth_r)
    own_f, oth_f = own_m.astype(F32), oth_m.astype(F32)
    sums = three(jnp.sum(own_f, axis=0, keepdims=True))
    sums += three(jnp.sum(oth_f, axis=0, keepdims=True))
    matrix = own_f + oth_f
    eye = lax.broadcasted_iota(I32, (128, 128), 0) == lax.broadcasted_iota(I32, (128, 128), 1)
    pivots, bands = [], []
    for b in range(F // 128):
        band = matrix[b * 128 : (b + 1) * 128]
        parts = [band[:, c * 128 : (c + 1) * 128] for c in range(F // 128)]
        pivots.append(jnp.sum(jnp.where(eye, parts[b], 0.0), axis=1, keepdims=True))
        parts[b] = jnp.where(eye, 0.0, parts[b])
        bands.append(jnp.concatenate(parts, 1))
    inverse = jnp.broadcast_to(1.0 / jnp.concatenate(pivots, 0), (F, COLS))
    high, low = split(jnp.concatenate(bands, 0))
    return source, inverse, high, low, sums


def sweep(x, state):
    source, inverse, high, low, _ = state
    x_h, x_l = split(x)
    wide = mm(high, jnp.concatenate([x_h, x_l], 1))
    return (source - (wide[:, :COLS] + wide[:, COLS:] + mm(low, x_h))) * inverse


def fluxes(x, own_r, oth_r, sums):
    line = lax.broadcasted_iota(I32, (16, F), 0)
    left = jnp.zeros((16, F), F32)
    for i, row in enumerate(sums):
        left = jnp.where(line == i, row, left)
    x_h, x_l = split(x)
    prod = mm(left.astype(BF), jnp.concatenate([own_r, oth_r, x_h, x_l], 1))[:8]
    moved = prod[:, 2 * COLS : 3 * COLS] + prod[:, 3 * COLS :]
    line = lax.broadcasted_iota(I32, (8, COLS), 0)
    scale = 1.0 / math.sqrt(F)
    own = jnp.where(line < 3, prod[:, :COLS] - moved, 0.0)
    oth = jnp.where((line >= 3) & (line < 6), prod[:, COLS : 2 * COLS] - moved, 0.0)
    return (
        jnp.sum(own, axis=0, keepdims=True) * scale,
        jnp.sum(oth, axis=0, keepdims=True) * scale,
    )


def solve_pair(own, others):
    states = [prepare(m, r, o[:, :F], o[:, F:]) for (m, r), o in zip(own, others)]
    xs = [s[0] * s[1] for s in states]
    for _ in range(ITERS):
        xs = [sweep(x, s) for x, s in zip(xs, states)]
    return [
        (x, *fluxes(x, r, o[:, F:], s[4])) for x, s, (_, r), o in zip(xs, states, own, others)
    ]


def keeper(su, sl, ru, rl, use_up, first, count, m, r, sem, row):
    def copies(i, sm, sr, face):
        return (
            pltpu.make_async_copy(sm.at[face], m.at[i], sem.at[row, i]),
            pltpu.make_async_copy(sr.at[face], r.at[i], sem.at[row + 1, i]),
        )

    def start(i):
        @pl.when(use_up)
        def _():
            for c in copies(i, su, ru, first + i):
                c.start()

        @pl.when(jnp.logical_not(use_up))
        def _():
            for c in copies(i, sl, rl, HALF + first + i):
                c.start()

    def wait(i):
        for c in copies(i, su, ru, first + i):
            c.wait()

    return start, wait


def count_of(lower, info, note):
    return jnp.where(lower, info[2].astype(F32), note.astype(F32)[:1])


def near_kernel(
    info, table, su, sl, ru, rl, got_1, got_2, x_out, flux_out, theirs_out, next_m, next_r, m, r, other, note, sem
):
    use_up = info[1] == 1
    own_start, own_wait = keeper(su, sl, ru, rl, use_up, 0, HALF, m, r, sem, 0)
    next_start, next_wait = keeper(
        su, sl, ru, rl, jnp.logical_not(use_up), 0, HALF, next_m, next_r, sem, 3
    )

    def got_copy(i):
        part, j = (got_1, i) if i < EARLY else (got_2, i - EARLY)
        return pltpu.make_async_copy(part.at[pl.ds(j * F, F)], other.at[i], sem.at[2, i])

    note_copy = pltpu.make_async_copy(got_1.at[pl.ds(EARLY * F, NOTE)], note, sem.at[2, HALF])
    for i in range(HALF):
        own_start(i)
        got_copy(i).start()
        if i == 0:
            note_copy.start()
    for i in range(HALF):
        next_start(i)
    flux_out[...] = jnp.zeros_like(flux_out)
    theirs_out[...] = jnp.zeros_like(theirs_out)
    base = jnp.where(use_up, 0, HALF)
    for start in range(0, HALF, 2):
        faces = (start, start + 1)
        for i in faces:
            own_wait(i)
            got_copy(i).wait()
        if start == 0:
            note_copy.wait()
            count = count_of(use_up, info, note[:, :COLS])
        solved = solve_pair([(m[i], r[i]) for i in faces], [other[i] for i in faces])
        for i, (x, mine, theirs) in zip(faces, solved):
            live = (base + i).astype(F32) < count
            x_out[i * F : (i + 1) * F, :] = jnp.where(live, x, 0.0)
            flux_out[i : i + 1, :] = jnp.where(live, mine, 0.0)
            theirs_out[i : i + 1, :] = jnp.where(live, theirs, 0.0)
    for i in range(HALF):
        next_wait(i)


def steps_of(top):
    step = jnp.maximum(top, 1e-28) * (1.0 / 32767.0)
    power = jnp.clip(jnp.floor(jnp.log(step) * (1.0 / math.log(2.0))), -120.0, 120.0)
    unit = jnp.exp2(power)
    digits = jnp.round(step / unit * float(2**21))
    return digits, power, digits * unit * (2.0**-21)


def coded(value, step):
    return jnp.clip(jnp.round(value / step), -32767.0, 32767.0).astype(I32)


def far_kernel(info, m, r, got, x_out, code_out, flux_out):
    use_up = info[0] == 1
    count = count_of(use_up, info, got[HALF * F : HALF * F + NOTE, :COLS])
    base = jnp.where(use_up, 0, HALF)
    line = lax.broadcasted_iota(I32, (NOTE, COLS), 0)
    tail = jnp.zeros((NOTE, COLS), I32)
    for start in range(0, HALF, 2):
        faces = (start, start + 1)
        solved = solve_pair(
            [(m[i], r[i]) for i in faces], [got[i * F : (i + 1) * F, :] for i in faces]
        )
        for i, (x, mine, theirs) in zip(faces, solved):
            live = (base + i).astype(F32) < count
            x = jnp.where(live, x, 0.0)
            x_out[i * F : (i + 1) * F, :] = x
            digits, power, step = steps_of(jnp.max(jnp.abs(x), axis=0, keepdims=True))
            code_out[i * F : (i + 1) * F, :] = coded(x, step).astype(I16)
            digits = digits.astype(I32)
            for j, row in enumerate((digits >> 11, digits & 2047, power.astype(I32))):
                tail = jnp.where(line == 3 * i + j, row, tail)
            flux_out[i : i + 1, :] = jnp.where(live, mine, 0.0)
            flux_out[HALF + i : HALF + i + 1, :] = jnp.where(live, theirs, 0.0)
    code_out[HALF * F :, :] = tail.astype(I16)


def kept(count):
    return [vmem((count, F, F), BF), vmem((count, F, COLS), BF)]


LARGE = pl.CostEstimate(flops=10**11, bytes_accessed=10**8, transcendentals=0)
SMALL = pl.CostEstimate(flops=1000, bytes_accessed=1000, transcendentals=0)


def solve_near(info, table, blocks, got_1, got_2):
    return pl.pallas_call(
        near_kernel,
        in_specs=[SM] * 2 + [ANY] * 6,
        out_specs=[VM] * 5,
        out_shape=[vmem((HALF * F, COLS), F32)] + [vmem((FC, COLS), F32)] * 2 + kept(HALF),
        scratch_shapes=[
            *kept(HALF),
            vmem((HALF, F, WIDE), BF),
            vmem((NOTE, WIDE), BF),
            pltpu.SemaphoreType.DMA((5, HALF + 1)),
        ],
        compiler_params=PARAMS,
        cost_estimate=SMALL,
    )(info, table, *[in_hbm(b) for b in blocks], in_hbm(got_1), in_hbm(got_2))


def solve_far(info, m, r, got):
    return pl.pallas_call(
        far_kernel,
        in_specs=[SM] + [VM] * 3,
        out_specs=[VM] * 3,
        out_shape=[
            vmem((HALF * F, COLS), F32),
            vmem((HALF * F + NOTE, COLS), I16),
            vmem((FC, COLS), F32),
        ],
        compiler_params=PARAMS,
        cost_estimate=SMALL,
    )(info, *map(in_vmem, (m, r, got)))


def place(ref, first, panels, sem, slot):
    out = []
    for i in range(HALF):
        c = pltpu.make_async_copy(panels.at[pl.ds(i * F, F)], ref.at[first + i], sem.at[slot, i])
        c.start()
        out.append(c)
    return out


def gather_kernel(x_e, back_e, x_o, up, low, sem):
    odd = lax.rem(lax.axis_index("sub"), 2) == 1

    @pl.when(odd)
    def _():
        copies = place(low, HALF, x_e, sem, 0) + place(low, 0, back_e, sem, 1)
        copies += place(up, 0, x_o, sem, 2)
        for c in copies:
            c.wait()

    @pl.when(jnp.logical_not(odd))
    def _():
        copies = place(up, 0, x_e, sem, 0) + place(up, HALF, back_e, sem, 1)
        copies += place(low, HALF, x_o, sem, 2)
        for c in copies:
            c.wait()


def gather(x_e, back_e, x_o):
    shape = pltpu.HBM((FC, F, COLS), F32)
    return pl.pallas_call(
        gather_kernel,
        in_specs=[VM] * 3,
        out_specs=[ANY] * 2,
        out_shape=[shape, shape],
        scratch_shapes=[pltpu.SemaphoreType.DMA((3, HALF))],
        compiler_params=PARAMS,
        cost_estimate=LARGE,
    )(x_e, back_e, x_o)


SLOTS = 4


def encode_kernel(table, flux_e, back_e, flux_o, got, out, codes, heads):
    rows = jnp.concatenate(
        [flux_e[:HALF], back_e[:HALF], flux_o[...]], 0
    )
    top = jnp.max(jnp.abs(rows), axis=1, keepdims=True)
    digits, power, step = steps_of(jnp.broadcast_to(top, rows.shape))
    codes[...] = coded(rows, step)
    heads[...] = digits.astype(I32) * 256 + (power.astype(I32) + 128)
    out[...] = jnp.zeros_like(out)
    lane = lax.broadcasted_iota(I32, (1, COLS), 1)
    none = jnp.zeros((1, COLS), I32)

    def place_row(i, owner, rank, local, far, valid):
        code = codes[i : i + 1, :]
        code = jnp.where(rank == 0, code * 65536, code & 65535)
        code = jnp.where(valid, code, 0)
        slot = rank + (2 if far else 0)
        head = jnp.where((lane == slot * CO_DEV + local) & valid, heads[i : i + 1, :], 0)
        out[owner] = out[owner] | jnp.concatenate(
            [none, code, head] if far else [code, none, head], 1
        )

    for i in range(3 * HALF):
        place_row(i, table[0, i], table[1, i], table[2, i], False, True)
    note = got[HALF * F : HALF * F + NOTE, :COLS].astype(F32)
    told = note[1:2] * 64.0 + note[2:3]
    owners = []
    for i in range(HALF):
        target = jnp.max(jnp.where(lane == i, told, 0.0)).astype(I32)
        owner = lax.div(target, CO_DEV)
        rank = 0
        for other in owners:
            rank = rank + jnp.where(other == owner, 1, 0)
        owners.append(owner)
        rank = jnp.minimum(rank, 1)
        place_row(3 * HALF + i, owner, rank, target - owner * CO_DEV, True, table[3, 0] == 1)


def encode(table, flux_e, back_e, flux_o, got, devices):
    return pl.pallas_call(
        encode_kernel,
        in_specs=[SM] + [VM] * 4,
        out_specs=VM,
        out_shape=vmem((devices, 1, 3 * COLS), I32),
        scratch_shapes=[vmem((4 * HALF, COLS), I32), vmem((4 * HALF, COLS), I32)],
        compiler_params=PARAMS,
        cost_estimate=SMALL,
    )(table, *map(in_vmem, (flux_e, back_e, flux_o, got)))


def decode(got):
    n = got.shape[0] // 3
    words = [got[pl.ds(c, n, stride=3), :] for c in range(3)]
    head = words[2]
    power = (head & 255).astype(F32) - 128.0
    step = jnp.where(head == 0, 0.0, (head >> 8).astype(F32) * (2.0**-21) * jnp.exp2(power))
    used = SLOTS * CO_DEV
    left = jnp.concatenate(three(step.T[:used]), 0).astype(BF)
    parts = []
    for w in words[:2]:
        for q in (w >> 16, (w << 16) >> 16):
            high = q >> 8
            parts.append((high.astype(F32) * 256.0).astype(BF))
            parts.append((q - high * 256).astype(F32).astype(BF))
    prods = mm(left, jnp.concatenate(parts, 1))
    prods = prods[:used] + prods[used : 2 * used] + prods[2 * used :]
    total = jnp.zeros((CO_DEV, COLS), F32)
    for r in range(SLOTS):
        rows = prods[r * CO_DEV : (r + 1) * CO_DEV]
        total = total + rows[:, 2 * r * COLS : (2 * r + 1) * COLS]
        total = total + rows[:, (2 * r + 1) * COLS : (2 * r + 2) * COLS]
    return total


def finish_kernel(arrived, back_o, up_in, low_in, up, low, coarse, panels, sem):
    odd = lax.rem(lax.axis_index("sub"), 2) == 1
    tail = back_o[HALF * F :, :].astype(I32)
    for i in range(HALF):
        high, rest, power = (tail[3 * i + j : 3 * i + j + 1] for j in range(3))
        step = (high * 2048 + rest).astype(F32) * jnp.exp2(power.astype(F32)) * (2.0**-21)
        panels[i] = back_o[i * F : (i + 1) * F, :].astype(I32).astype(F32) * step

        @pl.when(odd)
        def _():
            pltpu.make_async_copy(panels.at[i], up.at[HALF + i], sem.at[i]).start()

        @pl.when(jnp.logical_not(odd))
        def _():
            pltpu.make_async_copy(panels.at[i], low.at[i], sem.at[i]).start()

    coarse[...] = decode(arrived)
    for i in range(HALF):
        pltpu.make_async_copy(panels.at[i], up.at[HALF + i], sem.at[i]).wait()


def finish(arrived, back_o, up, low):
    shape = pltpu.HBM((FC, F, COLS), F32)
    return pl.pallas_call(
        finish_kernel,
        in_specs=[VM] * 2 + [ANY] * 2,
        out_specs=[ANY] * 2 + [VM],
        out_shape=[shape, shape, jax.ShapeDtypeStruct((CO_DEV, COLS), F32)],
        input_output_aliases={2: 0, 3: 1},
        scratch_shapes=[vmem((HALF, F, COLS), F32), pltpu.SemaphoreType.DMA((HALF,))],
        compiler_params=PARAMS,
    )(in_vmem(arrived), in_vmem(back_o), in_hbm(up), in_hbm(low))


def shards(schur_up, schur_low, resid_up, resid_low, counts, coarse_up, coarse_low):
    subs = lax.axis_size("sub")
    devices = lax.axis_size(BOTH)
    s = lax.axis_index("sub")
    odd = (s % 2).astype(I32)
    even = 1 - odd
    blocks = (schur_up, schur_low, resid_up, resid_low)

    def pick(if_odd, if_even):
        return jnp.where(odd == 1, if_odd, if_even)

    small = (counts, coarse_up, coarse_low)
    (pack_o,) = pack([(0, HALF, True)], blocks, small)
    got_o = swapped(pack_o, True)
    pack_1, pack_2 = pack(
        [(0, EARLY, False), (EARLY, HALF - EARLY, False)], blocks, small, (pack_o,)
    )
    got_1 = swapped(pack_1, False)
    got_2 = swapped(pack_2, False)

    count = jnp.where(s < subs - 1, counts[0], 0)
    info = jnp.stack([odd, even, count])
    targets = jnp.concatenate(
        [
            pick(coarse_low[HALF:], coarse_up[:HALF]),
            pick(coarse_low[:HALF], coarse_up[HALF:]),
            pick(coarse_up[:HALF], coarse_low[HALF:]),
        ]
    )
    order = jnp.arange(3 * HALF, dtype=I32)
    owner, local = targets // CO_DEV, targets % CO_DEV
    same = (owner[:, None] == owner[None, :]) & (order[None, :] < order[:, None])
    rank = jnp.minimum(jnp.sum(same, axis=1), 1).astype(I32)
    paired = jnp.broadcast_to(((s > 0) & (s < subs - 1)).astype(I32), owner.shape)
    table = jnp.stack([owner, rank, local, paired])

    x_e, flux_e, theirs_e, own_m, own_r = solve_near(info, table, blocks, got_1, got_2)
    back_e = swapped(x_e, False)
    back_flux = swapped(theirs_e, False)
    x_o, code_o, flux_o = solve_far(info, own_m, own_r, got_o)
    back_o = swapped(code_o, True)

    parcels = encode(table, flux_e, back_flux, flux_o, got_o, devices)
    arrived = lax.all_to_all(parcels, BOTH, 0, 0, tiled=True)
    up, low = gather(x_e, back_e, x_o)
    return finish(arrived.reshape(devices * 3, COLS), back_o, up, low)


def solution(mesh):
    return jax.shard_map(
        shards,
        mesh=mesh,
        in_specs=(
            P(BOTH, None, None),
            P(BOTH, None, None),
            P(BOTH, None, None),
            P(BOTH, None, None),
            P(BOTH),
            P(BOTH),
            P(BOTH),
        ),
        out_specs=(
            P(BOTH, None, None),
            P(BOTH, None, None),
            P(BOTH, None),
        ),
        check_vma=False,
    )
```

time: 81.6 us -> 67.9 us (0.83)
  local copies, waits for them, and re-layouts: 5.88 us -> 0.09 us
  other arithmetic: 5.48 us -> 0.58 us
  Pallas kernels: 24.7 us -> 22.5 us
  starting transfers between devices: 26.8 us -> 25.4 us
  waiting for transfers between devices: 16.8 us -> 17.7 us
    ppermute x5 -> x6, waiting for transfers between devices: 2.9 us -> 11.9 us  [swapped(): return lax.ppermute(value, 'sub', pairs)]
    all_to_all x1, waiting for transfers between devices: 13.9 us -> 5.81 us  [shards(): arrived = lax.all_to_all(parcels, BOTH, 0, 0, tiled=True)]
    unnamed x16 -> x4, local copies, waits for them, and re-layouts: 5.8 us -> 0.01 us
    pallas_call x7 -> x6, Pallas kernels: 23.2 us -> 21 us  [the longest x1 7.31 us: solve_near(): pl.pallas_call(near_kernel, in_specs=[SM] * 2 + [ANY] * 6, out_specs=[VM]...]
    concatenate x1 -> x0, other arithmetic: 1.91 us -> none  [shards(): average_up = jnp.concatenate([pick(x_o, x_e), pick(back_o, back_e)], 0)]
    ppermute x5 -> x6, starting transfers between devices: 10.9 us -> 9.32 us  [swapped(): return lax.ppermute(value, 'sub', pairs)]
    select_n x2 -> x0, other arithmetic: 1.57 us -> none  [the longest x1 0.82 us: shards(): sent % 64]
    select_n x2 -> x1, other arithmetic: 1.35 us -> 0.07 us  [pick(): return jnp.where(odd == 1, if_odd, if_even)]
  transfers between devices with their start and end apart: 6 -> 7, of which waited for: 2 -> 5; matrix products, arithmetic and copies ran while one was open for 5% -> 1% of each run, Pallas kernels for 21% -> 28%
where the time goes in v3:
time: 67.9 us; the launch traced here: 67.6 us
  starting transfers between devices  25.4 us (37%)
  Pallas kernels  22.5 us (33%)
  waiting for transfers between devices  17.7 us (26%)
  between operations  1.39 us (2%)
    all_to_all x1, starting transfers between devices, shards(): arrived = lax.all_to_all(parcels, BOTH, 0, 0, tiled=True)  16.1 us
    ppermute x6, waiting for transfers between devices, swapped(): return lax.ppermute(value, 'sub', pairs)  11.9 us
    ppermute x6, starting transfers between devices, swapped(): return lax.ppermute(value, 'sub', pairs)  9.32 us
    pallas_call x1, Pallas kernels, solve_near(): pl.pallas_call(near_kernel, in_specs=[SM] * 2 + [ANY] * 6, out_specs=[VM]...  7.31 us
    all_to_all x1, waiting for transfers between devices, shards(): arrived = lax.all_to_all(parcels, BOTH, 0, 0, tiled=True)  5.81 us
    pallas_call x1, Pallas kernels, solve_far(): pl.pallas_call(far_kernel, in_specs=[SM] + [VM] * 3, out_specs=[VM] * 3,...  4.7 us
    pallas_call x2, Pallas kernels, pack(): pl.pallas_call(functools.partial(pack_kernel, plans), in_specs=[ANY] * 4...  4.35 us
    pallas_call x1, Pallas kernels, gather(): pl.pallas_call(gather_kernel, in_specs=[VM] * 3, out_specs=[ANY] * 2, out...  2.86 us
  transfers between devices with their start and end apart: 7, of which 5 were waited for; matrix products, arithmetic and copies ran while one was open for 1% of the time, Pallas kernels for 28%

profile of v3, /device:TPU:1, one launch (start us, length us, event | category | flops | bytes accessed | tf_op | source)
XLA Modules:
  0.0 67.6 jit_solution(12147873204458149661)
XLA Ops:
  1.3 1.6 %shard_map.94.refs_7_ = bf16[1552,512]{1,0:T(8,128)(2,1)S(1)} custom-call(bf16[8,384,384]{2,1,0:T(8,128)(2,1)} %su.1, bf16[8,384,384]{2,1,0:T(8,128)(2,1)} %sl.1, bf16[8,384,128]{2,1,0:T(8,128)(2,1)} %ru.1, bf16[8,384,128]{2,1,0:T(8,128)(2,1)} %rl.1, s32[1]{0:T(128)} %copy.14.refs_4_, s32[1,8]{1,0:T(1,128)} %bitcast.15, s32[1,8]{1,0:T(1,128)} %bitcast.17), custom_call_target="tpu_custom_call" | custom-call | flops 1000 | bytes 1000 | tf_op jit(solution)/shard_map/pallas_call | solution.py:97
  2.9 4.6 %collective-permute-start.3 = (bf16[1552,512]{1,0:T(8,128)(2,1)S(1)}, bf16[1552,512]{1,0:T(8,128)(2,1)S(1)}, u32[]{:S(2)}, u32[]{:S(2)}) collective-permute-start(bf16[1552,512]{1,0:T(8,128)(2,1)S(1)} %shard_map.94.refs_7_), channel_id=1, source_target_pairs={{4,8},{8,4},{12,16},{16,12},{20,24},{24,20},{28,32},{32,28},{36,40... | collective-permute-start | bytes 4767752 | tf_op jit(solution)/shard_map/ppermute | solution.py:48
  7.5 2.7 %shard_map.95 = (bf16[784,512]{1,0:T(8,128)(2,1)}, bf16[768,512]{1,0:T(8,128)(2,1)}) custom-call(bf16[8,384,384]{2,1,0:T(8,128)(2,1)} %su.1, bf16[8,384,384]{2,1,0:T(8,128)(2,1)} %sl.1, bf16[8,384,128]{2,1,0:T(8,128)(2,1)} %ru.1, bf16[8,384,128]{2,1,0:T(8,128)(2,1)} %rl.1, s32[1]{0:T(128)} %copy.14.refs_4_, s32[1,8]{1,0:T(1,128)} %bitcast.16, ...), custom_call_target="tpu_custom_call" | custom-call | flops 1000 | bytes 1000 | tf_op jit(solution)/shard_map/pallas_call | solution.py:97
  10.3 0.1 collective-permute-start.1
  10.4 0.5 collective-permute-start
  10.9 0.1 and_select_fusion.1
  11.0 0.1 and_select_fusion.2
  11.1 0.1 pad_add_fusion.2.info
  11.2 0.1 pad.6.clone
  11.3 0.2 convert_reduce_fusion
  11.5 1.4 %collective-permute-done.1.got_2 = bf16[768,512]{1,0:T(8,128)(2,1)} collective-permute-done((bf16[768,512]{1,0:T(8,128)(2,1)}, bf16[768,512]{1,0:T(8,128)(2,1)}, u32[]{:S(2)}, u32[]{:S(2)}) %collective-permute-start.1) | collective-permute-done | bytes 786464 | tf_op jit(solution)/shard_map/ppermute | solution.py:48
  13.0 1.1 %collective-permute-done.got_1 = bf16[784,512]{1,0:T(8,128)(2,1)} collective-permute-done((bf16[784,512]{1,0:T(8,128)(2,1)}, bf16[784,512]{1,0:T(8,128)(2,1)}, u32[]{:S(2)}, u32[]{:S(2)}) %collective-permute-start) | collective-permute-done | bytes 802848 | tf_op jit(solution)/shard_map/ppermute | solution.py:48
  14.1 7.3 %shard_map.96 = (f32[1536,128]{1,0:T(8,128)}, f32[8,128]{1,0:T(8,128)S(1)}, f32[8,128]{1,0:T(8,128)S(1)}, bf16[4,384,384]{2,1,0:T(8,128)(2,1)S(1)}, bf16[4,384,128]{2,1,0:T(8,128)(2,1)S(1)}) custom-call(s32[3]{0:T(128)S(1)} %pad_add_fusion.2.info, s32[4,12]{1,0:T(4,128)S(1)} %add_add_fusion.table, bf16[8,384,384]{2,1,0:T(8,128)(2,1)} %su.1, ...), custom_call_target="tpu_custom_call" | custom-call | flops 1000 | bytes 1000 | tf_op jit(solution)/shard_map/pallas_call | solution.py:299
  21.5 0.2 collective-permute-start.5
  21.7 0.4 collective-permute-start.2
  22.1 3.7 %collective-permute-done.3.got = bf16[1552,512]{1,0:T(8,128)(2,1)S(1)} collective-permute-done((bf16[1552,512]{1,0:T(8,128)(2,1)S(1)}, bf16[1552,512]{1,0:T(8,128)(2,1)S(1)}, u32[]{:S(2)}, u32[]{:S(2)}) %collective-permute-start.3) | collective-permute-done | bytes 1589280 | tf_op jit(solution)/shard_map/ppermute | solution.py:48
  25.8 4.7 %shard_map.97 = (f32[1536,128]{1,0:T(8,128)S(1)}, s16[1552,128]{1,0:T(8,128)(2,1)S(1)}, f32[8,128]{1,0:T(8,128)S(1)}) custom-call(s32[3]{0:T(128)S(1)} %pad_add_fusion.2.info, bf16[4,384,384]{2,1,0:T(8,128)(2,1)S(1)} %get-tuple-element.19.m, bf16[4,384,128]{2,1,0:T(8,128)(2,1)S(1)} %get-tuple-element.20.r, bf16[1552,512]{1,0:T(8,128)(2,1)S(1)} %collective-permute-done.3.got), custom_call_target="tpu_custom_call" | custom-call | flops 1000 | bytes 1000 | tf_op jit(solution)/shard_map/pallas_call | solution.py:316
  30.5 1.5 %shard_map.98 = s32[256,1,384]{2,1,0:T(1,128)} custom-call(s32[4,12]{1,0:T(4,128)S(1)} %add_add_fusion.table, f32[8,128]{1,0:T(8,128)S(1)} %get-tuple-element.17.flux_e, f32[8,128]{1,0:T(8,128)S(1)} %collective-permute-done.2.back_e, f32[8,128]{1,0:T(8,128)S(1)} %get-tuple-element.21.flux_o, bf16[1552,512]{1,0:T(8,128)(2,1)S(1)} %collective-permute-done.3.got), custom_call_target="tpu_custom_call" | custom-call | flops 1000 | bytes 1000 | tf_op jit(solution)/shard_map/pallas_call | solution.py:412
  32.0 16.1 %all-to-all-start = ((s32[256,1,384]{2,1,0:T(1,128)}), s32[256,1,384]{2,1,0:T(1,128)S(1)}, u32[]{:S(2)}, u32[]{:S(2)}) async-start(s32[256,1,384]{2,1,0:T(1,128)} %shard_map.98), calls=%async_computation | async-start | bytes 786432 | tf_op jit(solution)/shard_map/all_to_all | solution.py:524
  48.1 3.5 %collective-permute-start.4 = (s16[1552,128]{1,0:T(8,128)(2,1)S(1)}, s16[1552,128]{1,0:T(8,128)(2,1)S(1)}, u32[]{:S(2)}, u32[]{:S(2)}) collective-permute-start(s16[1552,128]{1,0:T(8,128)(2,1)S(1)} %get-tuple-element.22), channel_id=1, source_target_pairs={{4,8},{8,4},{12,16},{16,12},{20,24},{24,20},{28,32},{32,28},{36,40... | collective-permute-start | bytes 1191944 | tf_op jit(solution)/shard_map/ppermute | solution.py:48
  51.6 2.9 %shard_map.99 = (f32[8,384,128]{2,1,0:T(8,128)}, f32[8,384,128]{2,1,0:T(8,128)}) custom-call(f32[1536,128]{1,0:T(8,128)} %get-tuple-element.23.x_e, f32[1536,128]{1,0:T(8,128)} %collective-permute-done.5.back_e, f32[1536,128]{1,0:T(8,128)S(1)} %get-tuple-element.24.x_o), custom_call_target="tpu_custom_call" | custom-call | flops 99999997952 | bytes 100000000 | tf_op jit(solution)/shard_map/pallas_call | solution.py:359
  54.5 5.5 %collective-permute-done.4.back_o = s16[1552,128]{1,0:T(8,128)(2,1)S(1)} collective-permute-done((s16[1552,128]{1,0:T(8,128)(2,1)S(1)}, s16[1552,128]{1,0:T(8,128)(2,1)S(1)}, u32[]{:S(2)}, u32[]{:S(2)}) %collective-permute-start.4) | collective-permute-done | bytes 397344 | tf_op jit(solution)/shard_map/ppermute | solution.py:48
  60.0 5.8 %all-to-all-done = s32[256,1,384]{2,1,0:T(1,128)S(1)} async-done(((s32[256,1,384]{2,1,0:T(1,128)}), s32[256,1,384]{2,1,0:T(1,128)S(1)}, u32[]{:S(2)}, u32[]{:S(2)}) %all-to-all-start) | async-done | bytes 393248 | tf_op jit(solution)/shard_map/all_to_all | solution.py:524
  65.9 1.8 %shard_map.100 = (f32[8,384,128]{2,1,0:T(8,128)}, f32[8,384,128]{2,1,0:T(8,128)}, f32[8,128]{1,0:T(8,128)}) custom-call(s32[768,128]{1,0:T(8,128)S(1)} %bitcast.14, s16[1552,128]{1,0:T(8,128)(2,1)S(1)} %collective-permute-done.4.back_o, f32[8,384,128]{2,1,0:T(8,128)} %get-tuple-element.25.up_in, ...), custom_call_target="tpu_custom_call", output_to_operand_aliasing={{0}: (2, {}), {1}: (3, {})} | custom-call | tf_op jit(solution)/shard_map/pallas_call | solution.py:470
  (10 shorter events, 0.2 us)
Async XLA Ops:
  2.9 8.0 %copy-start = (s32[8]{0:T(128)S(1)}, s32[8]{0:T(128)}, u32[]{:S(2)}) copy-start(s32[8]{0:T(128)} %param.12) | copy-start | bytes 100
  2.9 8.0 %copy-start.1 = (s32[8]{0:T(128)S(1)}, s32[8]{0:T(128)}, u32[]{:S(2)}) copy-start(s32[8]{0:T(128)} %param.13) | copy-start | bytes 100
  2.9 22.9 %collective-permute-start.3 = (bf16[1552,512]{1,0:T(8,128)(2,1)S(1)}, bf16[1552,512]{1,0:T(8,128)(2,1)S(1)}, u32[]{:S(2)}, u32[]{:S(2)}) collective-permute-start(bf16[1552,512]{1,0:T(8,128)(2,1)S(1)} %shard_map.94.refs_7_), channel_id=1, source_target_pairs={{4,8},{8,4},{12,16},{16,12},{20,24},{24,20},{28,32},{32,28},{36,40... | collective-permute-start | bytes 4767752 | tf_op jit(solution)/shard_map/ppermute | solution.py:48
  10.3 2.7 %collective-permute-start.1 = (bf16[768,512]{1,0:T(8,128)(2,1)}, bf16[768,512]{1,0:T(8,128)(2,1)}, u32[]{:S(2)}, u32[]{:S(2)}) collective-permute-start(bf16[768,512]{1,0:T(8,128)(2,1)} %get-tuple-element.16), channel_id=1, source_target_pairs={{0,4},{4,0},{8,12},{12,8},{16,20},{20,16},{24,28},{28,24},{32,36},... | collective-permute-start | bytes 2359304 | tf_op jit(solution)/shard_map/ppermute | solution.py:48
  10.4 3.8 %collective-permute-start = (bf16[784,512]{1,0:T(8,128)(2,1)}, bf16[784,512]{1,0:T(8,128)(2,1)}, u32[]{:S(2)}, u32[]{:S(2)}) collective-permute-start(bf16[784,512]{1,0:T(8,128)(2,1)} %get-tuple-element.15), channel_id=1, source_target_pairs={{0,4},{4,0},{8,12},{12,8},{16,20},{20,16},{24,28},{28,24},{32,36},... | collective-permute-start | bytes 2408456 | tf_op jit(solution)/shard_map/ppermute | solution.py:48
  21.5 30.2 %collective-permute-start.5 = (f32[1536,128]{1,0:T(8,128)}, f32[1536,128]{1,0:T(8,128)}, u32[]{:S(2)}, u32[]{:S(2)}) collective-permute-start(f32[1536,128]{1,0:T(8,128)} %get-tuple-element.23.x_e), channel_id=1, source_target_pairs={{0,4},{4,0},{8,12},{12,8},{16,20},{20,16},{24,28},{28,24},{32,36},... | collective-permute-start | bytes 2359304 | tf_op jit(solution)/shard_map/ppermute | solution.py:48
  21.7 8.8 %collective-permute-start.2 = (f32[8,128]{1,0:T(8,128)S(1)}, f32[8,128]{1,0:T(8,128)S(1)}, u32[]{:S(2)}, u32[]{:S(2)}) collective-permute-start(f32[8,128]{1,0:T(8,128)S(1)} %get-tuple-element.18), channel_id=1, source_target_pairs={{0,4},{4,0},{8,12},{12,8},{16,20},{20,16},{24,28},{28,24},{32,36},... | collective-permute-start | bytes 12296 | tf_op jit(solution)/shard_map/ppermute | solution.py:48
  32.0 33.9 %all-to-all-start = ((s32[256,1,384]{2,1,0:T(1,128)}), s32[256,1,384]{2,1,0:T(1,128)S(1)}, u32[]{:S(2)}, u32[]{:S(2)}) async-start(s32[256,1,384]{2,1,0:T(1,128)} %shard_map.98), calls=%async_computation | async-start | bytes 786432 | tf_op jit(solution)/shard_map/all_to_all | solution.py:524
  48.1 12.0 %collective-permute-start.4 = (s16[1552,128]{1,0:T(8,128)(2,1)S(1)}, s16[1552,128]{1,0:T(8,128)(2,1)S(1)}, u32[]{:S(2)}, u32[]{:S(2)}) collective-permute-start(s16[1552,128]{1,0:T(8,128)(2,1)S(1)} %get-tuple-element.22), channel_id=1, source_target_pairs={{4,8},{8,4},{12,16},{16,12},{20,24},{24,20},{28,32},{32,28},{36,40... | collective-permute-start | bytes 1191944 | tf_op jit(solution)/shard_map/ppermute | solution.py:48

commit v4 on v3

--- a/solution.py
+++ b/solution.py
@@ -50,12 +50,14 @@
 
 def pack_kernel(plans, *refs):
     su, sl, ru, rl = refs[:4]
+    noted = any(plan[3] for plan in plans)
     outs, (*small, note, sem) = refs[-4 - len(plans) : -4], refs[-4:]
-    for i, (ref, kept_at) in enumerate(zip(refs[5:7], small)):
-        pltpu.make_async_copy(ref, kept_at, sem.at[2, i]).start()
+    if noted:
+        for i, (ref, kept_at) in enumerate(zip(refs[5:7], small)):
+            pltpu.make_async_copy(ref, kept_at, sem.at[2, i]).start()
     odd = lax.rem(lax.axis_index("sub"), 2) == 1
     jobs = []
-    for out, (first, count, across) in zip(outs, plans):
+    for out, (first, count, across, _) in zip(outs, plans):
         for j in range(count):
             jobs.append((out, j, first + j, odd if across else jnp.logical_not(odd)))
 
@@ -77,26 +79,29 @@
             for c in copies(slot, out, j, sl, rl, face):
                 c.start()
 
-    for i, (ref, kept_at) in enumerate(zip(refs[5:7], small)):
-        pltpu.make_async_copy(ref, kept_at, sem.at[2, i]).wait()
-    coarse_up, coarse_low = small
-    target = jnp.where(odd, coarse_up[:, HALF:], coarse_low[:, :HALF])
-    note[...] = jnp.zeros_like(note)
-    note[0:1, :] = jnp.broadcast_to(refs[4][0].astype(F32), (1, WIDE))
-    note[1:2, :HALF] = (target // 64).astype(F32)
-    note[2:3, :HALF] = (target % 64).astype(F32)
-    rows = plans[0][1] * F
-    outs[0][rows : rows + NOTE, :] = note[...].astype(BF)
+    if noted:
+        for i, (ref, kept_at) in enumerate(zip(refs[5:7], small)):
+            pltpu.make_async_copy(ref, kept_at, sem.at[2, i]).wait()
+        coarse_up, coarse_low = small
+        target = jnp.where(odd, coarse_up[:, HALF:], coarse_low[:, :HALF])
+        note[...] = jnp.zeros_like(note)
+        note[0:1, :] = jnp.broadcast_to(refs[4][0].astype(F32), (1, WIDE))
+        note[1:2, :HALF] = (target // 64).astype(F32)
+        note[2:3, :HALF] = (target % 64).astype(F32)
+        for out, plan in zip(outs, plans):
+            if plan[3]:
+                out[plan[1] * F : plan[1] * F + NOTE, :] = note[...].astype(BF)
     for slot, (out, j, face, _) in enumerate(jobs):
         for c in copies(slot, out, j, su, ru, HALF + face):
             c.wait()
 
 
-def pack(plans, blocks, small, after=()):
-    shapes = [vmem((count * F + (0 if i else NOTE), WIDE), BF) for i, (_, count, _) in enumerate(plans)]
+def pack(plans, blocks, small=(), after=()):
+    shapes = [vmem((plan[1] * F + (NOTE if plan[3] else 0), WIDE), BF) for plan in plans]
+    given = [small[0], *[in_hbm(v[None]) for v in small[1:]]] if small else []
     return pl.pallas_call(
         functools.partial(pack_kernel, plans),
-        in_specs=[ANY] * 4 + [SM] + [ANY] * (2 + len(after)),
+        in_specs=[ANY] * 4 + [SM] * len(small[:1]) + [ANY] * (len(small[1:]) + len(after)),
         out_specs=[VM] * len(shapes),
         out_shape=shapes,
         scratch_shapes=[
@@ -107,7 +112,7 @@
         ],
         compiler_params=PARAMS,
         cost_estimate=SMALL,
-    )(*[in_hbm(b) for b in blocks], small[0], *[in_hbm(v[None]) for v in small[1:]], *after)
+    )(*[in_hbm(b) for b in blocks], *given, *after)
 
 
 def split(value):
@@ -218,10 +223,10 @@
     )
 
     def got_copy(i):
-        part, j = (got_1, i) if i < EARLY else (got_2, i - EARLY)
+        part, j = (got_1, i) if i < 2 else (got_2, i - 2)
         return pltpu.make_async_copy(part.at[pl.ds(j * F, F)], other.at[i], sem.at[2, i])
 
-    note_copy = pltpu.make_async_copy(got_1.at[pl.ds(EARLY * F, NOTE)], note, sem.at[2, HALF])
+    note_copy = pltpu.make_async_copy(got_1.at[pl.ds(2 * F, NOTE)], note, sem.at[2, HALF])
     for i in range(HALF):
         own_start(i)
         got_copy(i).start()
@@ -262,28 +267,60 @@
     return jnp.clip(jnp.round(value / step), -32767.0, 32767.0).astype(I32)
 
 
-def far_kernel(info, m, r, got, x_out, code_out, flux_out):
+def solve_all(first, count, m, r, got):
+    out = []
+    for start in range(0, count, 2):
+        faces = range(start, min(start + 2, count))
+        out += solve_pair(
+            [(m[first + i], r[first + i]) for i in faces],
+            [got[i * F : (i + 1) * F, :] for i in faces],
+        )
+    return out
+
+
+def put_codes(x, ref, i, tail):
+    digits, power, step = steps_of(jnp.max(jnp.abs(x), axis=0, keepdims=True))
+    ref[i * F : (i + 1) * F, :] = coded(x, step).astype(I16)
+    digits = digits.astype(I32)
+    line = lax.broadcasted_iota(I32, tail.shape, 0)
+    for j, row in enumerate((digits >> 11, digits & 2047, power.astype(I32))):
+        tail = jnp.where(line == 3 * i + j, row, tail)
+    return tail
+
+
+def far_kernel(m, r, got, x_out, code_out, tail_out, flux_out):
+    flux_out[...] = jnp.zeros_like(flux_out)
+    tail = jnp.zeros((NOTE, COLS), I32)
+    for i, (x, mine, theirs) in enumerate(solve_all(0, EARLY, m, r, got)):
+        x_out[i * F : (i + 1) * F, :] = x
+        tail = put_codes(x, code_out, i, tail)
+        flux_out[i : i + 1, :] = mine
+        flux_out[HALF + i : HALF + i + 1, :] = theirs
+    tail_out[...] = tail
+
+
+def last_kernel(info, m, r, got, x_in, code_in, tail_in, flux_in, x_out, code_out, flux_out):
+    late = HALF - EARLY
     use_up = info[0] == 1
-    count = count_of(use_up, info, got[HALF * F : HALF * F + NOTE, :COLS])
+    count = count_of(use_up, info, got[late * F : late * F + NOTE, :COLS])
     base = jnp.where(use_up, 0, HALF)
+    code_out[: EARLY * F, :] = code_in[...]
+    tail = tail_in[...]
+    solved = [
+        (x_in[k * F : (k + 1) * F, :], flux_in[k : k + 1, :], flux_in[HALF + k : HALF + k + 1, :])
+        for k in range(EARLY)
+    ]
+    solved += solve_all(EARLY, late, m, r, got)
     line = lax.broadcasted_iota(I32, (NOTE, COLS), 0)
-    tail = jnp.zeros((NOTE, COLS), I32)
-    for start in range(0, HALF, 2):
-        faces = (start, start + 1)
-        solved = solve_pair(
-            [(m[i], r[i]) for i in faces], [got[i * F : (i + 1) * F, :] for i in faces]
-        )
-        for i, (x, mine, theirs) in zip(faces, solved):
-            live = (base + i).astype(F32) < count
-            x = jnp.where(live, x, 0.0)
-            x_out[i * F : (i + 1) * F, :] = x
-            digits, power, step = steps_of(jnp.max(jnp.abs(x), axis=0, keepdims=True))
-            code_out[i * F : (i + 1) * F, :] = coded(x, step).astype(I16)
-            digits = digits.astype(I32)
-            for j, row in enumerate((digits >> 11, digits & 2047, power.astype(I32))):
-                tail = jnp.where(line == 3 * i + j, row, tail)
-            flux_out[i : i + 1, :] = jnp.where(live, mine, 0.0)
-            flux_out[HALF + i : HALF + i + 1, :] = jnp.where(live, theirs, 0.0)
+    for i, (x, mine, theirs) in enumerate(solved):
+        live = (base + i).astype(F32) < count
+        x_out[i * F : (i + 1) * F, :] = jnp.where(live, x, 0.0)
+        if i >= EARLY:
+            tail = put_codes(x, code_out, i, tail)
+        dead = jnp.logical_not(live)
+        tail = jnp.where((line >= 3 * i) & (line < 3 * i + 3) & dead, 0, tail)
+        flux_out[i : i + 1, :] = jnp.where(live, mine, 0.0)
+        flux_out[HALF + i : HALF + i + 1, :] = jnp.where(live, theirs, 0.0)
     code_out[HALF * F :, :] = tail.astype(I16)
 
 
@@ -291,7 +328,7 @@
     return [vmem((count, F, F), BF), vmem((count, F, COLS), BF)]
 
 
-LARGE = pl.CostEstimate(flops=10**11, bytes_accessed=10**8, transcendentals=0)
+LARGE = pl.CostEstimate(flops=10**9, bytes_accessed=10**7, transcendentals=0)
 SMALL = pl.CostEstimate(flops=1000, bytes_accessed=1000, transcendentals=0)
 
 
@@ -312,10 +349,26 @@
     )(info, table, *[in_hbm(b) for b in blocks], in_hbm(got_1), in_hbm(got_2))
 
 
-def solve_far(info, m, r, got):
+def solve_far(m, r, got):
     return pl.pallas_call(
         far_kernel,
-        in_specs=[SM] + [VM] * 3,
+        in_specs=[VM] * 3,
+        out_specs=[VM] * 4,
+        out_shape=[
+            vmem((EARLY * F, COLS), F32),
+            vmem((EARLY * F, COLS), I16),
+            vmem((NOTE, COLS), I32),
+            vmem((FC, COLS), F32),
+        ],
+        compiler_params=PARAMS,
+        cost_estimate=SMALL,
+    )(*map(in_vmem, (m, r, got)))
+
+
+def solve_last(info, m, r, got, *early):
+    return pl.pallas_call(
+        last_kernel,
+        in_specs=[SM] + [VM] * (3 + len(early)),
         out_specs=[VM] * 3,
         out_shape=[
             vmem((HALF * F, COLS), F32),
@@ -324,7 +377,7 @@
         ],
         compiler_params=PARAMS,
         cost_estimate=SMALL,
-    )(info, *map(in_vmem, (m, r, got)))
+    )(info, *map(in_vmem, (m, r, got, *early)))
 
 
 def place(ref, first, panels, sem, slot):
@@ -381,31 +434,29 @@
     out[...] = jnp.zeros_like(out)
     lane = lax.broadcasted_iota(I32, (1, COLS), 1)
     none = jnp.zeros((1, COLS), I32)
-
-    def place_row(i, owner, rank, local, far, valid):
-        code = codes[i : i + 1, :]
-        code = jnp.where(rank == 0, code * 65536, code & 65535)
-        code = jnp.where(valid, code, 0)
-        slot = rank + (2 if far else 0)
-        head = jnp.where((lane == slot * CO_DEV + local) & valid, heads[i : i + 1, :], 0)
-        out[owner] = out[owner] | jnp.concatenate(
-            [none, code, head] if far else [code, none, head], 1
-        )
-
-    for i in range(3 * HALF):
-        place_row(i, table[0, i], table[1, i], table[2, i], False, True)
-    note = got[HALF * F : HALF * F + NOTE, :COLS].astype(F32)
+    late = HALF - EARLY
+    note = got[late * F : late * F + NOTE, :COLS].astype(F32)
     told = note[1:2] * 64.0 + note[2:3]
-    owners = []
+    rows = [(table[0, i], table[1, i], table[2, i]) for i in range(3 * HALF)]
+    held = []
     for i in range(HALF):
         target = jnp.max(jnp.where(lane == i, told, 0.0)).astype(I32)
         owner = lax.div(target, CO_DEV)
         rank = 0
-        for other in owners:
+        for other in held:
             rank = rank + jnp.where(other == owner, 1, 0)
-        owners.append(owner)
-        rank = jnp.minimum(rank, 1)
-        place_row(3 * HALF + i, owner, rank, target - owner * CO_DEV, True, table[3, 0] == 1)
+        held.append(owner)
+        rows.append((owner, jnp.minimum(rank, 1), target - owner * CO_DEV))
+    for i, (owner, rank, local) in enumerate(rows):
+        far = i >= 3 * HALF
+        code = codes[i : i + 1, :]
+        code = jnp.where(rank == 0, code * 65536, code & 65535)
+        slot = rank + (2 if far else 0)
+        head = jnp.where(lane == slot * CO_DEV + local, heads[i : i + 1, :], 0)
+        line = jnp.concatenate([none, code, head] if far else [code, none, head], 1)
+        if far:
+            line = jnp.where(table[3, 0] == 1, line, 0)
+        out[owner] = out[owner] | line
 
 
 def encode(table, flux_e, back_e, flux_o, got, devices):
@@ -414,7 +465,7 @@
         in_specs=[SM] + [VM] * 4,
         out_specs=VM,
         out_shape=vmem((devices, 1, 3 * COLS), I32),
-        scratch_shapes=[vmem((4 * HALF, COLS), I32), vmem((4 * HALF, COLS), I32)],
+        scratch_shapes=[vmem((4 * HALF, COLS), I32)] * 2,
         compiler_params=PARAMS,
         cost_estimate=SMALL,
     )(table, *map(in_vmem, (flux_e, back_e, flux_o, got)))
@@ -444,7 +495,7 @@
     return total
 
 
-def finish_kernel(arrived, back_o, up_in, low_in, up, low, coarse, panels, sem):
+def panel_kernel(back_o, up_in, low_in, up, low, panels, sem):
     odd = lax.rem(lax.axis_index("sub"), 2) == 1
     tail = back_o[HALF * F :, :].astype(I32)
     for i in range(HALF):
@@ -460,22 +511,37 @@
         def _():
             pltpu.make_async_copy(panels.at[i], low.at[i], sem.at[i]).start()
 
-    coarse[...] = decode(arrived)
     for i in range(HALF):
         pltpu.make_async_copy(panels.at[i], up.at[HALF + i], sem.at[i]).wait()
 
 
-def finish(arrived, back_o, up, low):
+def put_panels(back_o, up, low):
     shape = pltpu.HBM((FC, F, COLS), F32)
     return pl.pallas_call(
-        finish_kernel,
-        in_specs=[VM] * 2 + [ANY] * 2,
-        out_specs=[ANY] * 2 + [VM],
-        out_shape=[shape, shape, jax.ShapeDtypeStruct((CO_DEV, COLS), F32)],
-        input_output_aliases={2: 0, 3: 1},
+        panel_kernel,
+        in_specs=[VM] + [ANY] * 2,
+        out_specs=[ANY] * 2,
+        out_shape=[shape, shape],
+        input_output_aliases={1: 0, 2: 1},
         scratch_shapes=[vmem((HALF, F, COLS), F32), pltpu.SemaphoreType.DMA((HALF,))],
         compiler_params=PARAMS,
-    )(in_vmem(arrived), in_vmem(back_o), in_hbm(up), in_hbm(low))
+        cost_estimate=SMALL,
+    )(in_vmem(back_o), in_hbm(up), in_hbm(low))
+
+
+def coarse_kernel(arrived, after, out):
+    out[...] = decode(arrived)
+
+
+def sum_rows(arrived, after):
+    return pl.pallas_call(
+        coarse_kernel,
+        in_specs=[VM, ANY],
+        out_specs=VM,
+        out_shape=jax.ShapeDtypeStruct((CO_DEV, COLS), F32),
+        compiler_params=PARAMS,
+        cost_estimate=SMALL,
+    )(in_vmem(arrived), in_hbm(after))
 
 
 def shards(schur_up, schur_low, resid_up, resid_low, counts, coarse_up, coarse_low):
@@ -489,14 +555,17 @@
     def pick(if_odd, if_even):
         return jnp.where(odd == 1, if_odd, if_even)
 
-    small = (counts, coarse_up, coarse_low)
-    (pack_o,) = pack([(0, HALF, True)], blocks, small)
-    got_o = swapped(pack_o, True)
-    pack_1, pack_2 = pack(
-        [(0, EARLY, False), (EARLY, HALF - EARLY, False)], blocks, small, (pack_o,)
+    (pack_a,) = pack([(0, EARLY, True, False)], blocks)
+    got_a = swapped(pack_a, True)
+    pack_1, pack_2, pack_b = pack(
+        [(0, 2, False, True), (2, 2, False, False), (EARLY, HALF - EARLY, True, True)],
+        blocks,
+        (counts, coarse_up, coarse_low),
+        (pack_a,),
     )
     got_1 = swapped(pack_1, False)
     got_2 = swapped(pack_2, False)
+    got_b = swapped(pack_b, True)
 
     count = jnp.where(s < subs - 1, counts[0], 0)
     info = jnp.stack([odd, even, count])
@@ -517,13 +586,15 @@
     x_e, flux_e, theirs_e, own_m, own_r = solve_near(info, table, blocks, got_1, got_2)
     back_e = swapped(x_e, False)
     back_flux = swapped(theirs_e, False)
-    x_o, code_o, flux_o = solve_far(info, own_m, own_r, got_o)
+    early = solve_far(own_m, own_r, got_a)
+    x_o, code_o, flux_o = solve_last(info, own_m, own_r, got_b, *early)
     back_o = swapped(code_o, True)
 
-    parcels = encode(table, flux_e, back_flux, flux_o, got_o, devices)
+    parcels = encode(table, flux_e, back_flux, flux_o, got_b, devices)
     arrived = lax.all_to_all(parcels, BOTH, 0, 0, tiled=True)
     up, low = gather(x_e, back_e, x_o)
-    return finish(arrived.reshape(devices * 3, COLS), back_o, up, low)
+    up, low = put_panels(back_o, up, low)
+    return (up, low, sum_rows(arrived.reshape(devices * 3, COLS), up))
 
 
 def solution(mesh):

time: 67.9 us -> 64.2 us (0.946)
  waiting for transfers between devices: 17.7 us -> 10.4 us
  starting transfers between devices: 25.4 us -> 28.5 us
    ppermute x6 -> x7, waiting for transfers between devices: 11.9 us -> 5.55 us  [swapped(): return lax.ppermute(value, 'sub', pairs)]
    ppermute x6 -> x7, starting transfers between devices: 9.32 us -> 12.5 us  [swapped(): return lax.ppermute(value, 'sub', pairs)]
    all_to_all x1, waiting for transfers between devices: 5.81 us -> 4.88 us  [shards(): arrived = lax.all_to_all(parcels, BOTH, 0, 0, tiled=True)]
    pallas_call x2 -> x4, Pallas kernels: 6.48 us -> 6.78 us  [the longest x1 2.72 us: solve_last(): pl.pallas_call(last_kernel, in_specs=[SM] + [VM] * (3 + len(early)), out_...]
  transfers between devices with their start and end apart: 7 -> 8, of which waited for: 5 -> 2; matrix products, arithmetic and copies ran while one was open for 1% -> 1% of each run, Pallas kernels for 28% -> 32%
where the time goes in v4:
time: 64.2 us; the launch traced here: 63.9 us
  starting transfers between devices  28.5 us (44%)
  Pallas kernels  22.8 us (36%)
  waiting for transfers between devices  10.4 us (16%)
  between operations  1.44 us (2%)
    all_to_all x1, starting transfers between devices, shards(): arrived = lax.all_to_all(parcels, BOTH, 0, 0, tiled=True)  16 us
    ppermute x7, starting transfers between devices, swapped(): return lax.ppermute(value, 'sub', pairs)  12.5 us
    pallas_call x1, Pallas kernels, solve_near(): pl.pallas_call(near_kernel, in_specs=[SM] * 2 + [ANY] * 6, out_specs=[VM]...  7.32 us
    ppermute x7, waiting for transfers between devices, swapped(): return lax.ppermute(value, 'sub', pairs)  5.55 us
    all_to_all x1, waiting for transfers between devices, shards(): arrived = lax.all_to_all(parcels, BOTH, 0, 0, tiled=True)  4.88 us
    pallas_call x2, Pallas kernels, pack(): pl.pallas_call(functools.partial(pack_kernel, plans), in_specs=[ANY] * 4...  4.33 us
    pallas_call x1, Pallas kernels, gather(): pl.pallas_call(gather_kernel, in_specs=[VM] * 3, out_specs=[ANY] * 2, out...  2.86 us
    pallas_call x1, Pallas kernels, solve_last(): pl.pallas_call(last_kernel, in_specs=[SM] + [VM] * (3 + len(early)), out_...  2.72 us
  transfers between devices with their start and end apart: 8, of which 2 were waited for; matrix products, arithmetic and copies ran while one was open for 1% of the time, Pallas kernels for 32%

profile of v4, /device:TPU:1, one launch (start us, length us, event | category | flops | bytes accessed | tf_op | source)
XLA Modules:
  0.0 63.9 jit_solution(9674103939628383538)
XLA Ops:
  0.6 1.3 %shard_map.94.refs_7_ = bf16[768,512]{1,0:T(8,128)(2,1)S(1)} custom-call(bf16[8,384,384]{2,1,0:T(8,128)(2,1)} %su.1, bf16[8,384,384]{2,1,0:T(8,128)(2,1)} %sl.1, bf16[8,384,128]{2,1,0:T(8,128)(2,1)} %ru.1, bf16[8,384,128]{2,1,0:T(8,128)(2,1)} %rl.1), custom_call_target="tpu_custom_call" | custom-call | flops 1000 | bytes 1000 | tf_op jit(solution)/shard_map/pallas_call | solution.py:102
  2.0 4.6 %collective-permute-start.3 = (bf16[768,512]{1,0:T(8,128)(2,1)S(1)}, bf16[768,512]{1,0:T(8,128)(2,1)S(1)}, u32[]{:S(2)}, u32[]{:S(2)}) collective-permute-start(bf16[768,512]{1,0:T(8,128)(2,1)S(1)} %shard_map.94.refs_7_), channel_id=1, source_target_pairs={{4,8},{8,4},{12,16},{16,12},{20,24},{24,20},{28,32},{32,28},{36,40... | collective-permute-start | bytes 2359304 | tf_op jit(solution)/shard_map/ppermute | solution.py:48
  7.3 3.0 %shard_map.95 = (bf16[784,512]{1,0:T(8,128)(2,1)}, bf16[768,512]{1,0:T(8,128)(2,1)}, bf16[784,512]{1,0:T(8,128)(2,1)S(1)}) custom-call(bf16[8,384,384]{2,1,0:T(8,128)(2,1)} %su.1, bf16[8,384,384]{2,1,0:T(8,128)(2,1)} %sl.1, bf16[8,384,128]{2,1,0:T(8,128)(2,1)} %ru.1, bf16[8,384,128]{2,1,0:T(8,128)(2,1)} %rl.1, s32[1]{0:T(128)} %copy.14.refs_4_, ...), custom_call_target="tpu_custom_call" | custom-call | flops 1000 | bytes 1000 | tf_op jit(solution)/shard_map/pallas_call | solution.py:102
  10.3 0.1 collective-permute-start.1
  10.4 0.5 collective-permute-start
  10.9 3.2 %collective-permute-start.2 = (bf16[784,512]{1,0:T(8,128)(2,1)S(1)}, bf16[784,512]{1,0:T(8,128)(2,1)S(1)}, u32[]{:S(2)}, u32[]{:S(2)}) collective-permute-start(bf16[784,512]{1,0:T(8,128)(2,1)S(1)} %get-tuple-element.26), channel_id=1, source_target_pairs={{4,8},{8,4},{12,16},{16,12},{20,24},{24,20},{28,32},{32,28},{36,40... | collective-permute-start | bytes 2408456 | tf_op jit(solution)/shard_map/ppermute | solution.py:48
  14.1 0.1 broadcast_select_fusion.2
  14.1 0.1 and_select_fusion.1
  14.2 0.2 convert_reduce_fusion
  14.4 0.1 and_select_fusion.2
  14.5 0.1 pad_add_fusion.info
  14.8 7.3 %shard_map.96 = (f32[1536,128]{1,0:T(8,128)}, f32[8,128]{1,0:T(8,128)S(1)}, f32[8,128]{1,0:T(8,128)S(1)}, bf16[4,384,384]{2,1,0:T(8,128)(2,1)S(1)}, bf16[4,384,128]{2,1,0:T(8,128)(2,1)S(1)}) custom-call(s32[3]{0:T(128)S(1)} %pad_add_fusion.info, s32[4,12]{1,0:T(4,128)S(1)} %add_add_fusion.table, bf16[8,384,384]{2,1,0:T(8,128)(2,1)} %su.1, ...), custom_call_target="tpu_custom_call" | custom-call | flops 1000 | bytes 1000 | tf_op jit(solution)/shard_map/pallas_call | solution.py:336
  22.1 0.1 collective-permute-start.5
  22.2 0.5 collective-permute-start.6
  22.7 2.2 %shard_map.97 = (f32[768,128]{1,0:T(8,128)S(1)}, s16[768,128]{1,0:T(8,128)(2,1)S(1)}, s32[16,128]{1,0:T(8,128)S(1)}, f32[8,128]{1,0:T(8,128)S(1)}) custom-call(bf16[4,384,384]{2,1,0:T(8,128)(2,1)S(1)} %get-tuple-element.24.m, bf16[4,384,128]{2,1,0:T(8,128)(2,1)S(1)} %get-tuple-element.25.r, bf16[768,512]{1,0:T(8,128)(2,1)S(1)} %collective-permute-done.3.got), custom_call_target="tpu_custom_call" | custom-call | flops 1000 | bytes 1000 | tf_op jit(solution)/shard_map/pallas_call | solution.py:353
  24.9 2.7 %shard_map.98 = (f32[1536,128]{1,0:T(8,128)S(1)}, s16[1552,128]{1,0:T(8,128)(2,1)S(1)}, f32[8,128]{1,0:T(8,128)S(1)}) custom-call(s32[3]{0:T(128)S(1)} %pad_add_fusion.info, bf16[4,384,384]{2,1,0:T(8,128)(2,1)S(1)} %get-tuple-element.24.m, bf16[4,384,128]{2,1,0:T(8,128)(2,1)S(1)} %get-tuple-element.25.r, bf16[784,512]{1,0:T(8,128)(2,1)S(1)} %collective-permute-done.2.got, ...), custom_call_target="tpu_custom_call" | custom-call | flops 1000 | bytes 1000 | tf_op jit(solution)/shard_map/pallas_call | solution.py:369
  27.6 1.5 %shard_map.101 = s32[256,1,384]{2,1,0:T(1,128)} custom-call(s32[4,12]{1,0:T(4,128)S(1)} %add_add_fusion.table, f32[8,128]{1,0:T(8,128)S(1)} %get-tuple-element.38.flux_e, f32[8,128]{1,0:T(8,128)S(1)} %collective-permute-done.6.back_e, f32[8,128]{1,0:T(8,128)S(1)} %get-tuple-element.40.flux_o, bf16[784,512]{1,0:T(8,128)(2,1)S(1)} %collective-permute-done.2.got), custom_call_target="tpu_custom_call" | custom-call | flops 1000 | bytes 1000 | tf_op jit(solution)/shard_map/pallas_call | solution.py:463
  29.1 16.0 %all-to-all-start = ((s32[256,1,384]{2,1,0:T(1,128)}), s32[256,1,384]{2,1,0:T(1,128)S(1)}, u32[]{:S(2)}, u32[]{:S(2)}) async-start(s32[256,1,384]{2,1,0:T(1,128)} %shard_map.101), calls=%async_computation | async-start | bytes 786432 | tf_op jit(solution)/shard_map/all_to_all | solution.py:594
  45.2 3.5 %collective-permute-start.4 = (s16[1552,128]{1,0:T(8,128)(2,1)S(1)}, s16[1552,128]{1,0:T(8,128)(2,1)S(1)}, u32[]{:S(2)}, u32[]{:S(2)}) collective-permute-start(s16[1552,128]{1,0:T(8,128)(2,1)S(1)} %get-tuple-element.31), channel_id=1, source_target_pairs={{4,8},{8,4},{12,16},{16,12},{20,24},{24,20},{28,32},{32,28},{36,40... | collective-permute-start | bytes 1191944 | tf_op jit(solution)/shard_map/ppermute | solution.py:48
  48.7 2.9 %shard_map.99 = (f32[8,384,128]{2,1,0:T(8,128)}, f32[8,384,128]{2,1,0:T(8,128)}) custom-call(f32[1536,128]{1,0:T(8,128)} %get-tuple-element.32.x_e, f32[1536,128]{1,0:T(8,128)} %collective-permute-done.5.back_e, f32[1536,128]{1,0:T(8,128)S(1)} %get-tuple-element.33.x_o), custom_call_target="tpu_custom_call" | custom-call | flops 1000000000 | bytes 10000000 | tf_op jit(solution)/shard_map/pallas_call | solution.py:412
  51.6 5.5 %collective-permute-done.4.back_o = s16[1552,128]{1,0:T(8,128)(2,1)S(1)} collective-permute-done((s16[1552,128]{1,0:T(8,128)(2,1)S(1)}, s16[1552,128]{1,0:T(8,128)(2,1)S(1)}, u32[]{:S(2)}, u32[]{:S(2)}) %collective-permute-start.4) | collective-permute-done | bytes 397344 | tf_op jit(solution)/shard_map/ppermute | solution.py:48
  57.2 0.9 %shard_map.100 = (f32[8,384,128]{2,1,0:T(8,128)}, f32[8,384,128]{2,1,0:T(8,128)}) custom-call(s16[1552,128]{1,0:T(8,128)(2,1)S(1)} %collective-permute-done.4.back_o, f32[8,384,128]{2,1,0:T(8,128)} %get-tuple-element.34.up_in, f32[8,384,128]{2,1,0:T(8,128)} %get-tuple-element.35.low_in), custom_call_target="tpu_custom_call", output_to_operand_aliasing={{0}: (1, {}), {1}: (2, {})} | custom-call | flops 1000 | bytes 1000 | tf_op jit(solution)/shard_map/pallas_call | solution.py:520
  58.1 4.9 %all-to-all-done = s32[256,1,384]{2,1,0:T(1,128)S(1)} async-done(((s32[256,1,384]{2,1,0:T(1,128)}), s32[256,1,384]{2,1,0:T(1,128)S(1)}, u32[]{:S(2)}, u32[]{:S(2)}) %all-to-all-start) | async-done | bytes 393248 | tf_op jit(solution)/shard_map/all_to_all | solution.py:594
  63.0 0.9 %shard_map.102 = f32[8,128]{1,0:T(8,128)} custom-call(s32[768,128]{1,0:T(8,128)S(1)} %bitcast.14, f32[8,384,128]{2,1,0:T(8,128)} %get-tuple-element.19.after), custom_call_target="tpu_custom_call" | custom-call | flops 1000 | bytes 1000 | tf_op jit(solution)/shard_map/pallas_call | solution.py:537
  (14 shorter events, 0.2 us)
Async XLA Ops:
  2.0 20.7 %collective-permute-start.3 = (bf16[768,512]{1,0:T(8,128)(2,1)S(1)}, bf16[768,512]{1,0:T(8,128)(2,1)S(1)}, u32[]{:S(2)}, u32[]{:S(2)}) collective-permute-start(bf16[768,512]{1,0:T(8,128)(2,1)S(1)} %shard_map.94.refs_7_), channel_id=1, source_target_pairs={{4,8},{8,4},{12,16},{16,12},{20,24},{24,20},{28,32},{32,28},{36,40... | collective-permute-start | bytes 2359304 | tf_op jit(solution)/shard_map/ppermute | solution.py:48
  7.2 6.8 %copy-start = (s32[8]{0:T(128)S(1)}, s32[8]{0:T(128)}, u32[]{:S(2)}) copy-start(s32[8]{0:T(128)} %param.12) | copy-start | bytes 100
  7.2 6.8 %copy-start.1 = (s32[8]{0:T(128)S(1)}, s32[8]{0:T(128)}, u32[]{:S(2)}) copy-start(s32[8]{0:T(128)} %param.13) | copy-start | bytes 100
  10.3 4.5 %collective-permute-start.1 = (bf16[768,512]{1,0:T(8,128)(2,1)}, bf16[768,512]{1,0:T(8,128)(2,1)}, u32[]{:S(2)}, u32[]{:S(2)}) collective-permute-start(bf16[768,512]{1,0:T(8,128)(2,1)} %get-tuple-element.23), channel_id=1, source_target_pairs={{0,4},{4,0},{8,12},{12,8},{16,20},{20,16},{24,28},{28,24},{32,36},... | collective-permute-start | bytes 2359304 | tf_op jit(solution)/shard_map/ppermute | solution.py:48
  10.4 4.4 %collective-permute-start = (bf16[784,512]{1,0:T(8,128)(2,1)}, bf16[784,512]{1,0:T(8,128)(2,1)}, u32[]{:S(2)}, u32[]{:S(2)}) collective-permute-start(bf16[784,512]{1,0:T(8,128)(2,1)} %get-tuple-element.22), channel_id=1, source_target_pairs={{0,4},{4,0},{8,12},{12,8},{16,20},{20,16},{24,28},{28,24},{32,36},... | collective-permute-start | bytes 2408456 | tf_op jit(solution)/shard_map/ppermute | solution.py:48
  10.9 14.0 %collective-permute-start.2 = (bf16[784,512]{1,0:T(8,128)(2,1)S(1)}, bf16[784,512]{1,0:T(8,128)(2,1)S(1)}, u32[]{:S(2)}, u32[]{:S(2)}) collective-permute-start(bf16[784,512]{1,0:T(8,128)(2,1)S(1)} %get-tuple-element.26), channel_id=1, source_target_pairs={{4,8},{8,4},{12,16},{16,12},{20,24},{24,20},{28,32},{32,28},{36,40... | collective-permute-start | bytes 2408456 | tf_op jit(solution)/shard_map/ppermute | solution.py:48
  22.1 26.7 %collective-permute-start.5 = (f32[1536,128]{1,0:T(8,128)}, f32[1536,128]{1,0:T(8,128)}, u32[]{:S(2)}, u32[]{:S(2)}) collective-permute-start(f32[1536,128]{1,0:T(8,128)} %get-tuple-element.32.x_e), channel_id=1, source_target_pairs={{0,4},{4,0},{8,12},{12,8},{16,20},{20,16},{24,28},{28,24},{32,36},... | collective-permute-start | bytes 2359304 | tf_op jit(solution)/shard_map/ppermute | solution.py:48
  22.2 5.4 %collective-permute-start.6 = (f32[8,128]{1,0:T(8,128)S(1)}, f32[8,128]{1,0:T(8,128)S(1)}, u32[]{:S(2)}, u32[]{:S(2)}) collective-permute-start(f32[8,128]{1,0:T(8,128)S(1)} %get-tuple-element.39), channel_id=1, source_target_pairs={{0,4},{4,0},{8,12},{12,8},{16,20},{20,16},{24,28},{28,24},{32,36},... | collective-permute-start | bytes 12296 | tf_op jit(solution)/shard_map/ppermute | solution.py:48
  29.1 33.8 %all-to-all-start = ((s32[256,1,384]{2,1,0:T(1,128)}), s32[256,1,384]{2,1,0:T(1,128)S(1)}, u32[]{:S(2)}, u32[]{:S(2)}) async-start(s32[256,1,384]{2,1,0:T(1,128)} %shard_map.101), calls=%async_computation | async-start | bytes 786432 | tf_op jit(solution)/shard_map/all_to_all | solution.py:594
  45.2 12.0 %collective-permute-start.4 = (s16[1552,128]{1,0:T(8,128)(2,1)S(1)}, s16[1552,128]{1,0:T(8,128)(2,1)S(1)}, u32[]{:S(2)}, u32[]{:S(2)}) collective-permute-start(s16[1552,128]{1,0:T(8,128)(2,1)S(1)} %get-tuple-element.31), channel_id=1, source_target_pairs={{4,8},{8,4},{12,16},{16,12},{20,24},{24,20},{28,32},{32,28},{36,40... | collective-permute-start | bytes 1191944 | tf_op jit(solution)/shard_map/ppermute | solution.py:48

commit v5 on v4

--- a/solution.py
+++ b/solution.py
@@ -17,7 +17,9 @@
 ITERS = 4
 CO_DEV = 8
 NOTE = 16
-BOTH = ("sub", "grp")
+SUB = ("z", "y", "c")
+ALL = (*SUB, "x")
+ROWS = 4 * HALF
 BF, F32, I32, I16 = jnp.bfloat16, jnp.float32, jnp.int32, jnp.int16
 
 ANY = pl.BlockSpec(memory_space=pl.ANY)
@@ -39,13 +41,13 @@
 
 
 def swapped(value, odd):
-    size = lax.axis_size("sub")
+    size = lax.axis_size(SUB)
     pairs = []
     for i in range(size):
         j = ((i + 1) ^ 1) - 1 if odd else i ^ 1
         if 0 <= j < size:
             pairs.append((i, j))
-    return lax.ppermute(value, "sub", pairs)
+    return lax.ppermute(value, SUB, pairs)
 
 
 def pack_kernel(plans, *refs):
@@ -55,7 +57,7 @@
     if noted:
         for i, (ref, kept_at) in enumerate(zip(refs[5:7], small)):
             pltpu.make_async_copy(ref, kept_at, sem.at[2, i]).start()
-    odd = lax.rem(lax.axis_index("sub"), 2) == 1
+    odd = lax.axis_index("c") == 1
     jobs = []
     for out, (first, count, across, _) in zip(outs, plans):
         for j in range(count):
@@ -86,8 +88,8 @@
         target = jnp.where(odd, coarse_up[:, HALF:], coarse_low[:, :HALF])
         note[...] = jnp.zeros_like(note)
         note[0:1, :] = jnp.broadcast_to(refs[4][0].astype(F32), (1, WIDE))
-        note[1:2, :HALF] = (target // 64).astype(F32)
-        note[2:3, :HALF] = (target % 64).astype(F32)
+        note[1:2, 3 * HALF : ROWS] = (target // 64).astype(F32)
+        note[2:3, 3 * HALF : ROWS] = (target % 64).astype(F32)
         for out, plan in zip(outs, plans):
             if plan[3]:
                 out[plan[1] * F : plan[1] * F + NOTE, :] = note[...].astype(BF)
@@ -214,7 +216,7 @@
 
 
 def near_kernel(
-    info, table, su, sl, ru, rl, got_1, got_2, x_out, flux_out, theirs_out, next_m, next_r, m, r, other, note, sem
+    info, owned, su, sl, ru, rl, got_1, got_2, x_out, flux_out, theirs_out, next_m, next_r, m, r, other, note, sem
 ):
     use_up = info[1] == 1
     own_start, own_wait = keeper(su, sl, ru, rl, use_up, 0, HALF, m, r, sem, 0)
@@ -299,7 +301,9 @@
     tail_out[...] = tail
 
 
-def last_kernel(info, m, r, got, x_in, code_in, tail_in, flux_in, x_out, code_out, flux_out):
+def last_kernel(
+    info, m, r, got, x_in, code_in, tail_in, flux_in, after, x_out, code_out, flux_out
+):
     late = HALF - EARLY
     use_up = info[0] == 1
     count = count_of(use_up, info, got[late * F : late * F + NOTE, :COLS])
@@ -328,14 +332,28 @@
     return [vmem((count, F, F), BF), vmem((count, F, COLS), BF)]
 
 
-LARGE = pl.CostEstimate(flops=10**9, bytes_accessed=10**7, transcendentals=0)
+SOME = pl.CostEstimate(flops=3*10**9, bytes_accessed=3*10**7, transcendentals=0)
 SMALL = pl.CostEstimate(flops=1000, bytes_accessed=1000, transcendentals=0)
 
 
-def solve_near(info, table, blocks, got_1, got_2):
+def passed_on(line):
+    def kernel(line, out):
+        out[...] = line[...]
+
+    return pl.pallas_call(
+        kernel,
+        in_specs=[VM],
+        out_specs=VM,
+        out_shape=vmem(line.shape, line.dtype),
+        compiler_params=PARAMS,
+        cost_estimate=SOME,
+    )(line)
+
+
+def solve_near(info, owned, blocks, got_1, got_2):
     return pl.pallas_call(
         near_kernel,
-        in_specs=[SM] * 2 + [ANY] * 6,
+        in_specs=[SM] + [ANY] * 7,
         out_specs=[VM] * 5,
         out_shape=[vmem((HALF * F, COLS), F32)] + [vmem((FC, COLS), F32)] * 2 + kept(HALF),
         scratch_shapes=[
@@ -346,7 +364,7 @@
         ],
         compiler_params=PARAMS,
         cost_estimate=SMALL,
-    )(info, table, *[in_hbm(b) for b in blocks], in_hbm(got_1), in_hbm(got_2))
+    )(info, owned, *[in_hbm(b) for b in blocks], in_hbm(got_1), in_hbm(got_2))
 
 
 def solve_far(m, r, got):
@@ -390,7 +408,7 @@
 
 
 def gather_kernel(x_e, back_e, x_o, up, low, sem):
-    odd = lax.rem(lax.axis_index("sub"), 2) == 1
+    odd = lax.axis_index("c") == 1
 
     @pl.when(odd)
     def _():
@@ -416,87 +434,76 @@
         out_shape=[shape, shape],
         scratch_shapes=[pltpu.SemaphoreType.DMA((3, HALF))],
         compiler_params=PARAMS,
-        cost_estimate=LARGE,
+        cost_estimate=SOME,
     )(x_e, back_e, x_o)
 
 
-SLOTS = 4
-
-
-def encode_kernel(table, flux_e, back_e, flux_o, got, out, codes, heads):
-    rows = jnp.concatenate(
-        [flux_e[:HALF], back_e[:HALF], flux_o[...]], 0
-    )
+def gather_rows_kernel(owned, flux_e, back_e, flux_o, got, out):
+    rows = jnp.concatenate([flux_e[:HALF], back_e[:HALF], flux_o[...]], 0)
     top = jnp.max(jnp.abs(rows), axis=1, keepdims=True)
     digits, power, step = steps_of(jnp.broadcast_to(top, rows.shape))
-    codes[...] = coded(rows, step)
-    heads[...] = digits.astype(I32) * 256 + (power.astype(I32) + 128)
-    out[...] = jnp.zeros_like(out)
-    lane = lax.broadcasted_iota(I32, (1, COLS), 1)
-    none = jnp.zeros((1, COLS), I32)
+    codes = coded(rows, step)
+    scales = digits.astype(I32) * 256 + (power.astype(I32) + 128)
     late = HALF - EARLY
     note = got[late * F : late * F + NOTE, :COLS].astype(F32)
-    told = note[1:2] * 64.0 + note[2:3]
-    rows = [(table[0, i], table[1, i], table[2, i]) for i in range(3 * HALF)]
-    held = []
-    for i in range(HALF):
-        target = jnp.max(jnp.where(lane == i, told, 0.0)).astype(I32)
-        owner = lax.div(target, CO_DEV)
-        rank = 0
-        for other in held:
-            rank = rank + jnp.where(other == owner, 1, 0)
-        held.append(owner)
-        rows.append((owner, jnp.minimum(rank, 1), target - owner * CO_DEV))
-    for i, (owner, rank, local) in enumerate(rows):
-        far = i >= 3 * HALF
-        code = codes[i : i + 1, :]
-        code = jnp.where(rank == 0, code * 65536, code & 65535)
-        slot = rank + (2 if far else 0)
-        head = jnp.where(lane == slot * CO_DEV + local, heads[i : i + 1, :], 0)
-        line = jnp.concatenate([none, code, head] if far else [code, none, head], 1)
-        if far:
-            line = jnp.where(table[3, 0] == 1, line, 0)
-        out[owner] = out[owner] | line
-
-
-def encode(table, flux_e, back_e, flux_o, got, devices):
-    return pl.pallas_call(
-        encode_kernel,
-        in_specs=[SM] + [VM] * 4,
+    head = (owned[...] + note[1:2] * 64.0 + note[2:3]).astype(I32)
+    lane = lax.broadcasted_iota(I32, (1, COLS), 1)
+    for i in range(ROWS):
+        head = jnp.where(lane == ROWS + i, scales[i : i + 1], head)
+    half = ROWS // 2
+    pairs = codes[:half] * 65536 + (codes[half:] & 65535)
+    line = jnp.concatenate([pairs[i : i + 1] for i in range(half)] + [head], 1)
+    for d in range(out.shape[0]):
+        out[d] = line
+
+
+def gather_rows(owned, flux_e, back_e, flux_o, got, peers):
+    return pl.pallas_call(
+        gather_rows_kernel,
+        in_specs=[VM] * 5,
         out_specs=VM,
-        out_shape=vmem((devices, 1, 3 * COLS), I32),
-        scratch_shapes=[vmem((4 * HALF, COLS), I32)] * 2,
+        out_shape=vmem((peers, 1, (ROWS // 2 + 1) * COLS), I32),
         compiler_params=PARAMS,
         cost_estimate=SMALL,
-    )(table, *map(in_vmem, (flux_e, back_e, flux_o, got)))
-
-
-def decode(got):
-    n = got.shape[0] // 3
-    words = [got[pl.ds(c, n, stride=3), :] for c in range(3)]
-    head = words[2]
-    power = (head & 255).astype(F32) - 128.0
-    step = jnp.where(head == 0, 0.0, (head >> 8).astype(F32) * (2.0**-21) * jnp.exp2(power))
-    used = SLOTS * CO_DEV
-    left = jnp.concatenate(three(step.T[:used]), 0).astype(BF)
-    parts = []
-    for w in words[:2]:
-        for q in (w >> 16, (w << 16) >> 16):
-            high = q >> 8
-            parts.append((high.astype(F32) * 256.0).astype(BF))
-            parts.append((q - high * 256).astype(F32).astype(BF))
-    prods = mm(left, jnp.concatenate(parts, 1))
-    prods = prods[:used] + prods[used : 2 * used] + prods[2 * used :]
-    total = jnp.zeros((CO_DEV, COLS), F32)
-    for r in range(SLOTS):
-        rows = prods[r * CO_DEV : (r + 1) * CO_DEV]
-        total = total + rows[:, 2 * r * COLS : (2 * r + 1) * COLS]
-        total = total + rows[:, (2 * r + 1) * COLS : (2 * r + 2) * COLS]
-    return total
+    )(*map(in_vmem, (owned, flux_e, back_e, flux_o, got)))
+
+
+def add_kernel(got, out):
+    half = ROWS // 2
+    peers = got.shape[0] // (half + 1)
+    m = lax.broadcasted_iota(I32, (1, COLS), 1)
+    wanted = (lax.axis_index("z") * 4 + (m >> 5)) * 2 + lax.axis_index("c")
+    wanted = (wanted * 4 + ((m >> 3) & 3)) * CO_DEV + (m & 7)
+    head = got[pl.ds(half, peers, stride=half + 1), :]
+    step = (head >> 8).astype(F32) * jnp.exp2((head & 255).astype(F32) - 128.0) * (2.0**-21)
+    words = [got[pl.ds(r, peers, stride=half + 1), :] for r in range(half)]
+    codes = [w >> 16 for w in words] + [(w << 16) >> 16 for w in words]
+    chosen, pieces = [], []
+    for r in range(ROWS):
+        target = jnp.broadcast_to(head[:, r : r + 1], (peers, COLS))
+        chosen.append(jnp.where(target == wanted, 1.0, 0.0))
+        pieces.append(codes[r].astype(F32) * step[:, ROWS + r : ROWS + r + 1])
+    chosen = jnp.concatenate(chosen, 0).T.astype(BF)
+    parts = [piece.astype(BF) for piece in three(jnp.concatenate(pieces, 0))]
+    sums = mm(chosen, jnp.concatenate(parts, 1))
+    sums = sums[:, :COLS] + sums[:, COLS : 2 * COLS] + sums[:, 2 * COLS :]
+    for d in range(out.shape[0]):
+        out[d] = sums[d * CO_DEV : (d + 1) * CO_DEV]
+
+
+def add_rows(arrived, peers):
+    return pl.pallas_call(
+        add_kernel,
+        in_specs=[VM],
+        out_specs=VM,
+        out_shape=vmem((peers, CO_DEV, COLS), F32),
+        compiler_params=PARAMS,
+        cost_estimate=SOME,
+    )(in_vmem(arrived))
 
 
 def panel_kernel(back_o, up_in, low_in, up, low, panels, sem):
-    odd = lax.rem(lax.axis_index("sub"), 2) == 1
+    odd = lax.axis_index("c") == 1
     tail = back_o[HALF * F :, :].astype(I32)
     for i in range(HALF):
         high, rest, power = (tail[3 * i + j : 3 * i + j + 1] for j in range(3))
@@ -530,7 +537,10 @@
 
 
 def coarse_kernel(arrived, after, out):
-    out[...] = decode(arrived)
+    total = arrived[0]
+    for d in range(1, arrived.shape[0]):
+        total = total + arrived[d]
+    out[...] = total
 
 
 def sum_rows(arrived, after):
@@ -545,10 +555,9 @@
 
 
 def shards(schur_up, schur_low, resid_up, resid_low, counts, coarse_up, coarse_low):
-    subs = lax.axis_size("sub")
-    devices = lax.axis_size(BOTH)
-    s = lax.axis_index("sub")
-    odd = (s % 2).astype(I32)
+    subs = lax.axis_size(SUB)
+    s = lax.axis_index(SUB)
+    odd = lax.axis_index("c").astype(I32)
     even = 1 - odd
     blocks = (schur_up, schur_low, resid_up, resid_low)
 
@@ -576,44 +585,46 @@
             pick(coarse_up[:HALF], coarse_low[HALF:]),
         ]
     )
-    order = jnp.arange(3 * HALF, dtype=I32)
-    owner, local = targets // CO_DEV, targets % CO_DEV
-    same = (owner[:, None] == owner[None, :]) & (order[None, :] < order[:, None])
-    rank = jnp.minimum(jnp.sum(same, axis=1), 1).astype(I32)
-    paired = jnp.broadcast_to(((s > 0) & (s < subs - 1)).astype(I32), owner.shape)
-    table = jnp.stack([owner, rank, local, paired])
-
-    x_e, flux_e, theirs_e, own_m, own_r = solve_near(info, table, blocks, got_1, got_2)
+    held = jnp.where((s > 0) & (s < subs - 1), 0, -1) * jnp.ones((HALF,), I32)
+    owned = jnp.pad(jnp.concatenate([targets, held]), (0, COLS - ROWS)).astype(F32)[None]
+    owned = passed_on(owned)
+
+    x_e, flux_e, theirs_e, own_m, own_r = solve_near(info, owned, blocks, got_1, got_2)
     back_e = swapped(x_e, False)
     back_flux = swapped(theirs_e, False)
     early = solve_far(own_m, own_r, got_a)
-    x_o, code_o, flux_o = solve_last(info, own_m, own_r, got_b, *early)
+    x_o, code_o, flux_o = solve_last(info, own_m, own_r, got_b, *early, back_flux)
     back_o = swapped(code_o, True)
 
-    parcels = encode(table, flux_e, back_flux, flux_o, got_b, devices)
-    arrived = lax.all_to_all(parcels, BOTH, 0, 0, tiled=True)
+    near_axes, far_axes = ("z", "c"), ("y", "x")
+    peers = lax.axis_size(near_axes)
+    parcels = gather_rows(owned, flux_e, back_flux, flux_o, got_b, peers)
+    arrived = lax.all_to_all(parcels, near_axes, 0, 0, tiled=True)
+    sums = add_rows(arrived.reshape(peers * (ROWS // 2 + 1), COLS), lax.axis_size(far_axes))
+    sums = lax.all_to_all(sums, far_axes, 0, 0, tiled=True)
     up, low = gather(x_e, back_e, x_o)
     up, low = put_panels(back_o, up, low)
-    return (up, low, sum_rows(arrived.reshape(devices * 3, COLS), up))
+    return (up, low, sum_rows(sums, up))
 
 
 def solution(mesh):
+    devices = mesh.devices.reshape(-1, 4, 2, mesh.shape["grp"])
     return jax.shard_map(
         shards,
-        mesh=mesh,
+        mesh=jax.sharding.Mesh(devices, ALL),
         in_specs=(
-            P(BOTH, None, None),
-            P(BOTH, None, None),
-            P(BOTH, None, None),
-            P(BOTH, None, None),
-            P(BOTH),
-            P(BOTH),
-            P(BOTH),
+            P(ALL, None, None),
+            P(ALL, None, None),
+            P(ALL, None, None),
+            P(ALL, None, None),
+            P(ALL),
+            P(ALL),
+            P(ALL),
         ),
         out_specs=(
-            P(BOTH, None, None),
-            P(BOTH, None, None),
-            P(BOTH, None),
+            P(ALL, None, None),
+            P(ALL, None, None),
+            P(ALL, None),
         ),
         check_vma=False,
     )

time: 64.2 us -> 62 us (0.966)
  waiting for transfers between devices: 10.4 us -> 9.2 us
    ppermute x7, waiting for transfers between devices: 5.55 us -> 0.46 us  [swapped(): return lax.ppermute(value, SUB, pairs)]
    all_to_all x1 -> x2, waiting for transfers between devices: 4.88 us -> 8.74 us  [the longest x1 6.06 us: shards(): arrived = lax.all_to_all(parcels, near_axes, 0, 0, tiled=True)]
    ppermute x7, starting transfers between devices: 12.5 us -> 10.9 us  [swapped(): return lax.ppermute(value, SUB, pairs)]
    all_to_all x1 -> x2, starting transfers between devices: 16 us -> 17.2 us  [the longest x1 12.3 us: shards(): arrived = lax.all_to_all(parcels, near_axes, 0, 0, tiled=True)]
    pallas_call x2 -> x4, Pallas kernels: 8.85 us -> 9.03 us  [the longest x1 7.28 us: solve_near(): pl.pallas_call(near_kernel, in_specs=[SM] + [ANY] * 7, out_specs=[VM] * 5...]
  transfers between devices with their start and end apart: 8 -> 9, of which waited for: 2 -> 3; matrix products, arithmetic and copies ran while one was open for 1% -> 0% of each run, Pallas kernels for 32% -> 34%
where the time goes in v5:
time: 62 us; the launch traced here: 61.6 us
  starting transfers between devices  28 us (45%)
  Pallas kernels  22.7 us (37%)
  waiting for transfers between devices  9.2 us (15%)
  between operations  1.45 us (2%)
    all_to_all x1, starting transfers between devices, shards(): arrived = lax.all_to_all(parcels, near_axes, 0, 0, tiled=True)  12.3 us
    ppermute x7, starting transfers between devices, swapped(): return lax.ppermute(value, SUB, pairs)  10.9 us
    pallas_call x1, Pallas kernels, solve_near(): pl.pallas_call(near_kernel, in_specs=[SM] + [ANY] * 7, out_specs=[VM] * 5...  7.28 us
    all_to_all x1, waiting for transfers between devices, shards(): arrived = lax.all_to_all(parcels, near_axes, 0, 0, tiled=True)  6.06 us
    all_to_all x1, starting transfers between devices, shards(): sums = lax.all_to_all(sums, far_axes, 0, 0, tiled=True)  4.83 us
    pallas_call x2, Pallas kernels, pack(): pl.pallas_call(functools.partial(pack_kernel, plans), in_specs=[ANY] * 4...  4.33 us
    pallas_call x1, Pallas kernels, gather(): pl.pallas_call(gather_kernel, in_specs=[VM] * 3, out_specs=[ANY] * 2, out...  2.86 us
    pallas_call x1, Pallas kernels, solve_last(): pl.pallas_call(last_kernel, in_specs=[SM] + [VM] * (3 + len(early)), out_...  2.71 us
  transfers between devices with their start and end apart: 9, of which 3 were waited for; matrix products, arithmetic and copies ran while one was open for 0% of the time, Pallas kernels for 34%

profile of v5, /device:TPU:1, one launch (start us, length us, event | category | flops | bytes accessed | tf_op | source)
XLA Modules:
  0.0 61.6 jit_solution(10651906548498864094)
XLA Ops:
  0.6 1.3 %shard_map.95.refs_7_ = bf16[768,512]{1,0:T(8,128)(2,1)S(1)} custom-call(bf16[8,384,384]{2,1,0:T(8,128)(2,1)} %su.1, bf16[8,384,384]{2,1,0:T(8,128)(2,1)} %sl.1, bf16[8,384,128]{2,1,0:T(8,128)(2,1)} %ru.1, bf16[8,384,128]{2,1,0:T(8,128)(2,1)} %rl.1), custom_call_target="tpu_custom_call" | custom-call | flops 1000 | bytes 1000 | tf_op jit(solution)/shard_map/pallas_call | solution.py:104
  2.0 4.6 %collective-permute-start.3 = (bf16[768,512]{1,0:T(8,128)(2,1)S(1)}, bf16[768,512]{1,0:T(8,128)(2,1)S(1)}, u32[]{:S(2)}, u32[]{:S(2)}) collective-permute-start(bf16[768,512]{1,0:T(8,128)(2,1)S(1)} %shard_map.95.refs_7_), channel_id=1, source_target_pairs={{4,8},{8,4},{12,16},{16,12},{20,24},{24,20},{28,32},{32,28},{36,40... | collective-permute-start | bytes 2359304 | tf_op jit(solution)/shard_map/ppermute | solution.py:50
  7.3 3.0 %shard_map.96 = (bf16[784,512]{1,0:T(8,128)(2,1)}, bf16[768,512]{1,0:T(8,128)(2,1)}, bf16[784,512]{1,0:T(8,128)(2,1)S(1)}) custom-call(bf16[8,384,384]{2,1,0:T(8,128)(2,1)} %su.1, bf16[8,384,384]{2,1,0:T(8,128)(2,1)} %sl.1, bf16[8,384,128]{2,1,0:T(8,128)(2,1)} %ru.1, bf16[8,384,128]{2,1,0:T(8,128)(2,1)} %rl.1, s32[1]{0:T(128)} %copy.14.refs_4_, ...), custom_call_target="tpu_custom_call" | custom-call | flops 1000 | bytes 1000 | tf_op jit(solution)/shard_map/pallas_call | solution.py:104
  10.3 0.1 collective-permute-start.1
  10.4 0.5 collective-permute-start
  10.8 3.2 %collective-permute-start.2 = (bf16[784,512]{1,0:T(8,128)(2,1)S(1)}, bf16[784,512]{1,0:T(8,128)(2,1)S(1)}, u32[]{:S(2)}, u32[]{:S(2)}) collective-permute-start(bf16[784,512]{1,0:T(8,128)(2,1)S(1)} %get-tuple-element.26), channel_id=1, source_target_pairs={{4,8},{8,4},{12,16},{16,12},{20,24},{24,20},{28,32},{32,28},{36,40... | collective-permute-start | bytes 2408456 | tf_op jit(solution)/shard_map/ppermute | solution.py:50
  14.2 0.1 pad_add_fusion.1
  14.2 0.1 pad_add_fusion.info
  14.3 7.3 %shard_map.97 = (f32[1536,128]{1,0:T(8,128)}, f32[8,128]{1,0:T(8,128)S(1)}, f32[8,128]{1,0:T(8,128)S(1)}, bf16[4,384,384]{2,1,0:T(8,128)(2,1)S(1)}, bf16[4,384,128]{2,1,0:T(8,128)(2,1)S(1)}) custom-call(s32[3]{0:T(128)S(1)} %pad_add_fusion.info, f32[1,128]{1,0:T(1,128)S(1)} %shard_map.94.owned, bf16[8,384,384]{2,1,0:T(8,128)(2,1)} %su.1, ...), custom_call_target="tpu_custom_call" | custom-call | flops 1000 | bytes 1000 | tf_op jit(solution)/shard_map/pallas_call | solution.py:354
  21.6 0.1 collective-permute-start.6
  21.7 0.5 collective-permute-start.4
  22.2 2.2 %shard_map.98 = (f32[768,128]{1,0:T(8,128)S(1)}, s16[768,128]{1,0:T(8,128)(2,1)S(1)}, s32[16,128]{1,0:T(8,128)S(1)}, f32[8,128]{1,0:T(8,128)S(1)}) custom-call(bf16[4,384,384]{2,1,0:T(8,128)(2,1)S(1)} %get-tuple-element.24.m, bf16[4,384,128]{2,1,0:T(8,128)(2,1)S(1)} %get-tuple-element.25.r, bf16[768,512]{1,0:T(8,128)(2,1)S(1)} %collective-permute-done.3.got), custom_call_target="tpu_custom_call" | custom-call | flops 1000 | bytes 1000 | tf_op jit(solution)/shard_map/pallas_call | solution.py:371
  24.4 0.4 collective-permute-done.2.got
  24.9 2.7 %shard_map.99 = (f32[1536,128]{1,0:T(8,128)S(1)}, s16[1552,128]{1,0:T(8,128)(2,1)S(1)}, f32[8,128]{1,0:T(8,128)S(1)}) custom-call(s32[3]{0:T(128)S(1)} %pad_add_fusion.info, bf16[4,384,384]{2,1,0:T(8,128)(2,1)S(1)} %get-tuple-element.24.m, bf16[4,384,128]{2,1,0:T(8,128)(2,1)S(1)} %get-tuple-element.25.r, bf16[784,512]{1,0:T(8,128)(2,1)S(1)} %collective-permute-done.2.got, ...), custom_call_target="tpu_custom_call" | custom-call | flops 1000 | bytes 1000 | tf_op jit(solution)/shard_map/pallas_call | solution.py:387
  27.6 0.8 %shard_map.102 = s32[16,1,1152]{2,1,0:T(1,128)} custom-call(f32[1,128]{1,0:T(1,128)S(1)} %shard_map.94.owned, f32[8,128]{1,0:T(8,128)S(1)} %get-tuple-element.39.flux_e, f32[8,128]{1,0:T(8,128)S(1)} %collective-permute-done.4.after.back_e, f32[8,128]{1,0:T(8,128)S(1)} %get-tuple-element.40.flux_o, bf16[784,512]{1,0:T(8,128)(2,1)S(1)} %collective-permute-done.2.got), custom_call_target="tpu_custom_call" | custom-call | flops 1000 | bytes 1000 | tf_op jit(solution)/shard_map/pallas_call | solution.py:461
  28.3 12.3 %all-to-all-start = ((s32[16,1,1152]{2,1,0:T(1,128)}), s32[16,1,1152]{2,1,0:T(1,128)S(1)}, u32[]{:S(2)}, u32[]{:S(2)}) async-start(s32[16,1,1152]{2,1,0:T(1,128)} %shard_map.102), calls=%async_computation | async-start | bytes 147456 | tf_op jit(solution)/shard_map/all_to_all | solution.py:602
  40.7 1.9 %collective-permute-start.5 = (s16[1552,128]{1,0:T(8,128)(2,1)S(1)}, s16[1552,128]{1,0:T(8,128)(2,1)S(1)}, u32[]{:S(2)}, u32[]{:S(2)}) collective-permute-start(s16[1552,128]{1,0:T(8,128)(2,1)S(1)} %get-tuple-element.32), channel_id=1, source_target_pairs={{4,8},{8,4},{12,16},{16,12},{20,24},{24,20},{28,32},{32,28},{36,40... | collective-permute-start | bytes 1191944 | tf_op jit(solution)/shard_map/ppermute | solution.py:50
  42.6 6.1 %all-to-all-done = s32[16,1,1152]{2,1,0:T(1,128)S(1)} async-done(((s32[16,1,1152]{2,1,0:T(1,128)}), s32[16,1,1152]{2,1,0:T(1,128)S(1)}, u32[]{:S(2)}, u32[]{:S(2)}) %all-to-all-start) | async-done | bytes 73760 | tf_op jit(solution)/shard_map/all_to_all | solution.py:602
  48.7 1.0 %shard_map.103 = f32[16,8,128]{2,1,0:T(8,128)} custom-call(s32[144,128]{1,0:T(8,128)S(1)} %bitcast.10), custom_call_target="tpu_custom_call" | custom-call | flops 3000000000 | bytes 30000000 | tf_op jit(solution)/shard_map/pallas_call | solution.py:495
  49.6 4.8 %all-to-all-start.1 = ((f32[16,8,128]{2,1,0:T(8,128)}), f32[16,8,128]{2,1,0:T(8,128)S(1)}, u32[]{:S(2)}, u32[]{:S(2)}) async-start(f32[16,8,128]{2,1,0:T(8,128)} %shard_map.103), calls=%async_computation.1 | async-start | bytes 131072 | tf_op jit(solution)/shard_map/all_to_all | solution.py:604
  54.5 2.9 %shard_map.100 = (f32[8,384,128]{2,1,0:T(8,128)}, f32[8,384,128]{2,1,0:T(8,128)}) custom-call(f32[1536,128]{1,0:T(8,128)} %get-tuple-element.33.x_e, f32[1536,128]{1,0:T(8,128)} %collective-permute-done.6.back_e, f32[1536,128]{1,0:T(8,128)S(1)} %get-tuple-element.34.x_o), custom_call_target="tpu_custom_call" | custom-call | flops 3000000000 | bytes 30000000 | tf_op jit(solution)/shard_map/pallas_call | solution.py:430
  57.4 0.9 %shard_map.101 = (f32[8,384,128]{2,1,0:T(8,128)}, f32[8,384,128]{2,1,0:T(8,128)}) custom-call(s16[1552,128]{1,0:T(8,128)(2,1)S(1)} %collective-permute-done.5.back_o, f32[8,384,128]{2,1,0:T(8,128)} %get-tuple-element.35.up_in, f32[8,384,128]{2,1,0:T(8,128)} %get-tuple-element.36.low_in), custom_call_target="tpu_custom_call", output_to_operand_aliasing={{0}: (1, {}), {1}: (2, {})} | custom-call | flops 1000 | bytes 1000 | tf_op jit(solution)/shard_map/pallas_call | solution.py:527
  58.3 2.7 %all-to-all-done.1.arrived = f32[16,8,128]{2,1,0:T(8,128)S(1)} async-done(((f32[16,8,128]{2,1,0:T(8,128)}), f32[16,8,128]{2,1,0:T(8,128)S(1)}, u32[]{:S(2)}, u32[]{:S(2)}) %all-to-all-start.1) | async-done | bytes 65568 | tf_op jit(solution)/shard_map/all_to_all | solution.py:604
  61.0 0.6 shard_map.104
  (14 shorter events, 0.1 us)
Async XLA Ops:
  2.0 20.2 %collective-permute-start.3 = (bf16[768,512]{1,0:T(8,128)(2,1)S(1)}, bf16[768,512]{1,0:T(8,128)(2,1)S(1)}, u32[]{:S(2)}, u32[]{:S(2)}) collective-permute-start(bf16[768,512]{1,0:T(8,128)(2,1)S(1)} %shard_map.95.refs_7_), channel_id=1, source_target_pairs={{4,8},{8,4},{12,16},{16,12},{20,24},{24,20},{28,32},{32,28},{36,40... | collective-permute-start | bytes 2359304 | tf_op jit(solution)/shard_map/ppermute | solution.py:50
  7.2 6.8 %copy-start = (s32[8]{0:T(128)S(1)}, s32[8]{0:T(128)}, u32[]{:S(2)}) copy-start(s32[8]{0:T(128)} %param.12) | copy-start | bytes 100
  7.2 6.8 %copy-start.1 = (s32[8]{0:T(128)S(1)}, s32[8]{0:T(128)}, u32[]{:S(2)}) copy-start(s32[8]{0:T(128)} %param.13) | copy-start | bytes 100
  10.3 4.1 %collective-permute-start.1 = (bf16[768,512]{1,0:T(8,128)(2,1)}, bf16[768,512]{1,0:T(8,128)(2,1)}, u32[]{:S(2)}, u32[]{:S(2)}) collective-permute-start(bf16[768,512]{1,0:T(8,128)(2,1)} %get-tuple-element.23), channel_id=1, source_target_pairs={{0,4},{4,0},{8,12},{12,8},{16,20},{20,16},{24,28},{28,24},{32,36},... | collective-permute-start | bytes 2359304 | tf_op jit(solution)/shard_map/ppermute | solution.py:50
  10.4 4.0 %collective-permute-start = (bf16[784,512]{1,0:T(8,128)(2,1)}, bf16[784,512]{1,0:T(8,128)(2,1)}, u32[]{:S(2)}, u32[]{:S(2)}) collective-permute-start(bf16[784,512]{1,0:T(8,128)(2,1)} %get-tuple-element.22), channel_id=1, source_target_pairs={{0,4},{4,0},{8,12},{12,8},{16,20},{20,16},{24,28},{28,24},{32,36},... | collective-permute-start | bytes 2408456 | tf_op jit(solution)/shard_map/ppermute | solution.py:50
  10.8 14.0 %collective-permute-start.2 = (bf16[784,512]{1,0:T(8,128)(2,1)S(1)}, bf16[784,512]{1,0:T(8,128)(2,1)S(1)}, u32[]{:S(2)}, u32[]{:S(2)}) collective-permute-start(bf16[784,512]{1,0:T(8,128)(2,1)S(1)} %get-tuple-element.26), channel_id=1, source_target_pairs={{4,8},{8,4},{12,16},{16,12},{20,24},{24,20},{28,32},{32,28},{36,40... | collective-permute-start | bytes 2408456 | tf_op jit(solution)/shard_map/ppermute | solution.py:50
  21.6 32.9 %collective-permute-start.6 = (f32[1536,128]{1,0:T(8,128)}, f32[1536,128]{1,0:T(8,128)}, u32[]{:S(2)}, u32[]{:S(2)}) collective-permute-start(f32[1536,128]{1,0:T(8,128)} %get-tuple-element.33.x_e), channel_id=1, source_target_pairs={{0,4},{4,0},{8,12},{12,8},{16,20},{20,16},{24,28},{28,24},{32,36},... | collective-permute-start | bytes 2359304 | tf_op jit(solution)/shard_map/ppermute | solution.py:50
  21.7 3.1 %collective-permute-start.4 = (f32[8,128]{1,0:T(8,128)S(1)}, f32[8,128]{1,0:T(8,128)S(1)}, u32[]{:S(2)}, u32[]{:S(2)}) collective-permute-start(f32[8,128]{1,0:T(8,128)S(1)} %get-tuple-element.31), channel_id=1, source_target_pairs={{0,4},{4,0},{8,12},{12,8},{16,20},{20,16},{24,28},{28,24},{32,36},... | collective-permute-start | bytes 12296 | tf_op jit(solution)/shard_map/ppermute | solution.py:50
  28.3 20.3 %all-to-all-start = ((s32[16,1,1152]{2,1,0:T(1,128)}), s32[16,1,1152]{2,1,0:T(1,128)S(1)}, u32[]{:S(2)}, u32[]{:S(2)}) async-start(s32[16,1,1152]{2,1,0:T(1,128)} %shard_map.102), calls=%async_computation | async-start | bytes 147456 | tf_op jit(solution)/shard_map/all_to_all | solution.py:602
  40.7 16.7 %collective-permute-start.5 = (s16[1552,128]{1,0:T(8,128)(2,1)S(1)}, s16[1552,128]{1,0:T(8,128)(2,1)S(1)}, u32[]{:S(2)}, u32[]{:S(2)}) collective-permute-start(s16[1552,128]{1,0:T(8,128)(2,1)S(1)} %get-tuple-element.32), channel_id=1, source_target_pairs={{4,8},{8,4},{12,16},{16,12},{20,24},{24,20},{28,32},{32,28},{36,40... | collective-permute-start | bytes 1191944 | tf_op jit(solution)/shard_map/ppermute | solution.py:50
  49.6 11.4 %all-to-all-start.1 = ((f32[16,8,128]{2,1,0:T(8,128)}), f32[16,8,128]{2,1,0:T(8,128)S(1)}, u32[]{:S(2)}, u32[]{:S(2)}) async-start(f32[16,8,128]{2,1,0:T(8,128)} %shard_map.103), calls=%async_computation.1 | async-start | bytes 131072 | tf_op jit(solution)/shard_map/all_to_all | solution.py:604

commit v6 on v5

--- a/solution.py
+++ b/solution.py
@@ -13,7 +13,7 @@
 WIDE = F + COLS
 FC = 8
 HALF = FC // 2
-EARLY = 2
+EARLY = 3
 ITERS = 4
 CO_DEV = 8
 NOTE = 16
@@ -53,7 +53,7 @@
 def pack_kernel(plans, *refs):
     su, sl, ru, rl = refs[:4]
     noted = any(plan[3] for plan in plans)
-    outs, (*small, note, sem) = refs[-4 - len(plans) : -4], refs[-4:]
+    outs, (*small, note, sem) = refs[-4 - len(plans) - noted : -4], refs[-4:]
     if noted:
         for i, (ref, kept_at) in enumerate(zip(refs[5:7], small)):
             pltpu.make_async_copy(ref, kept_at, sem.at[2, i]).start()
@@ -91,15 +91,30 @@
         note[1:2, 3 * HALF : ROWS] = (target // 64).astype(F32)
         note[2:3, 3 * HALF : ROWS] = (target % 64).astype(F32)
         for out, plan in zip(outs, plans):
-            if plan[3]:
-                out[plan[1] * F : plan[1] * F + NOTE, :] = note[...].astype(BF)
+            for k in range(plan[3]):
+                start = plan[1] * F + k * NOTE
+                out[start : start + NOTE, :] = note[...].astype(BF)
+        owned = outs[-1]
+        s = (lax.axis_index("z") * 4 + lax.axis_index("y")) * 2 + lax.axis_index("c")
+        alone = (s == 0) | (s == lax.axis_size(SUB) - 1)
+        owned[...] = jnp.zeros_like(owned)
+        parts = [
+            jnp.where(odd, coarse_low[:, HALF:], coarse_up[:, :HALF]),
+            jnp.where(odd, coarse_low[:, :HALF], coarse_up[:, HALF:]),
+            jnp.where(odd, coarse_up[:, :HALF], coarse_low[:, HALF:]),
+            jnp.broadcast_to(jnp.where(alone, -1, 0), (1, HALF)),
+        ]
+        for i, part in enumerate(parts):
+            owned[:, i * HALF : (i + 1) * HALF] = part.astype(F32)
     for slot, (out, j, face, _) in enumerate(jobs):
         for c in copies(slot, out, j, su, ru, HALF + face):
             c.wait()
 
 
 def pack(plans, blocks, small=(), after=()):
-    shapes = [vmem((plan[1] * F + (NOTE if plan[3] else 0), WIDE), BF) for plan in plans]
+    shapes = [vmem((plan[1] * F + NOTE * plan[3], WIDE), BF) for plan in plans]
+    if small:
+        shapes.append(jax.ShapeDtypeStruct((1, COLS), F32))
     given = [small[0], *[in_hbm(v[None]) for v in small[1:]]] if small else []
     return pl.pallas_call(
         functools.partial(pack_kernel, plans),
@@ -215,9 +230,9 @@
     return jnp.where(lower, info[2].astype(F32), note.astype(F32)[:1])
 
 
-def near_kernel(
-    info, owned, su, sl, ru, rl, got_1, got_2, x_out, flux_out, theirs_out, next_m, next_r, m, r, other, note, sem
-):
+def near_kernel(info, after, su, sl, ru, rl, *refs):
+    got = refs[:HALF]
+    x_out, flux_out, theirs_out, next_m, next_r, m, r, other, note, sem = refs[HALF:]
     use_up = info[1] == 1
     own_start, own_wait = keeper(su, sl, ru, rl, use_up, 0, HALF, m, r, sem, 0)
     next_start, next_wait = keeper(
@@ -225,17 +240,14 @@
     )
 
     def got_copy(i):
-        part, j = (got_1, i) if i < 2 else (got_2, i - 2)
-        return pltpu.make_async_copy(part.at[pl.ds(j * F, F)], other.at[i], sem.at[2, i])
-
-    note_copy = pltpu.make_async_copy(got_1.at[pl.ds(2 * F, NOTE)], note, sem.at[2, HALF])
+        return pltpu.make_async_copy(got[i].at[pl.ds(0, F)], other.at[i], sem.at[2, i])
+
+    note_copy = pltpu.make_async_copy(got[0].at[pl.ds(F, NOTE)], note, sem.at[2, HALF])
     for i in range(HALF):
         own_start(i)
         got_copy(i).start()
         if i == 0:
             note_copy.start()
-    for i in range(HALF):
-        next_start(i)
     flux_out[...] = jnp.zeros_like(flux_out)
     theirs_out[...] = jnp.zeros_like(theirs_out)
     base = jnp.where(use_up, 0, HALF)
@@ -245,6 +257,8 @@
             own_wait(i)
             got_copy(i).wait()
         if start == 0:
+            for i in range(HALF):
+                next_start(i)
             note_copy.wait()
             count = count_of(use_up, info, note[:, :COLS])
         solved = solve_pair([(m[i], r[i]) for i in faces], [other[i] for i in faces])
@@ -271,8 +285,8 @@
 
 def solve_all(first, count, m, r, got):
     out = []
-    for start in range(0, count, 2):
-        faces = range(start, min(start + 2, count))
+    for start in range(0, count, 3):
+        faces = range(start, min(start + 3, count))
         out += solve_pair(
             [(m[first + i], r[first + i]) for i in faces],
             [got[i * F : (i + 1) * F, :] for i in faces],
@@ -336,24 +350,24 @@
 SMALL = pl.CostEstimate(flops=1000, bytes_accessed=1000, transcendentals=0)
 
 
-def passed_on(line):
-    def kernel(line, out):
-        out[...] = line[...]
+def passed_on(value):
+    def kernel(value, out):
+        out[...] = value[...]
 
     return pl.pallas_call(
         kernel,
         in_specs=[VM],
         out_specs=VM,
-        out_shape=vmem(line.shape, line.dtype),
+        out_shape=vmem(value.shape, value.dtype),
         compiler_params=PARAMS,
         cost_estimate=SOME,
-    )(line)
-
-
-def solve_near(info, owned, blocks, got_1, got_2):
+    )(in_vmem(value))
+
+
+def solve_near(info, after, blocks, got_near):
     return pl.pallas_call(
         near_kernel,
-        in_specs=[SM] + [ANY] * 7,
+        in_specs=[SM] + [ANY] * (5 + HALF),
         out_specs=[VM] * 5,
         out_shape=[vmem((HALF * F, COLS), F32)] + [vmem((FC, COLS), F32)] * 2 + kept(HALF),
         scratch_shapes=[
@@ -364,7 +378,7 @@
         ],
         compiler_params=PARAMS,
         cost_estimate=SMALL,
-    )(info, owned, *[in_hbm(b) for b in blocks], in_hbm(got_1), in_hbm(got_2))
+    )(info, after, *[in_hbm(b) for b in (*blocks, *got_near)])
 
 
 def solve_far(m, r, got):
@@ -465,7 +479,7 @@
         out_shape=vmem((peers, 1, (ROWS // 2 + 1) * COLS), I32),
         compiler_params=PARAMS,
         cost_estimate=SMALL,
-    )(*map(in_vmem, (owned, flux_e, back_e, flux_o, got)))
+    )(owned, *map(in_vmem, (flux_e, back_e, flux_o, got)))
 
 
 def add_kernel(got, out):
@@ -484,9 +498,8 @@
         chosen.append(jnp.where(target == wanted, 1.0, 0.0))
         pieces.append(codes[r].astype(F32) * step[:, ROWS + r : ROWS + r + 1])
     chosen = jnp.concatenate(chosen, 0).T.astype(BF)
-    parts = [piece.astype(BF) for piece in three(jnp.concatenate(pieces, 0))]
-    sums = mm(chosen, jnp.concatenate(parts, 1))
-    sums = sums[:, :COLS] + sums[:, COLS : 2 * COLS] + sums[:, 2 * COLS :]
+    sums = mm(chosen, jnp.concatenate(split(jnp.concatenate(pieces, 0)), 1))
+    sums = sums[:, :COLS] + sums[:, COLS:]
     for d in range(out.shape[0]):
         out[d] = sums[d * CO_DEV : (d + 1) * CO_DEV]
 
@@ -561,35 +574,23 @@
     even = 1 - odd
     blocks = (schur_up, schur_low, resid_up, resid_low)
 
-    def pick(if_odd, if_even):
-        return jnp.where(odd == 1, if_odd, if_even)
-
-    (pack_a,) = pack([(0, EARLY, True, False)], blocks)
+    (pack_a,) = pack([(0, EARLY, True, 0)], blocks)
     got_a = swapped(pack_a, True)
-    pack_1, pack_2, pack_b = pack(
-        [(0, 2, False, True), (2, 2, False, False), (EARLY, HALF - EARLY, True, True)],
+    *near, pack_b, owned = pack(
+        [(k, 1, False, 1 if k == 0 else 0) for k in range(HALF)]
+        + [(EARLY, HALF - EARLY, True, 2)],
         blocks,
         (counts, coarse_up, coarse_low),
         (pack_a,),
     )
-    got_1 = swapped(pack_1, False)
-    got_2 = swapped(pack_2, False)
+    got_near = [swapped(value, False) for value in near]
+    pack_b = passed_on(pack_b)
     got_b = swapped(pack_b, True)
 
     count = jnp.where(s < subs - 1, counts[0], 0)
     info = jnp.stack([odd, even, count])
-    targets = jnp.concatenate(
-        [
-            pick(coarse_low[HALF:], coarse_up[:HALF]),
-            pick(coarse_low[:HALF], coarse_up[HALF:]),
-            pick(coarse_up[:HALF], coarse_low[HALF:]),
-        ]
-    )
-    held = jnp.where((s > 0) & (s < subs - 1), 0, -1) * jnp.ones((HALF,), I32)
-    owned = jnp.pad(jnp.concatenate([targets, held]), (0, COLS - ROWS)).astype(F32)[None]
-    owned = passed_on(owned)
-
-    x_e, flux_e, theirs_e, own_m, own_r = solve_near(info, owned, blocks, got_1, got_2)
+
+    x_e, flux_e, theirs_e, own_m, own_r = solve_near(info, pack_b, blocks, got_near)
     back_e = swapped(x_e, False)
     back_flux = swapped(theirs_e, False)
     early = solve_far(own_m, own_r, got_a)

time: 62 us -> 61.9 us (level)
  waiting for transfers between devices: 9.2 us -> 10 us
  Pallas kernels: 22.7 us -> 22 us
    pallas_call x1, Pallas kernels: 2.18 us -> 3.11 us  [solve_far(): pl.pallas_call(far_kernel, in_specs=[VM] * 3, out_specs=[VM] * 4, out_sha...]
    pallas_call x2, Pallas kernels: 7.28 us -> 6.44 us  [the longest x1 6.42 us: solve_near(): pl.pallas_call(near_kernel, in_specs=[SM] + [ANY] * (5 + HALF), out_specs...]
    ppermute x7 -> x9, starting transfers between devices: 10.9 us -> 11.4 us  [swapped(): return lax.ppermute(value, SUB, pairs)]
  transfers between devices with their start and end apart: 9 -> 11, of which waited for: 3 -> 3; matrix products, arithmetic and copies ran while one was open for 0% -> 0% of each run, Pallas kernels for 34% -> 32%
where the time goes in v6:
time: 61.9 us; the launch traced here: 61.5 us
  starting transfers between devices  28 us (45%)
  Pallas kernels  22 us (36%)
  waiting for transfers between devices  10 us (16%)
  between operations  1.42 us (2%)
    all_to_all x1, starting transfers between devices, shards(): arrived = lax.all_to_all(parcels, near_axes, 0, 0, tiled=True)  11.8 us
    ppermute x9, starting transfers between devices, swapped(): return lax.ppermute(value, SUB, pairs)  11.4 us
    pallas_call x1, Pallas kernels, solve_near(): pl.pallas_call(near_kernel, in_specs=[SM] + [ANY] * (5 + HALF), out_specs...  6.42 us
    all_to_all x1, waiting for transfers between devices, shards(): arrived = lax.all_to_all(parcels, near_axes, 0, 0, tiled=True)  6.06 us
    all_to_all x1, starting transfers between devices, shards(): sums = lax.all_to_all(sums, far_axes, 0, 0, tiled=True)  4.83 us
    pallas_call x2, Pallas kernels, pack(): pl.pallas_call(functools.partial(pack_kernel, plans), in_specs=[ANY] * 4...  4.18 us
    pallas_call x1, Pallas kernels, solve_far(): pl.pallas_call(far_kernel, in_specs=[VM] * 3, out_specs=[VM] * 4, out_sha...  3.11 us
    all_to_all x1, waiting for transfers between devices, shards(): sums = lax.all_to_all(sums, far_axes, 0, 0, tiled=True)  2.92 us
  transfers between devices with their start and end apart: 11, of which 3 were waited for; matrix products, arithmetic and copies ran while one was open for 0% of the time, Pallas kernels for 32%

profile of v6, /device:TPU:1, one launch (start us, length us, event | category | flops | bytes accessed | tf_op | source)
XLA Modules:
  0.0 61.5 jit_solution(15234021242359175162)
XLA Ops:
  0.6 1.5 %shard_map.94.refs_7_ = bf16[1152,512]{1,0:T(8,128)(2,1)S(1)} custom-call(bf16[8,384,384]{2,1,0:T(8,128)(2,1)} %su.1, bf16[8,384,384]{2,1,0:T(8,128)(2,1)} %sl.1, bf16[8,384,128]{2,1,0:T(8,128)(2,1)} %ru.1, bf16[8,384,128]{2,1,0:T(8,128)(2,1)} %rl.1), custom_call_target="tpu_custom_call" | custom-call | flops 1000 | bytes 1000 | tf_op jit(solution)/shard_map/pallas_call | solution.py:119
  2.1 4.6 %collective-permute-start.5 = (bf16[1152,512]{1,0:T(8,128)(2,1)S(1)}, bf16[1152,512]{1,0:T(8,128)(2,1)S(1)}, u32[]{:S(2)}, u32[]{:S(2)}) collective-permute-start(bf16[1152,512]{1,0:T(8,128)(2,1)S(1)} %shard_map.94.refs_7_), channel_id=1, source_target_pairs={{4,8},{8,4},{12,16},{16,12},{20,24},{24,20},{28,32},{32,28},{36,40... | collective-permute-start | bytes 3538952 | tf_op jit(solution)/shard_map/ppermute | solution.py:50
  7.4 2.7 %shard_map.95 = (bf16[400,512]{1,0:T(8,128)(2,1)S(1)}, bf16[384,512]{1,0:T(8,128)(2,1)}, bf16[384,512]{1,0:T(8,128)(2,1)}, bf16[384,512]{1,0:T(8,128)(2,1)}, bf1...) custom-call(bf16[8,384,384]{2,1,0:T(8,128)(2,1)} %su.1, bf16[8,384,384]{2,1,0:T(8,128)(2,1)} %sl.1, ...), custom_call_target="tpu_custom_call" | custom-call | flops 1000 | bytes 1000 | tf_op jit(solution)/shard_map/pallas_call | solution.py:119
  10.1 0.1 collective-permute-start.1
  10.2 0.5 collective-permute-start
  10.7 0.1 collective-permute-start.2
  10.8 0.4 collective-permute-start.3
  11.2 1.0 %collective-permute-done.1.refs_1_ = bf16[384,512]{1,0:T(8,128)(2,1)} collective-permute-done((bf16[384,512]{1,0:T(8,128)(2,1)}, bf16[384,512]{1,0:T(8,128)(2,1)}, u32[]{:S(2)}, u32[]{:S(2)}) %collective-permute-start.1) | collective-permute-done | bytes 393248 | tf_op jit(solution)/shard_map/ppermute | solution.py:50
  12.2 3.2 %collective-permute-start.4 = (bf16[416,512]{1,0:T(8,128)(2,1)S(1)}, bf16[416,512]{1,0:T(8,128)(2,1)S(1)}, u32[]{:S(2)}, u32[]{:S(2)}) collective-permute-start(bf16[416,512]{1,0:T(8,128)(2,1)S(1)} %shard_map.96.after), channel_id=1, source_target_pairs={{4,8},{8,4},{12,16},{16,12},{20,24},{24,20},{28,32},{32,28},{36,40... | collective-permute-start | bytes 1277960 | tf_op jit(solution)/shard_map/ppermute | solution.py:50
  15.5 6.4 %shard_map.97 = (f32[1536,128]{1,0:T(8,128)S(1)}, f32[8,128]{1,0:T(8,128)S(1)}, f32[8,128]{1,0:T(8,128)S(1)}, bf16[4,384,384]{2,1,0:T(8,128)(2,1)S(1)}, bf16[4,384,128]{2,1,0:T(8,128)(2,1)S(1)}) custom-call(s32[3]{0:T(128)S(1)} %pad_add_fusion.info, bf16[416,512]{1,0:T(8,128)(2,1)S(1)} %shard_map.96.after, bf16[8,384,384]{2,1,0:T(8,128)(2,1)} %su.1, ...), custom_call_target="tpu_custom_call" | custom-call | flops 1000 | bytes 1000 | tf_op jit(solution)/shard_map/pallas_call | solution.py:368
  22.0 0.1 collective-permute-start.8
  22.1 0.5 collective-permute-start.6
  22.6 3.1 %shard_map.98 = (f32[1152,128]{1,0:T(8,128)S(1)}, s16[1152,128]{1,0:T(8,128)(2,1)S(1)}, s32[16,128]{1,0:T(8,128)S(1)}, f32[8,128]{1,0:T(8,128)S(1)}) custom-call(bf16[4,384,384]{2,1,0:T(8,128)(2,1)S(1)} %get-tuple-element.30.m, bf16[4,384,128]{2,1,0:T(8,128)(2,1)S(1)} %get-tuple-element.31.r, bf16[1152,512]{1,0:T(8,128)(2,1)S(1)} %collective-permute-done.5.got), custom_call_target="tpu_custom_call" | custom-call | flops 1000 | bytes 1000 | tf_op jit(solution)/shard_map/pallas_call | solution.py:385
  25.7 2.3 %shard_map.99 = (f32[1536,128]{1,0:T(8,128)S(1)}, s16[1552,128]{1,0:T(8,128)(2,1)S(1)}, f32[8,128]{1,0:T(8,128)S(1)}) custom-call(s32[3]{0:T(128)S(1)} %pad_add_fusion.info, bf16[4,384,384]{2,1,0:T(8,128)(2,1)S(1)} %get-tuple-element.30.m, bf16[4,384,128]{2,1,0:T(8,128)(2,1)S(1)} %get-tuple-element.31.r, bf16[416,512]{1,0:T(8,128)(2,1)S(1)} %collective-permute-done.4.got, ...), custom_call_target="tpu_custom_call" | custom-call | flops 1000 | bytes 1000 | tf_op jit(solution)/shard_map/pallas_call | solution.py:401
  28.0 0.8 %shard_map.102 = s32[16,1,1152]{2,1,0:T(1,128)} custom-call(f32[1,128]{1,0:T(1,128)S(1)} %get-tuple-element.44.owned, f32[8,128]{1,0:T(8,128)S(1)} %get-tuple-element.45.flux_e, f32[8,128]{1,0:T(8,128)S(1)} %collective-permute-done.6.after.back_e, f32[8,128]{1,0:T(8,128)S(1)} %get-tuple-element.46.flux_o, bf16[416,512]{1,0:T(8,128)(2,1)S(1)} %collective-permute-done.4.got), custom_call_target="tpu_custom_call" | custom-call | flops 1000 | bytes 1000 | tf_op jit(solution)/shard_map/pallas_call | solution.py:475
  28.8 11.8 %all-to-all-start = ((s32[16,1,1152]{2,1,0:T(1,128)}), s32[16,1,1152]{2,1,0:T(1,128)S(1)}, u32[]{:S(2)}, u32[]{:S(2)}) async-start(s32[16,1,1152]{2,1,0:T(1,128)} %shard_map.102), calls=%async_computation | async-start | bytes 147456 | tf_op jit(solution)/shard_map/all_to_all | solution.py:603
  40.6 1.9 %collective-permute-start.7 = (s16[1552,128]{1,0:T(8,128)(2,1)S(1)}, s16[1552,128]{1,0:T(8,128)(2,1)S(1)}, u32[]{:S(2)}, u32[]{:S(2)}) collective-permute-start(s16[1552,128]{1,0:T(8,128)(2,1)S(1)} %get-tuple-element.37), channel_id=1, source_target_pairs={{4,8},{8,4},{12,16},{16,12},{20,24},{24,20},{28,32},{32,28},{36,40... | collective-permute-start | bytes 1191944 | tf_op jit(solution)/shard_map/ppermute | solution.py:50
  42.5 6.1 %all-to-all-done = s32[16,1,1152]{2,1,0:T(1,128)S(1)} async-done(((s32[16,1,1152]{2,1,0:T(1,128)}), s32[16,1,1152]{2,1,0:T(1,128)S(1)}, u32[]{:S(2)}, u32[]{:S(2)}) %all-to-all-start) | async-done | bytes 73760 | tf_op jit(solution)/shard_map/all_to_all | solution.py:603
  48.6 1.0 %shard_map.103 = f32[16,8,128]{2,1,0:T(8,128)} custom-call(s32[144,128]{1,0:T(8,128)S(1)} %bitcast.8), custom_call_target="tpu_custom_call" | custom-call | flops 3000000000 | bytes 30000000 | tf_op jit(solution)/shard_map/pallas_call | solution.py:508
  49.5 4.8 %all-to-all-start.1 = ((f32[16,8,128]{2,1,0:T(8,128)}), f32[16,8,128]{2,1,0:T(8,128)S(1)}, u32[]{:S(2)}, u32[]{:S(2)}) async-start(f32[16,8,128]{2,1,0:T(8,128)} %shard_map.103), calls=%async_computation.1 | async-start | bytes 131072 | tf_op jit(solution)/shard_map/all_to_all | solution.py:605
  54.4 2.6 %shard_map.100 = (f32[8,384,128]{2,1,0:T(8,128)}, f32[8,384,128]{2,1,0:T(8,128)}) custom-call(f32[1536,128]{1,0:T(8,128)S(1)} %get-tuple-element.38.x_e, f32[1536,128]{1,0:T(8,128)} %collective-permute-done.8.back_e, f32[1536,128]{1,0:T(8,128)S(1)} %get-tuple-element.39.x_o), custom_call_target="tpu_custom_call" | custom-call | flops 3000000000 | bytes 30000000 | tf_op jit(solution)/shard_map/pallas_call | solution.py:444
  57.0 0.9 %shard_map.101 = (f32[8,384,128]{2,1,0:T(8,128)}, f32[8,384,128]{2,1,0:T(8,128)}) custom-call(s16[1552,128]{1,0:T(8,128)(2,1)S(1)} %collective-permute-done.7.back_o, f32[8,384,128]{2,1,0:T(8,128)} %get-tuple-element.40.up_in, f32[8,384,128]{2,1,0:T(8,128)} %get-tuple-element.41.low_in), custom_call_target="tpu_custom_call", output_to_operand_aliasing={{0}: (1, {}), {1}: (2, {})} | custom-call | flops 1000 | bytes 1000 | tf_op jit(solution)/shard_map/pallas_call | solution.py:540
  58.0 2.9 %all-to-all-done.1.arrived = f32[16,8,128]{2,1,0:T(8,128)S(1)} async-done(((f32[16,8,128]{2,1,0:T(8,128)}), f32[16,8,128]{2,1,0:T(8,128)S(1)}, u32[]{:S(2)}, u32[]{:S(2)}) %all-to-all-start.1) | async-done | bytes 65568 | tf_op jit(solution)/shard_map/all_to_all | solution.py:605
  60.9 0.6 shard_map.104
  (10 shorter events, 0.1 us)
Async XLA Ops:
  2.1 20.5 %collective-permute-start.5 = (bf16[1152,512]{1,0:T(8,128)(2,1)S(1)}, bf16[1152,512]{1,0:T(8,128)(2,1)S(1)}, u32[]{:S(2)}, u32[]{:S(2)}) collective-permute-start(bf16[1152,512]{1,0:T(8,128)(2,1)S(1)} %shard_map.94.refs_7_), channel_id=1, source_target_pairs={{4,8},{8,4},{12,16},{16,12},{20,24},{24,20},{28,32},{32,28},{36,40... | collective-permute-start | bytes 3538952 | tf_op jit(solution)/shard_map/ppermute | solution.py:50
  10.1 2.2 %collective-permute-start.1 = (bf16[384,512]{1,0:T(8,128)(2,1)}, bf16[384,512]{1,0:T(8,128)(2,1)}, u32[]{:S(2)}, u32[]{:S(2)}) collective-permute-start(bf16[384,512]{1,0:T(8,128)(2,1)} %get-tuple-element.27), channel_id=1, source_target_pairs={{0,4},{4,0},{8,12},{12,8},{16,20},{20,16},{24,28},{28,24},{32,36},... | collective-permute-start | bytes 1179656 | tf_op jit(solution)/shard_map/ppermute | solution.py:50
  10.2 5.4 %collective-permute-start = (bf16[400,512]{1,0:T(8,128)(2,1)S(1)}, bf16[400,512]{1,0:T(8,128)(2,1)}, u32[]{:S(2)}, u32[]{:S(2)}) collective-permute-start(bf16[400,512]{1,0:T(8,128)(2,1)S(1)} %get-tuple-element.26), channel_id=1, source_target_pairs={{0,4},{4,0},{8,12},{12,8},{16,20},{20,16},{24,28},{28,24},{32,36},... | collective-permute-start | bytes 1228808 | tf_op jit(solution)/shard_map/ppermute | solution.py:50
  10.7 4.9 %collective-permute-start.2 = (bf16[384,512]{1,0:T(8,128)(2,1)}, bf16[384,512]{1,0:T(8,128)(2,1)}, u32[]{:S(2)}, u32[]{:S(2)}) collective-permute-start(bf16[384,512]{1,0:T(8,128)(2,1)} %get-tuple-element.28), channel_id=1, source_target_pairs={{0,4},{4,0},{8,12},{12,8},{16,20},{20,16},{24,28},{28,24},{32,36},... | collective-permute-start | bytes 1179656 | tf_op jit(solution)/shard_map/ppermute | solution.py:50
  10.8 4.8 %collective-permute-start.3 = (bf16[384,512]{1,0:T(8,128)(2,1)}, bf16[384,512]{1,0:T(8,128)(2,1)}, u32[]{:S(2)}, u32[]{:S(2)}) collective-permute-start(bf16[384,512]{1,0:T(8,128)(2,1)} %get-tuple-element.29), channel_id=1, source_target_pairs={{0,4},{4,0},{8,12},{12,8},{16,20},{20,16},{24,28},{28,24},{32,36},... | collective-permute-start | bytes 1179656 | tf_op jit(solution)/shard_map/ppermute | solution.py:50
  12.2 13.5 %collective-permute-start.4 = (bf16[416,512]{1,0:T(8,128)(2,1)S(1)}, bf16[416,512]{1,0:T(8,128)(2,1)S(1)}, u32[]{:S(2)}, u32[]{:S(2)}) collective-permute-start(bf16[416,512]{1,0:T(8,128)(2,1)S(1)} %shard_map.96.after), channel_id=1, source_target_pairs={{4,8},{8,4},{12,16},{16,12},{20,24},{24,20},{28,32},{32,28},{36,40... | collective-permute-start | bytes 1277960 | tf_op jit(solution)/shard_map/ppermute | solution.py:50
  22.0 32.4 %collective-permute-start.8 = (f32[1536,128]{1,0:T(8,128)S(1)}, f32[1536,128]{1,0:T(8,128)}, u32[]{:S(2)}, u32[]{:S(2)}) collective-permute-start(f32[1536,128]{1,0:T(8,128)S(1)} %get-tuple-element.38.x_e), channel_id=1, source_target_pairs={{0,4},{4,0},{8,12},{12,8},{16,20},{20,16},{24,28},{28,24},{32,36},... | collective-permute-start | bytes 2359304 | tf_op jit(solution)/shard_map/ppermute | solution.py:50
  22.1 3.6 %collective-permute-start.6 = (f32[8,128]{1,0:T(8,128)S(1)}, f32[8,128]{1,0:T(8,128)S(1)}, u32[]{:S(2)}, u32[]{:S(2)}) collective-permute-start(f32[8,128]{1,0:T(8,128)S(1)} %get-tuple-element.36), channel_id=1, source_target_pairs={{0,4},{4,0},{8,12},{12,8},{16,20},{20,16},{24,28},{28,24},{32,36},... | collective-permute-start | bytes 12296 | tf_op jit(solution)/shard_map/ppermute | solution.py:50
  28.8 19.7 %all-to-all-start = ((s32[16,1,1152]{2,1,0:T(1,128)}), s32[16,1,1152]{2,1,0:T(1,128)S(1)}, u32[]{:S(2)}, u32[]{:S(2)}) async-start(s32[16,1,1152]{2,1,0:T(1,128)} %shard_map.102), calls=%async_computation | async-start | bytes 147456 | tf_op jit(solution)/shard_map/all_to_all | solution.py:603
  40.6 16.4 %collective-permute-start.7 = (s16[1552,128]{1,0:T(8,128)(2,1)S(1)}, s16[1552,128]{1,0:T(8,128)(2,1)S(1)}, u32[]{:S(2)}, u32[]{:S(2)}) collective-permute-start(s16[1552,128]{1,0:T(8,128)(2,1)S(1)} %get-tuple-element.37), channel_id=1, source_target_pairs={{4,8},{8,4},{12,16},{16,12},{20,24},{24,20},{28,32},{32,28},{36,40... | collective-permute-start | bytes 1191944 | tf_op jit(solution)/shard_map/ppermute | solution.py:50
  49.5 11.4 %all-to-all-start.1 = ((f32[16,8,128]{2,1,0:T(8,128)}), f32[16,8,128]{2,1,0:T(8,128)S(1)}, u32[]{:S(2)}, u32[]{:S(2)}) async-start(f32[16,8,128]{2,1,0:T(8,128)} %shard_map.103), calls=%async_computation.1 | async-start | bytes 131072 | tf_op jit(solution)/shard_map/all_to_all | solution.py:605

commit v7 on v6

--- a/solution.py
+++ b/solution.py
@@ -280,7 +280,7 @@
 
 
 def coded(value, step):
-    return jnp.clip(jnp.round(value / step), -32767.0, 32767.0).astype(I32)
+    return jnp.clip(jnp.round(value * (1.0 / step)), -32767.0, 32767.0).astype(I32)
 
 
 def solve_all(first, count, m, r, got):
@@ -578,7 +578,7 @@
     got_a = swapped(pack_a, True)
     *near, pack_b, owned = pack(
         [(k, 1, False, 1 if k == 0 else 0) for k in range(HALF)]
-        + [(EARLY, HALF - EARLY, True, 2)],
+        + [(EARLY, HALF - EARLY, True, 1)],
         blocks,
         (counts, coarse_up, coarse_low),
         (pack_a,),

time: 61.9 us -> 61.7 us (level)
  no operation moved by 1% of the time
where the time goes in v7:
time: 61.7 us; the launch traced here: 61.3 us
  starting transfers between devices  27.8 us (45%)
  Pallas kernels  22 us (36%)
  waiting for transfers between devices  10 us (16%)
  between operations  1.42 us (2%)
    all_to_all x1, starting transfers between devices, shards(): arrived = lax.all_to_all(parcels, near_axes, 0, 0, tiled=True)  11.6 us
    ppermute x9, starting transfers between devices, swapped(): return lax.ppermute(value, SUB, pairs)  11.4 us
    pallas_call x1, Pallas kernels, solve_near(): pl.pallas_call(near_kernel, in_specs=[SM] + [ANY] * (5 + HALF), out_specs...  6.42 us
    all_to_all x1, waiting for transfers between devices, shards(): arrived = lax.all_to_all(parcels, near_axes, 0, 0, tiled=True)  6.06 us
    all_to_all x1, starting transfers between devices, shards(): sums = lax.all_to_all(sums, far_axes, 0, 0, tiled=True)  4.84 us
    pallas_call x2, Pallas kernels, pack(): pl.pallas_call(functools.partial(pack_kernel, plans), in_specs=[ANY] * 4...  4.18 us
    pallas_call x1, Pallas kernels, solve_far(): pl.pallas_call(far_kernel, in_specs=[VM] * 3, out_specs=[VM] * 4, out_sha...  3.11 us
    all_to_all x1, waiting for transfers between devices, shards(): sums = lax.all_to_all(sums, far_axes, 0, 0, tiled=True)  2.92 us
  transfers between devices with their start and end apart: 11, of which 3 were waited for; matrix products, arithmetic and copies ran while one was open for 0% of the time, Pallas kernels for 32%

profile of v7, /device:TPU:1, one launch (start us, length us, event | category | flops | bytes accessed | tf_op | source)
XLA Modules:
  0.0 61.3 jit_solution(4129681249953856148)
XLA Ops:
  0.6 1.5 %shard_map.94.refs_7_ = bf16[1152,512]{1,0:T(8,128)(2,1)S(1)} custom-call(bf16[8,384,384]{2,1,0:T(8,128)(2,1)} %su.1, bf16[8,384,384]{2,1,0:T(8,128)(2,1)} %sl.1, bf16[8,384,128]{2,1,0:T(8,128)(2,1)} %ru.1, bf16[8,384,128]{2,1,0:T(8,128)(2,1)} %rl.1), custom_call_target="tpu_custom_call" | custom-call | flops 1000 | bytes 1000 | tf_op jit(solution)/shard_map/pallas_call | solution.py:119
  2.1 4.6 %collective-permute-start.5 = (bf16[1152,512]{1,0:T(8,128)(2,1)S(1)}, bf16[1152,512]{1,0:T(8,128)(2,1)S(1)}, u32[]{:S(2)}, u32[]{:S(2)}) collective-permute-start(bf16[1152,512]{1,0:T(8,128)(2,1)S(1)} %shard_map.94.refs_7_), channel_id=1, source_target_pairs={{4,8},{8,4},{12,16},{16,12},{20,24},{24,20},{28,32},{32,28},{36,40... | collective-permute-start | bytes 3538952 | tf_op jit(solution)/shard_map/ppermute | solution.py:50
  7.4 2.7 %shard_map.95 = (bf16[400,512]{1,0:T(8,128)(2,1)S(1)}, bf16[384,512]{1,0:T(8,128)(2,1)}, bf16[384,512]{1,0:T(8,128)(2,1)}, bf16[384,512]{1,0:T(8,128)(2,1)}, bf1...) custom-call(bf16[8,384,384]{2,1,0:T(8,128)(2,1)} %su.1, bf16[8,384,384]{2,1,0:T(8,128)(2,1)} %sl.1, ...), custom_call_target="tpu_custom_call" | custom-call | flops 1000 | bytes 1000 | tf_op jit(solution)/shard_map/pallas_call | solution.py:119
  10.1 0.1 collective-permute-start.1
  10.2 0.5 collective-permute-start
  10.7 0.1 collective-permute-start.2
  10.8 0.4 collective-permute-start.3
  11.2 1.0 %collective-permute-done.1.refs_1_ = bf16[384,512]{1,0:T(8,128)(2,1)} collective-permute-done((bf16[384,512]{1,0:T(8,128)(2,1)}, bf16[384,512]{1,0:T(8,128)(2,1)}, u32[]{:S(2)}, u32[]{:S(2)}) %collective-permute-start.1) | collective-permute-done | bytes 393248 | tf_op jit(solution)/shard_map/ppermute | solution.py:50
  12.2 3.2 %collective-permute-start.4 = (bf16[400,512]{1,0:T(8,128)(2,1)S(1)}, bf16[400,512]{1,0:T(8,128)(2,1)S(1)}, u32[]{:S(2)}, u32[]{:S(2)}) collective-permute-start(bf16[400,512]{1,0:T(8,128)(2,1)S(1)} %shard_map.96.after), channel_id=1, source_target_pairs={{4,8},{8,4},{12,16},{16,12},{20,24},{24,20},{28,32},{32,28},{36,40... | collective-permute-start | bytes 1228808 | tf_op jit(solution)/shard_map/ppermute | solution.py:50
  15.5 6.4 %shard_map.97 = (f32[1536,128]{1,0:T(8,128)S(1)}, f32[8,128]{1,0:T(8,128)S(1)}, f32[8,128]{1,0:T(8,128)S(1)}, bf16[4,384,384]{2,1,0:T(8,128)(2,1)S(1)}, bf16[4,384,128]{2,1,0:T(8,128)(2,1)S(1)}) custom-call(s32[3]{0:T(128)S(1)} %pad_add_fusion.info, bf16[400,512]{1,0:T(8,128)(2,1)S(1)} %shard_map.96.after, bf16[8,384,384]{2,1,0:T(8,128)(2,1)} %su.1, ...), custom_call_target="tpu_custom_call" | custom-call | flops 1000 | bytes 1000 | tf_op jit(solution)/shard_map/pallas_call | solution.py:368
  22.0 0.1 collective-permute-start.8
  22.1 0.5 collective-permute-start.6
  22.6 3.1 %shard_map.98 = (f32[1152,128]{1,0:T(8,128)S(1)}, s16[1152,128]{1,0:T(8,128)(2,1)S(1)}, s32[16,128]{1,0:T(8,128)S(1)}, f32[8,128]{1,0:T(8,128)S(1)}) custom-call(bf16[4,384,384]{2,1,0:T(8,128)(2,1)S(1)} %get-tuple-element.30.m, bf16[4,384,128]{2,1,0:T(8,128)(2,1)S(1)} %get-tuple-element.31.r, bf16[1152,512]{1,0:T(8,128)(2,1)S(1)} %collective-permute-done.5.got), custom_call_target="tpu_custom_call" | custom-call | flops 1000 | bytes 1000 | tf_op jit(solution)/shard_map/pallas_call | solution.py:385
  25.7 2.3 %shard_map.99 = (f32[1536,128]{1,0:T(8,128)S(1)}, s16[1552,128]{1,0:T(8,128)(2,1)S(1)}, f32[8,128]{1,0:T(8,128)S(1)}) custom-call(s32[3]{0:T(128)S(1)} %pad_add_fusion.info, bf16[4,384,384]{2,1,0:T(8,128)(2,1)S(1)} %get-tuple-element.30.m, bf16[4,384,128]{2,1,0:T(8,128)(2,1)S(1)} %get-tuple-element.31.r, bf16[400,512]{1,0:T(8,128)(2,1)S(1)} %collective-permute-done.4.got, ...), custom_call_target="tpu_custom_call" | custom-call | flops 1000 | bytes 1000 | tf_op jit(solution)/shard_map/pallas_call | solution.py:401
  28.0 0.8 %shard_map.102 = s32[16,1,1152]{2,1,0:T(1,128)} custom-call(f32[1,128]{1,0:T(1,128)S(1)} %get-tuple-element.44.owned, f32[8,128]{1,0:T(8,128)S(1)} %get-tuple-element.45.flux_e, f32[8,128]{1,0:T(8,128)S(1)} %collective-permute-done.6.after.back_e, f32[8,128]{1,0:T(8,128)S(1)} %get-tuple-element.46.flux_o, bf16[400,512]{1,0:T(8,128)(2,1)S(1)} %collective-permute-done.4.got), custom_call_target="tpu_custom_call" | custom-call | flops 1000 | bytes 1000 | tf_op jit(solution)/shard_map/pallas_call | solution.py:475
  28.8 11.6 %all-to-all-start = ((s32[16,1,1152]{2,1,0:T(1,128)}), s32[16,1,1152]{2,1,0:T(1,128)S(1)}, u32[]{:S(2)}, u32[]{:S(2)}) async-start(s32[16,1,1152]{2,1,0:T(1,128)} %shard_map.102), calls=%async_computation | async-start | bytes 147456 | tf_op jit(solution)/shard_map/all_to_all | solution.py:603
  40.4 1.9 %collective-permute-start.7 = (s16[1552,128]{1,0:T(8,128)(2,1)S(1)}, s16[1552,128]{1,0:T(8,128)(2,1)S(1)}, u32[]{:S(2)}, u32[]{:S(2)}) collective-permute-start(s16[1552,128]{1,0:T(8,128)(2,1)S(1)} %get-tuple-element.37), channel_id=1, source_target_pairs={{4,8},{8,4},{12,16},{16,12},{20,24},{24,20},{28,32},{32,28},{36,40... | collective-permute-start | bytes 1191944 | tf_op jit(solution)/shard_map/ppermute | solution.py:50
  42.3 6.1 %all-to-all-done = s32[16,1,1152]{2,1,0:T(1,128)S(1)} async-done(((s32[16,1,1152]{2,1,0:T(1,128)}), s32[16,1,1152]{2,1,0:T(1,128)S(1)}, u32[]{:S(2)}, u32[]{:S(2)}) %all-to-all-start) | async-done | bytes 73760 | tf_op jit(solution)/shard_map/all_to_all | solution.py:603
  48.4 1.0 %shard_map.103 = f32[16,8,128]{2,1,0:T(8,128)} custom-call(s32[144,128]{1,0:T(8,128)S(1)} %bitcast.8), custom_call_target="tpu_custom_call" | custom-call | flops 3000000000 | bytes 30000000 | tf_op jit(solution)/shard_map/pallas_call | solution.py:508
  49.3 4.8 %all-to-all-start.1 = ((f32[16,8,128]{2,1,0:T(8,128)}), f32[16,8,128]{2,1,0:T(8,128)S(1)}, u32[]{:S(2)}, u32[]{:S(2)}) async-start(f32[16,8,128]{2,1,0:T(8,128)} %shard_map.103), calls=%async_computation.1 | async-start | bytes 131072 | tf_op jit(solution)/shard_map/all_to_all | solution.py:605
  54.2 2.6 %shard_map.100 = (f32[8,384,128]{2,1,0:T(8,128)}, f32[8,384,128]{2,1,0:T(8,128)}) custom-call(f32[1536,128]{1,0:T(8,128)S(1)} %get-tuple-element.38.x_e, f32[1536,128]{1,0:T(8,128)} %collective-permute-done.8.back_e, f32[1536,128]{1,0:T(8,128)S(1)} %get-tuple-element.39.x_o), custom_call_target="tpu_custom_call" | custom-call | flops 3000000000 | bytes 30000000 | tf_op jit(solution)/shard_map/pallas_call | solution.py:444
  56.8 0.9 %shard_map.101 = (f32[8,384,128]{2,1,0:T(8,128)}, f32[8,384,128]{2,1,0:T(8,128)}) custom-call(s16[1552,128]{1,0:T(8,128)(2,1)S(1)} %collective-permute-done.7.back_o, f32[8,384,128]{2,1,0:T(8,128)} %get-tuple-element.40.up_in, f32[8,384,128]{2,1,0:T(8,128)} %get-tuple-element.41.low_in), custom_call_target="tpu_custom_call", output_to_operand_aliasing={{0}: (1, {}), {1}: (2, {})} | custom-call | flops 1000 | bytes 1000 | tf_op jit(solution)/shard_map/pallas_call | solution.py:540
  57.8 2.9 %all-to-all-done.1.arrived = f32[16,8,128]{2,1,0:T(8,128)S(1)} async-done(((f32[16,8,128]{2,1,0:T(8,128)}), f32[16,8,128]{2,1,0:T(8,128)S(1)}, u32[]{:S(2)}, u32[]{:S(2)}) %all-to-all-start.1) | async-done | bytes 65568 | tf_op jit(solution)/shard_map/all_to_all | solution.py:605
  60.7 0.6 shard_map.104
  (10 shorter events, 0.1 us)
Async XLA Ops:
  2.1 20.5 %collective-permute-start.5 = (bf16[1152,512]{1,0:T(8,128)(2,1)S(1)}, bf16[1152,512]{1,0:T(8,128)(2,1)S(1)}, u32[]{:S(2)}, u32[]{:S(2)}) collective-permute-start(bf16[1152,512]{1,0:T(8,128)(2,1)S(1)} %shard_map.94.refs_7_), channel_id=1, source_target_pairs={{4,8},{8,4},{12,16},{16,12},{20,24},{24,20},{28,32},{32,28},{36,40... | collective-permute-start | bytes 3538952 | tf_op jit(solution)/shard_map/ppermute | solution.py:50
  10.1 2.2 %collective-permute-start.1 = (bf16[384,512]{1,0:T(8,128)(2,1)}, bf16[384,512]{1,0:T(8,128)(2,1)}, u32[]{:S(2)}, u32[]{:S(2)}) collective-permute-start(bf16[384,512]{1,0:T(8,128)(2,1)} %get-tuple-element.27), channel_id=1, source_target_pairs={{0,4},{4,0},{8,12},{12,8},{16,20},{20,16},{24,28},{28,24},{32,36},... | collective-permute-start | bytes 1179656 | tf_op jit(solution)/shard_map/ppermute | solution.py:50
  10.2 5.4 %collective-permute-start = (bf16[400,512]{1,0:T(8,128)(2,1)S(1)}, bf16[400,512]{1,0:T(8,128)(2,1)}, u32[]{:S(2)}, u32[]{:S(2)}) collective-permute-start(bf16[400,512]{1,0:T(8,128)(2,1)S(1)} %get-tuple-element.26), channel_id=1, source_target_pairs={{0,4},{4,0},{8,12},{12,8},{16,20},{20,16},{24,28},{28,24},{32,36},... | collective-permute-start | bytes 1228808 | tf_op jit(solution)/shard_map/ppermute | solution.py:50
  10.7 4.9 %collective-permute-start.2 = (bf16[384,512]{1,0:T(8,128)(2,1)}, bf16[384,512]{1,0:T(8,128)(2,1)}, u32[]{:S(2)}, u32[]{:S(2)}) collective-permute-start(bf16[384,512]{1,0:T(8,128)(2,1)} %get-tuple-element.28), channel_id=1, source_target_pairs={{0,4},{4,0},{8,12},{12,8},{16,20},{20,16},{24,28},{28,24},{32,36},... | collective-permute-start | bytes 1179656 | tf_op jit(solution)/shard_map/ppermute | solution.py:50
  10.8 4.8 %collective-permute-start.3 = (bf16[384,512]{1,0:T(8,128)(2,1)}, bf16[384,512]{1,0:T(8,128)(2,1)}, u32[]{:S(2)}, u32[]{:S(2)}) collective-permute-start(bf16[384,512]{1,0:T(8,128)(2,1)} %get-tuple-element.29), channel_id=1, source_target_pairs={{0,4},{4,0},{8,12},{12,8},{16,20},{20,16},{24,28},{28,24},{32,36},... | collective-permute-start | bytes 1179656 | tf_op jit(solution)/shard_map/ppermute | solution.py:50
  12.2 13.5 %collective-permute-start.4 = (bf16[400,512]{1,0:T(8,128)(2,1)S(1)}, bf16[400,512]{1,0:T(8,128)(2,1)S(1)}, u32[]{:S(2)}, u32[]{:S(2)}) collective-permute-start(bf16[400,512]{1,0:T(8,128)(2,1)S(1)} %shard_map.96.after), channel_id=1, source_target_pairs={{4,8},{8,4},{12,16},{16,12},{20,24},{24,20},{28,32},{32,28},{36,40... | collective-permute-start | bytes 1228808 | tf_op jit(solution)/shard_map/ppermute | solution.py:50
  22.0 32.2 %collective-permute-start.8 = (f32[1536,128]{1,0:T(8,128)S(1)}, f32[1536,128]{1,0:T(8,128)}, u32[]{:S(2)}, u32[]{:S(2)}) collective-permute-start(f32[1536,128]{1,0:T(8,128)S(1)} %get-tuple-element.38.x_e), channel_id=1, source_target_pairs={{0,4},{4,0},{8,12},{12,8},{16,20},{20,16},{24,28},{28,24},{32,36},... | collective-permute-start | bytes 2359304 | tf_op jit(solution)/shard_map/ppermute | solution.py:50
  22.1 3.6 %collective-permute-start.6 = (f32[8,128]{1,0:T(8,128)S(1)}, f32[8,128]{1,0:T(8,128)S(1)}, u32[]{:S(2)}, u32[]{:S(2)}) collective-permute-start(f32[8,128]{1,0:T(8,128)S(1)} %get-tuple-element.36), channel_id=1, source_target_pairs={{0,4},{4,0},{8,12},{12,8},{16,20},{20,16},{24,28},{28,24},{32,36},... | collective-permute-start | bytes 12296 | tf_op jit(solution)/shard_map/ppermute | solution.py:50
  28.8 19.6 %all-to-all-start = ((s32[16,1,1152]{2,1,0:T(1,128)}), s32[16,1,1152]{2,1,0:T(1,128)S(1)}, u32[]{:S(2)}, u32[]{:S(2)}) async-start(s32[16,1,1152]{2,1,0:T(1,128)} %shard_map.102), calls=%async_computation | async-start | bytes 147456 | tf_op jit(solution)/shard_map/all_to_all | solution.py:603
  40.4 16.4 %collective-permute-start.7 = (s16[1552,128]{1,0:T(8,128)(2,1)S(1)}, s16[1552,128]{1,0:T(8,128)(2,1)S(1)}, u32[]{:S(2)}, u32[]{:S(2)}) collective-permute-start(s16[1552,128]{1,0:T(8,128)(2,1)S(1)} %get-tuple-element.37), channel_id=1, source_target_pairs={{4,8},{8,4},{12,16},{16,12},{20,24},{24,20},{28,32},{32,28},{36,40... | collective-permute-start | bytes 1191944 | tf_op jit(solution)/shard_map/ppermute | solution.py:50
  49.3 11.4 %all-to-all-start.1 = ((f32[16,8,128]{2,1,0:T(8,128)}), f32[16,8,128]{2,1,0:T(8,128)S(1)}, u32[]{:S(2)}, u32[]{:S(2)}) async-start(f32[16,8,128]{2,1,0:T(8,128)} %shard_map.103), calls=%async_computation.1 | async-start | bytes 131072 | tf_op jit(solution)/shard_map/all_to_all | solution.py:605

commit v8 on v7

--- a/solution.py
+++ b/solution.py
@@ -497,8 +497,9 @@
         target = jnp.broadcast_to(head[:, r : r + 1], (peers, COLS))
         chosen.append(jnp.where(target == wanted, 1.0, 0.0))
         pieces.append(codes[r].astype(F32) * step[:, ROWS + r : ROWS + r + 1])
-    chosen = jnp.concatenate(chosen, 0).T.astype(BF)
-    sums = mm(chosen, jnp.concatenate(split(jnp.concatenate(pieces, 0)), 1))
+    chosen = jnp.concatenate(chosen, 0).astype(BF)
+    parts = jnp.concatenate(split(jnp.concatenate(pieces, 0)), 1)
+    sums = lax.dot_general(chosen, parts, (((0,), (0,)), ((), ())), preferred_element_type=F32)
     sums = sums[:, :COLS] + sums[:, COLS:]
     for d in range(out.shape[0]):
         out[d] = sums[d * CO_DEV : (d + 1) * CO_DEV]

time: 61.7 us -> 61.7 us (level)
  no operation moved by 1% of the time
where the time goes in v8:
time: 61.7 us; the launch traced here: 61.3 us
  starting transfers between devices  27.8 us (45%)
  Pallas kernels  21.9 us (35%)
  waiting for transfers between devices  10 us (16%)
  between operations  1.42 us (2%)
    all_to_all x1, starting transfers between devices, shards(): arrived = lax.all_to_all(parcels, near_axes, 0, 0, tiled=True)  11.6 us
    ppermute x9, starting transfers between devices, swapped(): return lax.ppermute(value, SUB, pairs)  11.4 us
    pallas_call x1, Pallas kernels, solve_near(): pl.pallas_call(near_kernel, in_specs=[SM] + [ANY] * (5 + HALF), out_specs...  6.42 us
    all_to_all x1, waiting for transfers between devices, shards(): arrived = lax.all_to_all(parcels, near_axes, 0, 0, tiled=True)  6.06 us
    all_to_all x1, starting transfers between devices, shards(): sums = lax.all_to_all(sums, far_axes, 0, 0, tiled=True)  4.84 us
    pallas_call x2, Pallas kernels, pack(): pl.pallas_call(functools.partial(pack_kernel, plans), in_specs=[ANY] * 4...  4.18 us
    pallas_call x1, Pallas kernels, solve_far(): pl.pallas_call(far_kernel, in_specs=[VM] * 3, out_specs=[VM] * 4, out_sha...  3.11 us
    all_to_all x1, waiting for transfers between devices, shards(): sums = lax.all_to_all(sums, far_axes, 0, 0, tiled=True)  2.92 us
  transfers between devices with their start and end apart: 11, of which 3 were waited for; matrix products, arithmetic and copies ran while one was open for 0% of the time, Pallas kernels for 32%

profile of v8, /device:TPU:1, one launch (start us, length us, event | category | flops | bytes accessed | tf_op | source)
XLA Modules:
  0.0 61.3 jit_solution(12361884801263584)
XLA Ops:
  0.6 1.5 %shard_map.94.refs_7_ = bf16[1152,512]{1,0:T(8,128)(2,1)S(1)} custom-call(bf16[8,384,384]{2,1,0:T(8,128)(2,1)} %su.1, bf16[8,384,384]{2,1,0:T(8,128)(2,1)} %sl.1, bf16[8,384,128]{2,1,0:T(8,128)(2,1)} %ru.1, bf16[8,384,128]{2,1,0:T(8,128)(2,1)} %rl.1), custom_call_target="tpu_custom_call" | custom-call | flops 1000 | bytes 1000 | tf_op jit(solution)/shard_map/pallas_call | solution.py:119
  2.1 4.6 %collective-permute-start.5 = (bf16[1152,512]{1,0:T(8,128)(2,1)S(1)}, bf16[1152,512]{1,0:T(8,128)(2,1)S(1)}, u32[]{:S(2)}, u32[]{:S(2)}) collective-permute-start(bf16[1152,512]{1,0:T(8,128)(2,1)S(1)} %shard_map.94.refs_7_), channel_id=1, source_target_pairs={{4,8},{8,4},{12,16},{16,12},{20,24},{24,20},{28,32},{32,28},{36,40... | collective-permute-start | bytes 3538952 | tf_op jit(solution)/shard_map/ppermute | solution.py:50
  7.4 2.7 %shard_map.95 = (bf16[400,512]{1,0:T(8,128)(2,1)S(1)}, bf16[384,512]{1,0:T(8,128)(2,1)}, bf16[384,512]{1,0:T(8,128)(2,1)}, bf16[384,512]{1,0:T(8,128)(2,1)}, bf1...) custom-call(bf16[8,384,384]{2,1,0:T(8,128)(2,1)} %su.1, bf16[8,384,384]{2,1,0:T(8,128)(2,1)} %sl.1, ...), custom_call_target="tpu_custom_call" | custom-call | flops 1000 | bytes 1000 | tf_op jit(solution)/shard_map/pallas_call | solution.py:119
  10.1 0.1 collective-permute-start.1
  10.2 0.5 collective-permute-start
  10.7 0.1 collective-permute-start.2
  10.8 0.4 collective-permute-start.3
  11.2 1.0 %collective-permute-done.1.refs_1_ = bf16[384,512]{1,0:T(8,128)(2,1)} collective-permute-done((bf16[384,512]{1,0:T(8,128)(2,1)}, bf16[384,512]{1,0:T(8,128)(2,1)}, u32[]{:S(2)}, u32[]{:S(2)}) %collective-permute-start.1) | collective-permute-done | bytes 393248 | tf_op jit(solution)/shard_map/ppermute | solution.py:50
  12.2 3.2 %collective-permute-start.4 = (bf16[400,512]{1,0:T(8,128)(2,1)S(1)}, bf16[400,512]{1,0:T(8,128)(2,1)S(1)}, u32[]{:S(2)}, u32[]{:S(2)}) collective-permute-start(bf16[400,512]{1,0:T(8,128)(2,1)S(1)} %shard_map.96.after), channel_id=1, source_target_pairs={{4,8},{8,4},{12,16},{16,12},{20,24},{24,20},{28,32},{32,28},{36,40... | collective-permute-start | bytes 1228808 | tf_op jit(solution)/shard_map/ppermute | solution.py:50
  15.5 6.4 %shard_map.97 = (f32[1536,128]{1,0:T(8,128)S(1)}, f32[8,128]{1,0:T(8,128)S(1)}, f32[8,128]{1,0:T(8,128)S(1)}, bf16[4,384,384]{2,1,0:T(8,128)(2,1)S(1)}, bf16[4,384,128]{2,1,0:T(8,128)(2,1)S(1)}) custom-call(s32[3]{0:T(128)S(1)} %pad_add_fusion.info, bf16[400,512]{1,0:T(8,128)(2,1)S(1)} %shard_map.96.after, bf16[8,384,384]{2,1,0:T(8,128)(2,1)} %su.1, ...), custom_call_target="tpu_custom_call" | custom-call | flops 1000 | bytes 1000 | tf_op jit(solution)/shard_map/pallas_call | solution.py:368
  22.0 0.1 collective-permute-start.8
  22.1 0.5 collective-permute-start.6
  22.6 3.1 %shard_map.98 = (f32[1152,128]{1,0:T(8,128)S(1)}, s16[1152,128]{1,0:T(8,128)(2,1)S(1)}, s32[16,128]{1,0:T(8,128)S(1)}, f32[8,128]{1,0:T(8,128)S(1)}) custom-call(bf16[4,384,384]{2,1,0:T(8,128)(2,1)S(1)} %get-tuple-element.30.m, bf16[4,384,128]{2,1,0:T(8,128)(2,1)S(1)} %get-tuple-element.31.r, bf16[1152,512]{1,0:T(8,128)(2,1)S(1)} %collective-permute-done.5.got), custom_call_target="tpu_custom_call" | custom-call | flops 1000 | bytes 1000 | tf_op jit(solution)/shard_map/pallas_call | solution.py:385
  25.7 2.3 %shard_map.99 = (f32[1536,128]{1,0:T(8,128)S(1)}, s16[1552,128]{1,0:T(8,128)(2,1)S(1)}, f32[8,128]{1,0:T(8,128)S(1)}) custom-call(s32[3]{0:T(128)S(1)} %pad_add_fusion.info, bf16[4,384,384]{2,1,0:T(8,128)(2,1)S(1)} %get-tuple-element.30.m, bf16[4,384,128]{2,1,0:T(8,128)(2,1)S(1)} %get-tuple-element.31.r, bf16[400,512]{1,0:T(8,128)(2,1)S(1)} %collective-permute-done.4.got, ...), custom_call_target="tpu_custom_call" | custom-call | flops 1000 | bytes 1000 | tf_op jit(solution)/shard_map/pallas_call | solution.py:401
  28.0 0.8 %shard_map.102 = s32[16,1,1152]{2,1,0:T(1,128)} custom-call(f32[1,128]{1,0:T(1,128)S(1)} %get-tuple-element.44.owned, f32[8,128]{1,0:T(8,128)S(1)} %get-tuple-element.45.flux_e, f32[8,128]{1,0:T(8,128)S(1)} %collective-permute-done.6.after.back_e, f32[8,128]{1,0:T(8,128)S(1)} %get-tuple-element.46.flux_o, bf16[400,512]{1,0:T(8,128)(2,1)S(1)} %collective-permute-done.4.got), custom_call_target="tpu_custom_call" | custom-call | flops 1000 | bytes 1000 | tf_op jit(solution)/shard_map/pallas_call | solution.py:475
  28.8 11.6 %all-to-all-start = ((s32[16,1,1152]{2,1,0:T(1,128)}), s32[16,1,1152]{2,1,0:T(1,128)S(1)}, u32[]{:S(2)}, u32[]{:S(2)}) async-start(s32[16,1,1152]{2,1,0:T(1,128)} %shard_map.102), calls=%async_computation | async-start | bytes 147456 | tf_op jit(solution)/shard_map/all_to_all | solution.py:604
  40.4 1.9 %collective-permute-start.7 = (s16[1552,128]{1,0:T(8,128)(2,1)S(1)}, s16[1552,128]{1,0:T(8,128)(2,1)S(1)}, u32[]{:S(2)}, u32[]{:S(2)}) collective-permute-start(s16[1552,128]{1,0:T(8,128)(2,1)S(1)} %get-tuple-element.37), channel_id=1, source_target_pairs={{4,8},{8,4},{12,16},{16,12},{20,24},{24,20},{28,32},{32,28},{36,40... | collective-permute-start | bytes 1191944 | tf_op jit(solution)/shard_map/ppermute | solution.py:50
  42.3 6.1 %all-to-all-done = s32[16,1,1152]{2,1,0:T(1,128)S(1)} async-done(((s32[16,1,1152]{2,1,0:T(1,128)}), s32[16,1,1152]{2,1,0:T(1,128)S(1)}, u32[]{:S(2)}, u32[]{:S(2)}) %all-to-all-start) | async-done | bytes 73760 | tf_op jit(solution)/shard_map/all_to_all | solution.py:604
  48.4 0.9 %shard_map.103 = f32[16,8,128]{2,1,0:T(8,128)} custom-call(s32[144,128]{1,0:T(8,128)S(1)} %bitcast.8), custom_call_target="tpu_custom_call" | custom-call | flops 3000000000 | bytes 30000000 | tf_op jit(solution)/shard_map/pallas_call | solution.py:509
  49.3 4.8 %all-to-all-start.1 = ((f32[16,8,128]{2,1,0:T(8,128)}), f32[16,8,128]{2,1,0:T(8,128)S(1)}, u32[]{:S(2)}, u32[]{:S(2)}) async-start(f32[16,8,128]{2,1,0:T(8,128)} %shard_map.103), calls=%async_computation.1 | async-start | bytes 131072 | tf_op jit(solution)/shard_map/all_to_all | solution.py:606
  54.2 2.6 %shard_map.100 = (f32[8,384,128]{2,1,0:T(8,128)}, f32[8,384,128]{2,1,0:T(8,128)}) custom-call(f32[1536,128]{1,0:T(8,128)S(1)} %get-tuple-element.38.x_e, f32[1536,128]{1,0:T(8,128)} %collective-permute-done.8.back_e, f32[1536,128]{1,0:T(8,128)S(1)} %get-tuple-element.39.x_o), custom_call_target="tpu_custom_call" | custom-call | flops 3000000000 | bytes 30000000 | tf_op jit(solution)/shard_map/pallas_call | solution.py:444
  56.8 0.9 %shard_map.101 = (f32[8,384,128]{2,1,0:T(8,128)}, f32[8,384,128]{2,1,0:T(8,128)}) custom-call(s16[1552,128]{1,0:T(8,128)(2,1)S(1)} %collective-permute-done.7.back_o, f32[8,384,128]{2,1,0:T(8,128)} %get-tuple-element.40.up_in, f32[8,384,128]{2,1,0:T(8,128)} %get-tuple-element.41.low_in), custom_call_target="tpu_custom_call", output_to_operand_aliasing={{0}: (1, {}), {1}: (2, {})} | custom-call | flops 1000 | bytes 1000 | tf_op jit(solution)/shard_map/pallas_call | solution.py:541
  57.8 2.9 %all-to-all-done.1.arrived = f32[16,8,128]{2,1,0:T(8,128)S(1)} async-done(((f32[16,8,128]{2,1,0:T(8,128)}), f32[16,8,128]{2,1,0:T(8,128)S(1)}, u32[]{:S(2)}, u32[]{:S(2)}) %all-to-all-start.1) | async-done | bytes 65568 | tf_op jit(solution)/shard_map/all_to_all | solution.py:606
  60.7 0.6 shard_map.104
  (10 shorter events, 0.1 us)
Async XLA Ops:
  2.1 20.5 %collective-permute-start.5 = (bf16[1152,512]{1,0:T(8,128)(2,1)S(1)}, bf16[1152,512]{1,0:T(8,128)(2,1)S(1)}, u32[]{:S(2)}, u32[]{:S(2)}) collective-permute-start(bf16[1152,512]{1,0:T(8,128)(2,1)S(1)} %shard_map.94.refs_7_), channel_id=1, source_target_pairs={{4,8},{8,4},{12,16},{16,12},{20,24},{24,20},{28,32},{32,28},{36,40... | collective-permute-start | bytes 3538952 | tf_op jit(solution)/shard_map/ppermute | solution.py:50
  10.1 2.2 %collective-permute-start.1 = (bf16[384,512]{1,0:T(8,128)(2,1)}, bf16[384,512]{1,0:T(8,128)(2,1)}, u32[]{:S(2)}, u32[]{:S(2)}) collective-permute-start(bf16[384,512]{1,0:T(8,128)(2,1)} %get-tuple-element.27), channel_id=1, source_target_pairs={{0,4},{4,0},{8,12},{12,8},{16,20},{20,16},{24,28},{28,24},{32,36},... | collective-permute-start | bytes 1179656 | tf_op jit(solution)/shard_map/ppermute | solution.py:50
  10.2 5.4 %collective-permute-start = (bf16[400,512]{1,0:T(8,128)(2,1)S(1)}, bf16[400,512]{1,0:T(8,128)(2,1)}, u32[]{:S(2)}, u32[]{:S(2)}) collective-permute-start(bf16[400,512]{1,0:T(8,128)(2,1)S(1)} %get-tuple-element.26), channel_id=1, source_target_pairs={{0,4},{4,0},{8,12},{12,8},{16,20},{20,16},{24,28},{28,24},{32,36},... | collective-permute-start | bytes 1228808 | tf_op jit(solution)/shard_map/ppermute | solution.py:50
  10.7 4.9 %collective-permute-start.2 = (bf16[384,512]{1,0:T(8,128)(2,1)}, bf16[384,512]{1,0:T(8,128)(2,1)}, u32[]{:S(2)}, u32[]{:S(2)}) collective-permute-start(bf16[384,512]{1,0:T(8,128)(2,1)} %get-tuple-element.28), channel_id=1, source_target_pairs={{0,4},{4,0},{8,12},{12,8},{16,20},{20,16},{24,28},{28,24},{32,36},... | collective-permute-start | bytes 1179656 | tf_op jit(solution)/shard_map/ppermute | solution.py:50
  10.8 4.8 %collective-permute-start.3 = (bf16[384,512]{1,0:T(8,128)(2,1)}, bf16[384,512]{1,0:T(8,128)(2,1)}, u32[]{:S(2)}, u32[]{:S(2)}) collective-permute-start(bf16[384,512]{1,0:T(8,128)(2,1)} %get-tuple-element.29), channel_id=1, source_target_pairs={{0,4},{4,0},{8,12},{12,8},{16,20},{20,16},{24,28},{28,24},{32,36},... | collective-permute-start | bytes 1179656 | tf_op jit(solution)/shard_map/ppermute | solution.py:50
  12.2 13.5 %collective-permute-start.4 = (bf16[400,512]{1,0:T(8,128)(2,1)S(1)}, bf16[400,512]{1,0:T(8,128)(2,1)S(1)}, u32[]{:S(2)}, u32[]{:S(2)}) collective-permute-start(bf16[400,512]{1,0:T(8,128)(2,1)S(1)} %shard_map.96.after), channel_id=1, source_target_pairs={{4,8},{8,4},{12,16},{16,12},{20,24},{24,20},{28,32},{32,28},{36,40... | collective-permute-start | bytes 1228808 | tf_op jit(solution)/shard_map/ppermute | solution.py:50
  22.0 32.2 %collective-permute-start.8 = (f32[1536,128]{1,0:T(8,128)S(1)}, f32[1536,128]{1,0:T(8,128)}, u32[]{:S(2)}, u32[]{:S(2)}) collective-permute-start(f32[1536,128]{1,0:T(8,128)S(1)} %get-tuple-element.38.x_e), channel_id=1, source_target_pairs={{0,4},{4,0},{8,12},{12,8},{16,20},{20,16},{24,28},{28,24},{32,36},... | collective-permute-start | bytes 2359304 | tf_op jit(solution)/shard_map/ppermute | solution.py:50
  22.1 3.6 %collective-permute-start.6 = (f32[8,128]{1,0:T(8,128)S(1)}, f32[8,128]{1,0:T(8,128)S(1)}, u32[]{:S(2)}, u32[]{:S(2)}) collective-permute-start(f32[8,128]{1,0:T(8,128)S(1)} %get-tuple-element.36), channel_id=1, source_target_pairs={{0,4},{4,0},{8,12},{12,8},{16,20},{20,16},{24,28},{28,24},{32,36},... | collective-permute-start | bytes 12296 | tf_op jit(solution)/shard_map/ppermute | solution.py:50
  28.8 19.6 %all-to-all-start = ((s32[16,1,1152]{2,1,0:T(1,128)}), s32[16,1,1152]{2,1,0:T(1,128)S(1)}, u32[]{:S(2)}, u32[]{:S(2)}) async-start(s32[16,1,1152]{2,1,0:T(1,128)} %shard_map.102), calls=%async_computation | async-start | bytes 147456 | tf_op jit(solution)/shard_map/all_to_all | solution.py:604
  40.4 16.4 %collective-permute-start.7 = (s16[1552,128]{1,0:T(8,128)(2,1)S(1)}, s16[1552,128]{1,0:T(8,128)(2,1)S(1)}, u32[]{:S(2)}, u32[]{:S(2)}) collective-permute-start(s16[1552,128]{1,0:T(8,128)(2,1)S(1)} %get-tuple-element.37), channel_id=1, source_target_pairs={{4,8},{8,4},{12,16},{16,12},{20,24},{24,20},{28,32},{32,28},{36,40... | collective-permute-start | bytes 1191944 | tf_op jit(solution)/shard_map/ppermute | solution.py:50
  49.3 11.4 %all-to-all-start.1 = ((f32[16,8,128]{2,1,0:T(8,128)}), f32[16,8,128]{2,1,0:T(8,128)S(1)}, u32[]{:S(2)}, u32[]{:S(2)}) async-start(f32[16,8,128]{2,1,0:T(8,128)} %shard_map.103), calls=%async_computation.1 | async-start | bytes 131072 | tf_op jit(solution)/shard_map/all_to_all | solution.py:606
